TPU v7x, 256 devices: a whole 4x4x8 slice. The times are simulated.
256 devices in a mesh: group: 16 (over z_lo, y, core), tile: 16 (over x, z_hi).
Axes of the slice: x: 4, y: 4, z: 8 (z_hi: 4, z_lo: 2; z = z_hi * 2 + z_lo), core: 2. Of those that a mesh axis runs over, the one named last changes fastest.
Arguments:
- fields: float32 [16, 3, 8, 256, 256], P('group', None, None, 'tile'), may hold values from -6 to 6
- sample_index: int32 [16, 3], P('group'), may hold values from 0 to 3
- stencil: int32 [4, 256, 128], replicated, may hold values from 0 to 8191, as said below
- stencil_weight: float32 [4, 256, 128], replicated, may hold values from 0 to 1, as said below
Outputs:
- new_fields: float32 [16, 3, 8, 256, 256], P('group', None, None, 'tile')
Inputs may be any that keep to these rules, and one draw needn't show every extreme that they name: `sample_index`: column 0 is a group's yaw index, column 1 its spacing index, column 2 its veer index. `stencil`: entry [a, y, x * 4 + k] is a flat index row * 32 + column into the outflow band for the k-th point of fringe cell (y, x) at yaw index a; the 4 points of one cell lie in two cyclically neighbouring rows and two neighbouring columns. `stencil_weight`: the 4 weights of each fringe cell are bilinear and sum to one.
All inputs are finite; a program needn't handle non-finite values.
Results may differ from a plain program's by a relative error of at most 0.0003.
Values sent between devices are 32-bit elements; how exact they have to be, the bound alone decides.
No kernel may reach another device: no remote copies, remote signals or barrier semaphores. Data moves between devices by JAX's collectives and lax.ppermute only.
A program may use at most 64 MiB of HBM per device.

v0:
```python
import jax
import jax.numpy as jnp
from jax import lax
from jax.sharding import PartitionSpec as P

COMP = 3
LEV = 8
CY = 16
FR = 32
STEN = 4


TIME_STEP = 0.2
LATERAL_NU = 0.5
VERTICAL_NU = 0.5
SIGMA_PEAK = 2.5
DRAG_COEFF = 1.0
YAW_STEP = 0.2


def with_halo(array, sides, width):
    for axis, dim in sides:
        size, length = (lax.axis_size(axis), array.shape[dim])
        up = [(i, (i + 1) % size) for i in range(size)]
        down = [(j, i) for i, j in up]
        last = lax.slice_in_dim(array, length - width, length, axis=dim)
        leading = lax.slice_in_dim(array, 0, width, axis=dim)
        before = lax.ppermute(last, axis, up)
        after = lax.ppermute(leading, axis, down)
        array = jnp.concatenate([before, array, after], axis=dim)
    return array


def spread(value, axis, source):
    kept = jnp.where(lax.axis_index(axis) == source, value, 0).astype(value.dtype)
    return lax.psum(kept, axis)


def fringe_rate():
    column_ids = jnp.arange(FR, dtype=jnp.int32).astype(jnp.float32)
    return SIGMA_PEAK * 4.0 * (column_ids + 1.0) * (FR - column_ids) / float((FR + 1) ** 2)


def turbine_mask(spacing_index, row_start, row_count, width):
    column_ids = jnp.arange(width, dtype=jnp.int32)
    spacing = (spacing_index + 2) * (width // 32)
    first_col = FR + width // 16
    along_x = (
        (column_ids >= first_col)
        & (column_ids < width - width // 16)
        & ((column_ids - first_col) % spacing == 0)
    )
    row_ids = row_start + jnp.arange(row_count, dtype=jnp.int32)
    within = row_ids % CY
    along_y = (within >= CY * 3 // 8) & (within < CY * 5 // 8)
    level_ids = jnp.arange(LEV, dtype=jnp.int32)
    along_z = (level_ids >= 1) & (level_ids <= LEV // 2)
    joined = along_z[:, None, None] & along_y[None, :, None] & along_x[None, None, :]
    return joined.astype(jnp.float32)[None]


def rotate(planar, yaw_index):
    angle = YAW_STEP * (yaw_index.astype(jnp.float32) - 1.5)
    cosine = jnp.cos(angle)
    sine = jnp.sin(angle)
    return jnp.stack(
        [cosine * planar[0] - sine * planar[1], sine * planar[0] + cosine * planar[1], planar[2]]
    )


def tendency(current, side_values, relax_target, relax_rate, turbines, farm_flag):
    east_side, west_side, north_side, south_side = side_values
    stream = current[0:1]
    cross = current[1:2]
    advect = 0.5 * (stream * (east_side - west_side) + cross * (north_side - south_side))
    lateral = LATERAL_NU * (east_side + west_side + north_side + south_side - 4.0 * current)
    below = jnp.concatenate([-current[:, :1], current[:, :-1]], axis=1)
    above = jnp.concatenate([current[:, 1:], current[:, -1:]], axis=1)
    vertical = VERTICAL_NU * (above - 2.0 * current + below)
    drag = -DRAG_COEFF * turbines * jnp.abs(stream) * current
    relax = relax_rate * (relax_target - current[..., :FR])
    relax_full = jnp.concatenate([relax, jnp.zeros(current[..., FR:].shape, jnp.float32)], axis=3)
    return lateral + vertical - advect + farm_flag * (drag + relax_full)


def advance(initial, relax_target, turbines, farm_flag, neighbours):
    relax_rate = fringe_rate()
    predicted = initial + TIME_STEP * tendency(
        initial, neighbours(initial), relax_target, relax_rate, turbines, farm_flag
    )
    corrected = tendency(
        predicted, neighbours(predicted), relax_target, relax_rate, turbines, farm_flag
    )
    return 0.5 * (initial + predicted + TIME_STEP * corrected)


def halo_sides(current):
    padded = with_halo(current, (("tile", 2),), 1)
    return (
        jnp.roll(current, -1, axis=3),
        jnp.roll(current, 1, axis=3),
        padded[:, :, 2:],
        padded[:, :, :-2],
    )


def interpolate(band, table_rows, weight_rows, veer_index, total_rows, row_start):
    band_rows = band.shape[2] // FR
    grid = band.reshape(COMP, LEV, band_rows, FR)
    cell_count = table_rows.shape[0] * FR
    source = table_rows.reshape(cell_count, STEN)
    weights = weight_rows.reshape(cell_count, STEN)
    level_ids = jnp.arange(LEV, dtype=jnp.int32)
    veer_shift = veer_index * (level_ids + 1) * (CY // 4)
    row_ids = row_start + jnp.arange(band_rows, dtype=jnp.int32)
    col_ids = jnp.arange(FR, dtype=jnp.int32)
    summed = jnp.zeros((COMP, LEV, cell_count), jnp.float32)
    for point in range(STEN):
        source_row = source[:, point] // FR
        source_col = source[:, point] % FR
        moved = (source_row[None, :] + veer_shift[:, None]) % total_rows
        pick_rows = (moved[:, :, None] == row_ids[None, None, :]).astype(jnp.float32)
        row_values = jnp.einsum("lnr,clrf->clnf", pick_rows, grid, precision=lax.Precision.HIGHEST)
        pick_cols = jnp.where(
            source_col[:, None] == col_ids[None, :], weights[:, point : point + 1], 0.0
        )
        summed = summed + jnp.einsum(
            "clnf,nf->cln", row_values, pick_cols, precision=lax.Precision.HIGHEST
        )
    return summed


def local(fields, sample_index, stencil, stencil_weight):
    tile_rows = fields.shape[3]
    width = fields.shape[4]
    total_rows = tile_rows * lax.axis_size("tile")
    row_start = lax.axis_index("tile") * tile_rows
    farm_flag = (lax.axis_index("group") > 0).astype(jnp.float32)
    yaw_index = sample_index[0, 0]
    veer_index = sample_index[0, 2]
    current = fields[0]
    outflow_band = current[:, :, :, width - FR :].reshape(COMP, LEV, tile_rows * FR)
    inflow = spread(outflow_band, "group", 0)
    yaw_table = lax.dynamic_index_in_dim(stencil, yaw_index, 0, keepdims=False)
    weight_table = lax.dynamic_index_in_dim(stencil_weight, yaw_index, 0, keepdims=False)
    partial_sum = interpolate(inflow, yaw_table, weight_table, veer_index, total_rows, row_start)
    planar = lax.psum_scatter(partial_sum, "tile", scatter_dimension=2, tiled=True).reshape(
        COMP, LEV, tile_rows, FR
    )
    relax_target = rotate(planar, yaw_index)
    turbines = turbine_mask(sample_index[0, 1], row_start, tile_rows, width)
    return advance(current, relax_target, turbines, farm_flag, halo_sides)[None]


def solution(mesh):
    in_specs = (P("group", None, None, "tile", None), P("group", None), P(), P())
    out_specs = P("group", None, None, "tile", None)
    return jax.shard_map(local, mesh=mesh, in_specs=in_specs, out_specs=out_specs, check_vma=False)
```

profile of v0, /device:TPU:1, one launch (start us, length us, event | category | flops | bytes accessed | tf_op | source)
XLA Modules:
  0.0 282.3 jit_solution(7644922023659796687)
XLA Ops:
  6.5 1.4 fusion.73
  9.8 5.6 %reshape.459 = s32[8192,4]{1,0:T(8,128)} reshape(s32[1,256,128]{2,1,0:T(8,128)S(1)} %constant_dynamic-slice_fusion.1) | data formatting | bytes 262144 | tf_op jit(solution)/shard_map/reshape | solution.py:111
  15.5 17.8 %slice_reduce_fusion.7 = (s32[8192]{0:T(1024)S(1)}, s32[8192]{0:T(1024)S(1)}, s32[8192]{0:T(1024)S(1)}, s32[8192]{0:T(1024)S(1)}, s32[8192]{0:T(1024)S(1)}, /*in...) fusion(s32[8192,4]{1,0:T(8,128)} %reshape.459), kind=kLoop, calls=%fused_computation.43 | loop fusion | flops 360448 | bytes 393216 | tf_op jit(solution)/shard_map/slice | solution.py:120
  33.2 0.6 multiply_multiply_fusion
  33.8 0.9 constant_dynamic-slice_fusion
  34.8 5.6 %reshape.460 = f32[8192,4]{1,0:T(8,128)} reshape(f32[1,256,128]{2,1,0:T(8,128)S(1)} %constant_dynamic-slice_fusion) | data formatting | bytes 262144 | tf_op jit(solution)/shard_map/reshape | solution.py:112
  40.4 14.0 %slice_reduce_fusion.3 = (f32[8192]{0:T(1024)S(1)}, f32[8192]{0:T(1024)S(1)}, f32[8192]{0:T(1024)S(1)}, f32[8192]{0:T(1024)S(1)}) fusion(f32[8192,4]{1,0:T(8,128)} %reshape.460), kind=kLoop, calls=%fused_computation.31 | loop fusion | bytes 262144 | tf_op jit(solution)/shard_map/slice | solution.py:125
  54.6 55.4 %psum.7 = f32[3,8,16,32]{3,2,0,1:T(8,128)S(1)} all-reduce(f32[3,8,16,32]{3,2,0,1:T(8,128)S(1)} %slice_select_fusion), channel_id=1, replica_groups=mesh['group'=16,'tile'=16] {'group'}, use_global_device_ids=true, to_apply=%region_0.1 | all-reduce | flops 12288 | bytes 98304 | tf_op jit(solution)/shard_map/psum | solution.py:36
  110.8 13.0 %fusion.3 = f32[8192,3,8]{0,1,2:T(4,128)S(1)} fusion(f32[3,8,16,32]{3,2,0,1:T(8,128)S(1)} %psum.7, f32[8192,32]{0,1:T(8,128)S(1)} %get-tuple-element.52, s32[8,8192]{1,0:T(8,128)S(1)} %get-tuple-element.48, s32[16]{0:T(128)S(1)} %iota_add_fusion), kind=kOutput, calls=%fused_computation.7 | convolution fusion | flops 1221394432 | bytes 2146368 | tf_op jit(solution)/shard_map/lnr,clrf->clnf/dot_general | solution.py:123
  123.8 13.0 %fusion.2 = f32[8192,3,8]{0,1,2:T(4,128)S(1)} fusion(f32[3,8,16,32]{3,2,0,1:T(8,128)S(1)} %psum.7, f32[8192,32]{0,1:T(8,128)S(1)} %get-tuple-element.53, s32[8,8192]{1,0:T(8,128)S(1)} %get-tuple-element.49, s32[16]{0:T(128)S(1)} %iota_add_fusion), kind=kOutput, calls=%fused_computation.5 | convolution fusion | flops 1221394432 | bytes 2146368 | tf_op jit(solution)/shard_map/lnr,clrf->clnf/dot_general | solution.py:123
  137.0 13.0 %fusion.1 = f32[8192,3,8]{0,1,2:T(4,128)S(1)} fusion(f32[3,8,16,32]{3,2,0,1:T(8,128)S(1)} %psum.7, f32[8192,32]{0,1:T(8,128)S(1)} %get-tuple-element.54, s32[8,8192]{1,0:T(8,128)S(1)} %get-tuple-element.50, s32[16]{0:T(128)S(1)} %iota_add_fusion), kind=kOutput, calls=%fused_computation.3 | convolution fusion | flops 1221394432 | bytes 2146368 | tf_op jit(solution)/shard_map/lnr,clrf->clnf/dot_general | solution.py:123
  150.0 13.2 %fusion = f32[8192,3,8]{0,1,2:T(4,128)S(1)} fusion(f32[3,8,16,32]{3,2,0,1:T(8,128)S(1)} %psum.7, f32[8192,32]{0,1:T(8,128)S(1)} %get-tuple-element.55, s32[8,8192]{1,0:T(8,128)S(1)} %get-tuple-element.51, s32[16]{0:T(128)S(1)} %iota_add_fusion), kind=kOutput, calls=%fused_computation.1 | convolution fusion | flops 1221394432 | bytes 2146368 | tf_op jit(solution)/shard_map/lnr,clrf->clnf/dot_general | solution.py:123
  163.2 2.6 fusion.32
  165.8 0.6 fusion.70
  166.5 7.3 %collective-permute-start = (f32[3,8,1,256]{3,2,0,1:T(1,128)}, f32[3,8,1,256]{3,2,0,1:T(1,128)}, u32[]{:S(2)}, u32[]{:S(2)}) collective-permute-start(f32[3,8,1,256]{3,2,0,1:T(1,128)} %get-tuple-element.36), channel_id=1, source_target_pairs={{1,0},{2,1},{3,2},{4,3},{5,4},{6,5},{7,6},{8,7},{9,8},{10,9},{11,1... | collective-permute-start | bytes 73736 | tf_op jit(solution)/shard_map/ppermute | solution.py:29
  176.0 0.6 slice_negate_fusion.1
  176.7 0.7 slice_bitcast_fusion.2
  177.8 75.6 %reduce-scatter.2.cloned.1.call-done = f32[3,8,512]{2,1,0:T(8,128)} async-done(((f32[3,8,8192]{2,1,0:T(8,128)}), f32[3,8,512]{2,1,0:T(8,128)}) %reduce-scatter.2.cloned.1.call-update) | async-done | bytes 49168 | tf_op jit(solution)/shard_map/reduce_scatter | solution.py:147
  253.5 1.4 fusion.72
  254.8 0.7 sub.99
  255.5 0.8 constant_dynamic-update-slice_fusion.2
  256.4 1.4 add.340
  257.8 1.4 slice.185
  259.2 0.8 constant_dynamic-update-slice_fusion.1
  260.0 0.8 constant_dynamic-update-slice_fusion
  260.9 0.6 fusion.54
  261.6 1.5 fusion.39
  263.7 3.3 %collective-permute-start.2 = (f32[3,8,1,256]{3,2,0,1:T(1,128)S(1)}, f32[3,8,1,256]{3,2,0,1:T(1,128)S(1)}, u32[]{:S(2)}, u32[]{:S(2)}) collective-permute-start(f32[3,8,1,256]{3,2,0,1:T(1,128)S(1)} %get-tuple-element.24), channel_id=1, source_target_pairs={{1,0},{2,1},{3,2},{4,3},{5,4},{6,5},{7,6},{8,7},{9,8},{10,9},{11,1... | collective-permute-start | bytes 73736 | tf_op jit(solution)/shard_map/ppermute | solution.py:29
  267.0 0.9 collective-permute-done.2
  267.9 6.2 %collective-permute-done.3 = f32[3,8,1,256]{3,2,0,1:T(1,128)S(1)} collective-permute-done((f32[3,8,1,256]{3,2,0,1:T(1,128)S(1)}, f32[3,8,1,256]{3,2,0,1:T(1,128)S(1)}, u32[]{:S(2)}, u32[]{:S(2)}) %collective-permute-start.3) | collective-permute-done | bytes 24608 | tf_op jit(solution)/shard_map/ppermute | solution.py:28
  274.2 0.6 fusion.48
  274.7 0.8 copy.8
  (45 shorter events, 2.9 us)
Async XLA Ops:
  6.5 3.2 %copy-start = (s32[4,256,128]{2,1,0:T(8,128)S(1)}, s32[4,256,128]{2,1,0:T(8,128)}, u32[]{:S(2)}) copy-start(s32[4,256,128]{2,1,0:T(8,128)} %param.6) | copy-start | bytes 1572868
  6.5 246.9 %reduce-scatter.2.cloned.1.call-start = ((), (), s32[]{:S(2)}) async-start(), calls=%async_computation.1 | async-start | bytes 835584 | tf_op jit(solution)/shard_map/reduce_scatter | solution.py:147
  40.4 14.0 %copy-start.1 = (f32[1,3,8,16,256]{4,3,2,1,0:T(8,128)S(1)}, f32[1,3,8,16,256]{4,3,2,1,0:T(8,128)}, u32[]{:S(2)}) copy-start(f32[1,3,8,16,256]{4,3,2,1,0:T(8,128)} %param.4) | copy-start | bytes 1179652
  166.5 95.1 %collective-permute-start = (f32[3,8,1,256]{3,2,0,1:T(1,128)}, f32[3,8,1,256]{3,2,0,1:T(1,128)}, u32[]{:S(2)}, u32[]{:S(2)}) collective-permute-start(f32[3,8,1,256]{3,2,0,1:T(1,128)} %get-tuple-element.36), channel_id=1, source_target_pairs={{1,0},{2,1},{3,2},{4,3},{5,4},{6,5},{7,6},{8,7},{9,8},{10,9},{11,1... | collective-permute-start | bytes 73736 | tf_op jit(solution)/shard_map/ppermute | solution.py:29
  173.8 87.8 %collective-permute-start.1 = (f32[3,8,1,256]{3,2,0,1:T(1,128)}, f32[3,8,1,256]{3,2,0,1:T(1,128)}, u32[]{:S(2)}, u32[]{:S(2)}) collective-permute-start(f32[3,8,1,256]{3,2,0,1:T(1,128)} %get-tuple-element.37), channel_id=1, source_target_pairs={{0,1},{1,2},{2,3},{3,4},{4,5},{5,6},{6,7},{7,8},{8,9},{9,10},{10,1... | collective-permute-start | bytes 73736 | tf_op jit(solution)/shard_map/ppermute | solution.py:28
  173.9 2.8 %copy-start.2 = (pred[8,16]{1,0:T(8,128)(4,1)}, pred[8,16]{1,0:T(8,128)(4,1)S(1)}, u32[]{:S(2)}) copy-start(pred[8,16]{1,0:T(8,128)(4,1)S(1)} %broadcast_and_fusion) | copy-start | bytes 388
  176.0 0.7 copy-start.4
  259.2 3.9 %copy-start.6 = (f32[32]{0:T(128)S(1)}, f32[32]{0:T(128)}, u32[]{:S(2)}) copy-start(f32[32]{0:T(128)} %multiply_multiply_fusion.1) | copy-start | bytes 388
  259.2 4.2 %copy-start.3 = (pred[8,16]{1,0:T(8,128)(4,1)S(1)}, pred[8,16]{1,0:T(8,128)(4,1)}, u32[]{:S(2)}) copy-start(pred[8,16]{1,0:T(8,128)(4,1)} %copy-done.2) | copy-start | bytes 388
  259.2 4.2 %copy-start.5 = (pred[256]{0:T(512)(128)(4,1)S(1)}, pred[256]{0:T(512)(128)(4,1)}, u32[]{:S(2)}) copy-start(pred[256]{0:T(512)(128)(4,1)} %copy-done.4) | copy-start | bytes 772
  263.7 4.3 %collective-permute-start.2 = (f32[3,8,1,256]{3,2,0,1:T(1,128)S(1)}, f32[3,8,1,256]{3,2,0,1:T(1,128)S(1)}, u32[]{:S(2)}, u32[]{:S(2)}) collective-permute-start(f32[3,8,1,256]{3,2,0,1:T(1,128)S(1)} %get-tuple-element.24), channel_id=1, source_target_pairs={{1,0},{2,1},{3,2},{4,3},{5,4},{6,5},{7,6},{8,7},{9,8},{10,9},{11,1... | collective-permute-start | bytes 73736 | tf_op jit(solution)/shard_map/ppermute | solution.py:29
  267.0 7.2 %collective-permute-start.3 = (f32[3,8,1,256]{3,2,0,1:T(1,128)S(1)}, f32[3,8,1,256]{3,2,0,1:T(1,128)S(1)}, u32[]{:S(2)}, u32[]{:S(2)}) collective-permute-start(f32[3,8,1,256]{3,2,0,1:T(1,128)S(1)} %get-tuple-element.25), channel_id=1, source_target_pairs={{0,1},{1,2},{2,3},{3,4},{4,5},{5,6},{6,7},{7,8},{8,9},{9,10},{10,1... | collective-permute-start | bytes 73736 | tf_op jit(solution)/shard_map/ppermute | solution.py:28
Sparse Core Ops, SparseCore 0:
  165.9 87.4 reduce-scatter.1
where the time goes:
time: 285 us; the launch traced here: 282 us
  waiting for transfers between devices  82.8 us (29%)
  blocking collectives  55.4 us (19%)
  matrix products  52.3 us (18%)
  local copies, waits for them, and re-layouts  36.6 us (13%)
  other arithmetic  27.6 us (10%)
  between operations  17 us (6%)
  starting transfers between devices  10.7 us (4%)
    reduce_scatter x1, waiting for transfers between devices, local(): lax.psum_scatter(partial_sum, 'tile', scatter_dimension=2, tiled=True)  75.6 us
    psum x1, blocking collectives, spread(): return lax.psum(kept, axis)  55.4 us
    dot_general x4, matrix products, interpolate(): jnp.einsum('lnr,clrf->clnf', pick_rows, grid, precision=lax.Precision.HIG...  52.3 us
    slice x1, other arithmetic, interpolate(): source_col = source[:, point] % FR  17.8 us
    slice x1, local copies, waits for them, and re-layouts, interpolate(): weights[:, point:point + 1]  14 us
    ppermute x2, starting transfers between devices, with_halo(): after = lax.ppermute(leading, axis, down)  10.7 us
    ppermute x2, waiting for transfers between devices, with_halo(): before = lax.ppermute(last, axis, up)  6.21 us
  transfers between devices with their start and end apart: 5, of which 3 were waited for; matrix products, arithmetic and copies ran while one was open for 4% of the time, Pallas kernels for 0%

commit v1 on v0

v1 whole, which is shorter than its diff:
```python
import jax
import jax.numpy as jnp
import numpy as np
from jax import lax
from jax.experimental import pallas as pl
from jax.experimental.pallas import tpu as pltpu
from jax.sharding import PartitionSpec as P

COMP = 3
LEV = 8
CY = 16
NX = 256
FR = 32
STEN = 4
NYAW = 4
GROUPS = 16
NY = 256
TILES = NY // CY
HALF = CY // 2
LANES = 128
VC = NYAW * COMP

TIME_STEP = 0.2
YAW_STEP = 0.2
SIGMA_PEAK = 2.5

F32 = jnp.float32
BF16 = jnp.bfloat16
VMEM = pl.BlockSpec(memory_space=pltpu.VMEM)
SMEM = pl.BlockSpec(memory_space=pltpu.SMEM)
ANY = pl.BlockSpec(memory_space=pl.ANY)


def params():
    return pltpu.CompilerParams(vmem_limit_bytes=48 * 1024 * 1024)


def cost(flops, moved):
    return pl.CostEstimate(flops=flops, bytes_accessed=moved, transcendentals=0)


def shape(*dims, dtype=F32):
    return jax.ShapeDtypeStruct(dims, dtype)


def lane_iota(rows, lanes):
    return lax.broadcasted_iota(jnp.int32, (rows, lanes), 1)


def row_iota(rows, lanes):
    return lax.broadcasted_iota(jnp.int32, (rows, lanes), 0)


def pack_kernel(sample_ref, fields_ref, msg_ref, low_ref, high_ref):
    combo = (sample_ref[0, 2] * NYAW + sample_ref[0, 0]).astype(F32)
    lane = lane_iota(CY, LANES)
    for lev in range(LEV):
        packed = jnp.full((CY, LANES), combo, F32)
        for comp in range(COMP):
            band = pltpu.roll(fields_ref[0, comp, lev, :, NX - LANES :], (comp + 1) * FR, 1)
            packed = jnp.where((lane >= comp * FR) & (lane < (comp + 1) * FR), band, packed)
        msg_ref[2 * lev] = packed
        msg_ref[2 * lev + 1] = packed
        for comp in range(COMP):
            for row in range(2):
                low_ref[comp, row, lev : lev + 1, :] = fields_ref[0, comp, lev, row : row + 1, :]
                high_ref[comp, row, lev : lev + 1, :] = fields_ref[
                    0, comp, lev, CY - 2 + row : CY - 1 + row, :
                ]


def prepare_kernel(
    stencil_ref, weight_ref, base_ref, key_ref, out_weight_ref, sten, wts, sten_x, wts_x, perm, sems
):
    half = lax.axis_index("group") % 2
    start = lax.axis_index("tile") * CY + half * HALF
    beyond = (start + jnp.where(half == 0, NY - HALF, HALF)) % NY
    start = pl.multiple_of(start, HALF)
    beyond = pl.multiple_of(beyond, HALF)
    copies = [
        pltpu.make_async_copy(stencil_ref.at[:, pl.ds(start, HALF), :], sten, sems.at[0]),
        pltpu.make_async_copy(weight_ref.at[:, pl.ds(start, HALF), :], wts, sems.at[1]),
        pltpu.make_async_copy(stencil_ref.at[:, pl.ds(beyond, HALF), :], sten_x, sems.at[2]),
        pltpu.make_async_copy(weight_ref.at[:, pl.ds(beyond, HALF), :], wts_x, sems.at[3]),
    ]
    for copy in copies:
        copy.start()
    source = row_iota(512, 512)
    target = (source % 4) * LANES + (source // LANES) * FR + (source % LANES) // 4
    perm[...] = jnp.where(target == lane_iota(512, 512), 1.0, 0.0).astype(BF16)
    for copy in copies:
        copy.wait()

    def gathered(main, extra):
        parts = []
        for part in range(4):
            rows = [main[yaw, part + 4 * j : part + 4 * j + 1, :] for yaw in range(NYAW) for j in range(2)]
            outer = jnp.where(half == 0, extra[part, HALF - 1 : HALF, :], extra[part, 0:1, :])
            rows.append(outer)
            rows.append(jnp.zeros((7, LANES), outer.dtype))
            parts.append(jnp.concatenate(rows, axis=0))
        return jnp.concatenate(parts, axis=1)

    index = gathered(sten, sten_x)
    weight = gathered(wts, wts_x)
    first = weight.astype(BF16)
    rest = weight - first.astype(F32)
    second = rest.astype(BF16)
    third = (rest - second.astype(F32)).astype(BF16)
    source_row = (index >> 5).astype(F32).astype(BF16)
    source_col = (index & 31).astype(F32).astype(BF16)
    stacked = jnp.concatenate([source_row, source_col, first, second, third], axis=0)
    sorted_ = jnp.dot(stacked, perm[...], preferred_element_type=F32)
    weight = (sorted_[32:48] + sorted_[48:64]) + sorted_[64:80]
    rows = [sorted_[0:16, k * LANES : (k + 1) * LANES] for k in range(STEN)]
    cols = [sorted_[16:32, k * LANES : (k + 1) * LANES] for k in range(STEN)]
    below = jnp.zeros((16, LANES), F32)
    for k in range(1, STEN):
        delta = rows[k] - rows[0]
        below = jnp.where((delta == -1.0) | (delta == NY - 1.0), 1.0, below)
    base = rows[0] - below
    base = jnp.where(base < 0.0, base + NY, base)
    base_ref[...] = base.astype(jnp.int32)
    for k in range(STEN):
        offset = rows[k] - base
        offset = jnp.where(offset < 0.0, offset + NY, offset)
        key_ref[k] = (offset * FR + cols[k]).astype(jnp.int32)
        out_weight_ref[k] = weight[:, k * LANES : (k + 1) * LANES]


def interpolate_kernel(
    band_ref, asked_ref, base_ref, key_ref, weight_ref, out_ref, table, hot, product, picked, outer
):
    level = lax.axis_index("group") // 2
    band = band_ref[...].reshape(NY, LANES).T[: COMP * FR]
    for veer in range(NYAW):
        for step in range(2):
            shift = (NY - (veer * (level + 1) * (CY // 4) + step)) % NY
            moved = band if veer + step == 0 else pltpu.roll(band, shift, 1)
            upper = moved.astype(BF16)
            lower = (moved - upper.astype(F32)).astype(BF16)
            for comp in range(COMP):
                at = ((veer * COMP + comp) * 2 + step) * FR
                table[at : at + FR, 0:NY] = upper[comp * FR : (comp + 1) * FR]
                table[at : at + FR, NY : 2 * NY] = lower[comp * FR : (comp + 1) * FR]
    row_ids = row_iota(NY, LANES)
    key_ids = row_iota(2 * FR, LANES)
    for pair in range(5):
        cells = [cell for cell in (2 * pair, 2 * pair + 1) if cell <= 2 * NYAW]
        width = LANES * len(cells)
        for at, cell in enumerate(cells):
            ones = jnp.where(row_ids == base_ref[cell : cell + 1, :], 1.0, 0.0).astype(BF16)
            hot[0:NY, at * LANES : (at + 1) * LANES] = ones
            hot[NY : 2 * NY, at * LANES : (at + 1) * LANES] = ones
        product[:, 0:width] = jnp.dot(table[...], hot[:, 0:width], preferred_element_type=F32)
        for at, cell in enumerate(cells):
            weights = jnp.zeros((2 * FR, LANES), F32)
            for k in range(STEN):
                weights = weights + jnp.where(
                    key_ids == key_ref[k, cell : cell + 1, :], weight_ref[k, cell : cell + 1, :], 0.0
                )
            for one in range(VC):
                value = jnp.sum(
                    product[one * 2 * FR : (one + 1) * 2 * FR, at * LANES : (at + 1) * LANES] * weights,
                    axis=0,
                    keepdims=True,
                )
                veer, comp = divmod(one, COMP)
                if cell < 2 * NYAW:
                    yaw, j = divmod(cell, 2)
                    picked[veer * NYAW + yaw, 2 * comp + j : 2 * comp + j + 1, :] = value
                else:
                    outer[one : one + 1, :] = value
    lane = lane_iota(1, LANES)
    rolled = [outer[...] if turn == 0 else pltpu.roll(outer[...], turn * FR, 1) for turn in range(4)]
    for veer in range(NYAW):
        for yaw in range(NYAW):
            rows = [
                rolled[(comp - yaw) % 4][veer * COMP + comp : veer * COMP + comp + 1] for comp in range(COMP)
            ]
            row = jnp.where(lane < FR, rows[0], jnp.where(lane < 2 * FR, rows[1], rows[2]))
            picked[veer * NYAW + yaw, 6:7, :] = row
            picked[veer * NYAW + yaw, 7:8, :] = row
    tile_lane = lane_iota(8, LANES)
    for group in range(GROUPS):
        asked = jnp.where(tile_lane >= COMP * FR, asked_ref[group, 0:8, :], 0.0)
        asked = asked + pltpu.roll(asked, FR, 1)
        asked = asked + pltpu.roll(asked, 2 * FR, 1)
        chosen = picked[0]
        for combo in range(1, NYAW * NYAW):
            chosen = jnp.where(asked == float(combo), picked[combo], chosen)
        out_ref[group] = chosen


def step_kernel(
    sample_ref, fields_ref, planar_ref, low_ref, high_ref, before_ref, after_ref, out_ref, target, pred, edge
):
    flag = jnp.where(lax.axis_index("group") > 0, TIME_STEP, 0.0).astype(F32)
    yaw = sample_ref[0, 0]
    angles = np.float32(YAW_STEP) * (np.arange(NYAW, dtype=np.float32) - np.float32(1.5))
    cosine = jnp.float32(np.cos(angles[0]))
    sine = jnp.float32(np.sin(angles[0]))
    for at in range(1, NYAW):
        cosine = jnp.where(yaw == at, jnp.float32(np.cos(angles[at])), cosine)
        sine = jnp.where(yaw == at, jnp.float32(np.sin(angles[at])), sine)
    spacing = ((sample_ref[0, 1] + 2) * (NX // 32)).astype(F32)

    column = lane_iota(1, LANES).astype(F32)
    rate = SIGMA_PEAK * 4.0 * (column + 1.0) * (FR - column) / float((FR + 1) ** 2)
    rate = jnp.where(column < FR, rate, 0.0) * flag
    rate = jnp.concatenate([rate, jnp.zeros((1, LANES), F32)], axis=1)

    column = lane_iota(CY, NX).astype(F32)
    row = row_iota(CY, NX)
    first_col = float(FR + NX // 16)
    away = column - first_col
    count = jnp.floor(away / spacing + 0.5)
    mask = (column >= first_col) & (column < NX - NX // 16) & (count * spacing == away)
    mask = mask & (row >= CY * 3 // 8) & (row < CY * 5 // 8)
    drag = jnp.where(mask, flag, 0.0)

    for lev in range(LEV):
        for half in range(2):
            packed = planar_ref[2 * lev + half]
            for part in range(4):
                turned = packed if part == 0 else pltpu.roll(packed, LANES - part * FR, 1)
                for comp in range(COMP):
                    for j in range(2):
                        at = half * HALF + 4 * j + part
                        target[comp, lev, at : at + 1, :] = turned[2 * comp + j : 2 * comp + j + 1]
        first, second = target[0, lev], target[1, lev]
        target[0, lev] = cosine * first - sine * second
        target[1, lev] = sine * first + cosine * second

    def west_east(u):
        return pltpu.roll(u, 1, 1), pltpu.roll(u, NX - 1, 1)

    def padded(aim):
        return jnp.concatenate([aim, jnp.zeros(aim.shape, F32)], axis=1)

    def change(u, stream, cross, north, south, above, below, aim, drag_rate):
        west, east = west_east(u)
        total = (east + west) + (north + south) + (above + below) - 6.0 * u
        total = total - stream * (east - west) - cross * (north - south)
        total = 0.1 * total + rate * (padded(aim) - u)
        if drag_rate is not None:
            total = total - drag_rate * u
        return total

    level_ids = row_iota(LEV, NX)
    for side in range(2):
        if side == 0:
            here = [before_ref[comp, 1] for comp in range(COMP)]
            south = [before_ref[comp, 0] for comp in range(COMP)]
            north = [low_ref[comp, 0] for comp in range(COMP)]
        else:
            here = [after_ref[comp, 0] for comp in range(COMP)]
            south = [high_ref[comp, 1] for comp in range(COMP)]
            north = [after_ref[comp, 1] for comp in range(COMP)]
        packed = jnp.concatenate([planar_ref[2 * lev + side, 6:7, :] for lev in range(LEV)], axis=0)
        aims = [packed] + [pltpu.roll(packed, LANES - comp * FR, 1) for comp in range(1, COMP)]
        aims = [cosine * aims[0] - sine * aims[1], sine * aims[0] + cosine * aims[1], aims[2]]
        for comp in range(COMP):
            u = here[comp]
            below = jnp.where(level_ids == 0, -u, pltpu.roll(u, 1, 0))
            above = jnp.where(level_ids == LEV - 1, u, pltpu.roll(u, LEV - 1, 0))
            edge[side, comp] = u + change(
                u, here[0], here[1], north[comp], south[comp], above, below, aims[comp], None
            )

    def stage(read, low_row, high_row, write):
        for lev in range(LEV):
            stream, cross = read(0, lev), read(1, lev)
            drag_rate = drag * jnp.abs(stream) if 1 <= lev <= LEV // 2 else None
            for comp in range(COMP):
                u = (stream, cross)[comp] if comp < 2 else read(comp, lev)
                below = -u if lev == 0 else read(comp, lev - 1)
                above = u if lev == LEV - 1 else read(comp, lev + 1)
                north = jnp.where(row == CY - 1, high_row(comp, lev), pltpu.roll(u, CY - 1, 0))
                south = jnp.where(row == 0, low_row(comp, lev), pltpu.roll(u, 1, 0))
                moved = change(u, stream, cross, north, south, above, below, target[comp, lev], drag_rate)
                write(comp, lev, u, moved)

    def write_pred(comp, lev, u, moved):
        pred[comp, lev] = u + moved

    def write_out(comp, lev, u, moved):
        out_ref[0, comp, lev] = 0.5 * (fields_ref[0, comp, lev] + u + moved)

    stage(
        lambda comp, lev: fields_ref[0, comp, lev],
        lambda comp, lev: before_ref[comp, 1, lev : lev + 1, :],
        lambda comp, lev: after_ref[comp, 0, lev : lev + 1, :],
        write_pred,
    )
    stage(
        lambda comp, lev: pred[comp, lev],
        lambda comp, lev: edge[0, comp, lev : lev + 1, :],
        lambda comp, lev: edge[1, comp, lev : lev + 1, :],
        write_out,
    )


def local(fields, sample_index, stencil, stencil_weight):
    message, low, high = pl.pallas_call(
        pack_kernel,
        out_shape=(shape(GROUPS, CY, LANES), shape(COMP, 2, LEV, NX), shape(COMP, 2, LEV, NX)),
        in_specs=[SMEM, VMEM],
        out_specs=(VMEM, VMEM, VMEM),
        compiler_params=params(),
        name="pack",
    )(sample_index, fields)
    up = [(i, (i + 1) % TILES) for i in range(TILES)]
    down = [(j, i) for i, j in up]
    before = lax.ppermute(high, "tile", up)
    after = lax.ppermute(low, "tile", down)
    asked = lax.all_to_all(message, "group", 0, 0, tiled=True)
    base, key, weight = pl.pallas_call(
        prepare_kernel,
        out_shape=(
            shape(16, LANES, dtype=jnp.int32),
            shape(STEN, 16, LANES, dtype=jnp.int32),
            shape(STEN, 16, LANES),
        ),
        in_specs=[ANY, ANY],
        out_specs=(VMEM, VMEM, VMEM),
        scratch_shapes=[
            pltpu.VMEM((NYAW, HALF, LANES), jnp.int32),
            pltpu.VMEM((NYAW, HALF, LANES), F32),
            pltpu.VMEM((NYAW, HALF, LANES), jnp.int32),
            pltpu.VMEM((NYAW, HALF, LANES), F32),
            pltpu.VMEM((512, 512), BF16),
            pltpu.SemaphoreType.DMA((4,)),
        ],
        compiler_params=params(),
        cost_estimate=cost(2 * 80 * 512 * 512, 200_000),
        name="prepare",
    )(stencil, stencil_weight)
    band = lax.all_to_all(
        jnp.broadcast_to(asked[0:1], (TILES, CY, LANES)), "tile", 0, 0, tiled=True
    )
    answers = pl.pallas_call(
        interpolate_kernel,
        out_shape=shape(GROUPS, 8, LANES),
        in_specs=[VMEM] * 5,
        out_specs=VMEM,
        scratch_shapes=[
            pltpu.VMEM((VC * 2 * FR, 2 * NY), BF16),
            pltpu.VMEM((2 * NY, 2 * LANES), BF16),
            pltpu.VMEM((VC * 2 * FR, 2 * LANES), F32),
            pltpu.VMEM((NYAW * NYAW, 8, LANES), F32),
            pltpu.VMEM((16, LANES), F32),
        ],
        compiler_params=params(),
        name="interpolate",
    )(band, asked, base, key, weight)
    planar = lax.all_to_all(answers, "group", 0, 0, tiled=True)
    return pl.pallas_call(
        step_kernel,
        out_shape=shape(1, COMP, LEV, CY, NX),
        in_specs=[SMEM] + [VMEM] * 6,
        out_specs=VMEM,
        scratch_shapes=[
            pltpu.VMEM((COMP, LEV, CY, LANES), F32),
            pltpu.VMEM((COMP, LEV, CY, NX), F32),
            pltpu.VMEM((2, COMP, LEV, NX), F32),
        ],
        compiler_params=params(),
        name="step",
    )(sample_index, fields, planar, low, high, before, after)


def solution(mesh):
    in_specs = (P("group", None, None, "tile", None), P("group", None), P(), P())
    out_specs = P("group", None, None, "tile", None)
    return jax.shard_map(local, mesh=mesh, in_specs=in_specs, out_specs=out_specs, check_vma=False)
```

time: 285 us -> 53.6 us (0.19)
  waiting for transfers between devices: 82.8 us -> 10.8 us
  matrix products: 52.3 us -> 0 us
  blocking collectives: 55.4 us -> 13.3 us
  local copies, waits for them, and re-layouts: 36.6 us -> 2.34 us
  other arithmetic: 27.6 us -> 0 us
  between operations: 17 us -> 0.07 us
  starting transfers between devices: 10.7 us -> 20.6 us
  Pallas kernels: 0 us -> 5.73 us
    reduce_scatter x1 -> x0, waiting for transfers between devices: 75.6 us -> none  [local(): lax.psum_scatter(partial_sum, 'tile', scatter_dimension=2, tiled=True)]
    psum x1 -> x0, blocking collectives: 55.4 us -> none  [spread(): return lax.psum(kept, axis)]
    dot_general x4 -> x0, matrix products: 52.3 us -> none  [interpolate(): jnp.einsum('lnr,clrf->clnf', pick_rows, grid, precision=lax.Precision.HIG...]
    slice x2 -> x0, other arithmetic: 19.1 us -> none  [the longest x1 17.8 us: interpolate(): source_col = source[:, point] % FR]
    slice x11 -> x0, local copies, waits for them, and re-layouts: 18.2 us -> none  [the longest x1 14 us: interpolate(): weights[:, point:point + 1]]
    all_to_all x0 -> x2, starting transfers between devices: none -> 14.9 us  [the longest x1 9.85 us: local(): lax.all_to_all(jnp.broadcast_to(asked[0:1], (TILES, CY, LANES)), 'tile',...]
    all_to_all x0 -> x1, blocking collectives: none -> 13.3 us  [local(): asked = lax.all_to_all(message, 'group', 0, 0, tiled=True)]
    reshape x2 -> x0, local copies, waits for them, and re-layouts: 11.3 us -> none  [the longest x1 5.64 us: interpolate(): source = table_rows.reshape(cell_count, STEN)]
  transfers between devices with their start and end apart: 5 -> 4, of which waited for: 3 -> 2; matrix products, arithmetic and copies ran while one was open for 4% -> 0% of each run, Pallas kernels for 0% -> 1%
where the time goes in v1:
time: 53.6 us; the launch traced here: 52.9 us
  starting transfers between devices  20.6 us (38%)
  blocking collectives  13.3 us (25%)
  waiting for transfers between devices  10.8 us (20%)
  Pallas kernels  5.73 us (11%)
  local copies, waits for them, and re-layouts  2.34 us (4%)
    all_to_all x1, blocking collectives, local(): asked = lax.all_to_all(message, 'group', 0, 0, tiled=True)  13.3 us
    all_to_all x1, starting transfers between devices, local(): lax.all_to_all(jnp.broadcast_to(asked[0:1], (TILES, CY, LANES)), 'tile',...  9.85 us
    all_to_all x1, waiting for transfers between devices, local(): lax.all_to_all(jnp.broadcast_to(asked[0:1], (TILES, CY, LANES)), 'tile',...  9.3 us
    ppermute x1, starting transfers between devices, local(): after = lax.ppermute(low, 'tile', down)  5.31 us
    all_to_all x1, starting transfers between devices, local(): planar = lax.all_to_all(answers, 'group', 0, 0, tiled=True)  5.03 us
    pallas_call x1, Pallas kernels, local(): pl.pallas_call(interpolate_kernel, out_shape=shape(GROUPS, 8, LANES), in_...  2.29 us
    pallas_call x1, Pallas kernels, local(): pl.pallas_call(step_kernel, out_shape=shape(1, COMP, LEV, CY, NX), in_spe...  2.23 us
    unnamed x12, local copies, waits for them, and re-layouts  1.67 us
  transfers between devices with their start and end apart: 4, of which 2 were waited for; matrix products, arithmetic and copies ran while one was open for 0% of the time, Pallas kernels for 1%

profile of v1, /device:TPU:1, one launch (start us, length us, event | category | flops | bytes accessed | tf_op | source)
XLA Modules:
  0.0 52.9 jit_solution(7152535864908174964)
XLA Ops:
  0.0 0.0 copy-start
  0.0 1.0 %copy-done = f32[1,3,8,16,256]{4,3,2,1,0:T(8,128)S(1)} copy-done((f32[1,3,8,16,256]{4,3,2,1,0:T(8,128)S(1)}, f32[1,3,8,16,256]{4,3,2,1,0:T(8,128)}, u32[]{:S(2)}) %copy-start) | copy-done | bytes 393240
  1.0 0.0 copy-start.4
  1.0 0.7 %copy-done.4 = s32[1,3]{1,0:T(1,128)S(1)} copy-done((s32[1,3]{1,0:T(1,128)S(1)}, s32[1,3]{1,0:T(1,128)}, u32[]{:S(2)}) %copy-start.4) | copy-done | bytes 36
  1.7 0.0 copy-start.2
  1.7 0.0 copy-start.3
  1.7 0.7 %pack.1 = (f32[16,16,128]{2,1,0:T(8,128)S(1)}, f32[3,2,8,256]{3,2,1,0:T(8,128)S(1)}, f32[3,2,8,256]{3,2,1,0:T(8,128)S(1)}) custom-call(s32[1,3]{1,0:T(1,128)S(1)} %copy-done.4, f32[1,3,8,16,256]{4,3,2,1,0:T(8,128)S(1)} %copy-done), custom_call_target="tpu_custom_call" | custom-call | tf_op jit(solution)/shard_map/pack/pallas_call | solution.py:305
  2.4 13.3 %all_to_all.15.asked_ref = f32[16,16,128]{2,1,0:T(8,128)S(1)} all-to-all(f32[16,16,128]{2,1,0:T(8,128)S(1)} %get-tuple-element.11), channel_id=1, replica_groups=mesh['group'=16,'tile'=16] {'group'}, dimensions={0} | all-to-all | bytes 262144 | tf_op jit(solution)/shard_map/all_to_all | solution.py:317
  15.6 0.7 %broadcast_in_dim.8 = f32[16,16,128]{2,1,0:T(8,128)} broadcast(f32[16,128]{1,0:T(8,128)S(1)} %slice_bitcast_fusion), dimensions={1,2} | broadcast | bytes 139264 | tf_op jit(solution)/shard_map/broadcast_in_dim | solution.py:340
  16.3 9.9 %all-to-all-start.1 = ((f32[16,16,128]{2,1,0:T(8,128)}), f32[16,16,128]{2,1,0:T(8,128)S(1)}, u32[]{:S(2)}, u32[]{:S(2)}) async-start(f32[16,16,128]{2,1,0:T(8,128)} %broadcast_in_dim.8), calls=%async_computation.1 | async-start | bytes 262144 | tf_op jit(solution)/shard_map/all_to_all | solution.py:339
  26.2 0.0 copy-done.2
  26.2 0.0 copy-done.3
  26.2 0.5 prepare.1
  26.7 0.0 copy-start.1
  26.7 9.3 %all-to-all-done.1.band_ref = f32[16,16,128]{2,1,0:T(8,128)S(1)} async-done(((f32[16,16,128]{2,1,0:T(8,128)}), f32[16,16,128]{2,1,0:T(8,128)S(1)}, u32[]{:S(2)}, u32[]{:S(2)}) %all-to-all-start.1) | async-done | bytes 131104 | tf_op jit(solution)/shard_map/all_to_all | solution.py:339
  36.0 2.3 %interpolate.1 = f32[16,8,128]{2,1,0:T(8,128)} custom-call(f32[16,16,128]{2,1,0:T(8,128)S(1)} %all-to-all-done.1.band_ref, f32[16,16,128]{2,1,0:T(8,128)S(1)} %all_to_all.15.asked_ref, s32[16,128]{1,0:T(8,128)S(1)} %get-tuple-element.12.base_ref, s32[4,16,128]{2,1,0:T(8,128)S(1)} %get-tuple-element.13.key_ref, f32[4,16,128]{2,1,0:T(8,128)S(1)} %get-tuple-element.14.weight_ref), custom_call_target="tpu_custom_call" | custom-call | tf_op jit(solution)/shard_map/interpolate/pallas_call | solution.py:342
  38.3 5.0 %all-to-all-start.2 = ((f32[16,8,128]{2,1,0:T(8,128)}), f32[16,8,128]{2,1,0:T(8,128)S(1)}, u32[]{:S(2)}, u32[]{:S(2)}) async-start(f32[16,8,128]{2,1,0:T(8,128)} %interpolate.1), calls=%async_computation.2 | async-start | bytes 131072 | tf_op jit(solution)/shard_map/all_to_all | solution.py:357
  43.3 0.0 copy-start.5
  43.3 0.5 collective-permute-start
  43.8 5.3 %collective-permute-start.1 = (f32[3,2,8,256]{3,2,1,0:T(8,128)S(1)}, f32[3,2,8,256]{3,2,1,0:T(8,128)S(1)}, u32[]{:S(2)}, u32[]{:S(2)}) collective-permute-start(f32[3,2,8,256]{3,2,1,0:T(8,128)S(1)} %get-tuple-element.15.low_ref), channel_id=1, source_target_pairs={{1,0},{2,1},{3,2},{4,3},{5,4},{6,5},{7,6},{8,7},{9,8},{10,9},{11,1... | collective-permute-start | bytes 147464 | tf_op jit(solution)/shard_map/ppermute | solution.py:316
  49.1 1.5 %collective-permute-done.before_ref = f32[3,2,8,256]{3,2,1,0:T(8,128)S(1)} collective-permute-done((f32[3,2,8,256]{3,2,1,0:T(8,128)S(1)}, f32[3,2,8,256]{3,2,1,0:T(8,128)S(1)}, u32[]{:S(2)}, u32[]{:S(2)}) %collective-permute-start) | collective-permute-done | bytes 49184 | tf_op jit(solution)/shard_map/ppermute | solution.py:315
  50.6 0.0 collective-permute-done.1.after_ref
  50.6 0.0 all-to-all-done.2.planar_ref
  50.6 0.0 copy-done.1
  50.6 0.0 copy-done.5
  50.6 2.2 %step.1 = f32[1,3,8,16,256]{4,3,2,1,0:T(8,128)} custom-call(s32[1,3]{1,0:T(1,128)S(1)} %copy-done.5, f32[1,3,8,16,256]{4,3,2,1,0:T(8,128)S(1)} %copy-done.1, f32[16,8,128]{2,1,0:T(8,128)S(1)} %all-to-all-done.2.planar_ref, f32[3,2,8,256]{3,2,1,0:T(8,128)S(1)} %get-tuple-element.15.low_ref, f32[3,2,8,256]{3,2,1,0:T(8,128)S(1)} %get-tuple-element.16.high_ref, ...), custom_call_target="tpu_custom_call" | custom-call | tf_op jit(solution)/shard_map/step/pallas_call | solution.py:358
  (1 shorter events, 0.0 us)
Async XLA Ops:
  0.0 1.0 %copy-start = (f32[1,3,8,16,256]{4,3,2,1,0:T(8,128)S(1)}, f32[1,3,8,16,256]{4,3,2,1,0:T(8,128)}, u32[]{:S(2)}) copy-start(f32[1,3,8,16,256]{4,3,2,1,0:T(8,128)} %fields_ref.3) | copy-start | bytes 1179652
  1.0 0.7 %copy-start.4 = (s32[1,3]{1,0:T(1,128)S(1)}, s32[1,3]{1,0:T(1,128)}, u32[]{:S(2)}) copy-start(s32[1,3]{1,0:T(1,128)} %sample_ref.3) | copy-start | bytes 40
  1.7 24.5 %copy-start.2 = (s32[4,256,128]{2,1,0:T(8,128)S(1)}, s32[4,256,128]{2,1,0:T(8,128)}, u32[]{:S(2)}) copy-start(s32[4,256,128]{2,1,0:T(8,128)} %stencil_ref.1) | copy-start | bytes 1572868
  1.7 24.5 %copy-start.3 = (f32[4,256,128]{2,1,0:T(8,128)S(1)}, f32[4,256,128]{2,1,0:T(8,128)}, u32[]{:S(2)}) copy-start(f32[4,256,128]{2,1,0:T(8,128)} %weight_ref.1) | copy-start | bytes 1572868
  16.3 19.7 %all-to-all-start.1 = ((f32[16,16,128]{2,1,0:T(8,128)}), f32[16,16,128]{2,1,0:T(8,128)S(1)}, u32[]{:S(2)}, u32[]{:S(2)}) async-start(f32[16,16,128]{2,1,0:T(8,128)} %broadcast_in_dim.8), calls=%async_computation.1 | async-start | bytes 262144 | tf_op jit(solution)/shard_map/all_to_all | solution.py:339
  26.7 23.9 %copy-start.1 = (f32[1,3,8,16,256]{4,3,2,1,0:T(8,128)S(1)}, f32[1,3,8,16,256]{4,3,2,1,0:T(8,128)}, u32[]{:S(2)}) copy-start(f32[1,3,8,16,256]{4,3,2,1,0:T(8,128)} %fields_ref.3) | copy-start | bytes 1179652
  38.3 12.3 %all-to-all-start.2 = ((f32[16,8,128]{2,1,0:T(8,128)}), f32[16,8,128]{2,1,0:T(8,128)S(1)}, u32[]{:S(2)}, u32[]{:S(2)}) async-start(f32[16,8,128]{2,1,0:T(8,128)} %interpolate.1), calls=%async_computation.2 | async-start | bytes 131072 | tf_op jit(solution)/shard_map/all_to_all | solution.py:357
  43.3 7.3 %copy-start.5 = (s32[1,3]{1,0:T(1,128)S(1)}, s32[1,3]{1,0:T(1,128)}, u32[]{:S(2)}) copy-start(s32[1,3]{1,0:T(1,128)} %sample_ref.3) | copy-start | bytes 40
  43.3 7.3 %collective-permute-start = (f32[3,2,8,256]{3,2,1,0:T(8,128)S(1)}, f32[3,2,8,256]{3,2,1,0:T(8,128)S(1)}, u32[]{:S(2)}, u32[]{:S(2)}) collective-permute-start(f32[3,2,8,256]{3,2,1,0:T(8,128)S(1)} %get-tuple-element.16.high_ref), channel_id=1, source_target_pairs={{0,1},{1,2},{2,3},{3,4},{4,5},{5,6},{6,7},{7,8},{8,9},{9,10},{10,1... | collective-permute-start | bytes 147464 | tf_op jit(solution)/shard_map/ppermute | solution.py:315
  43.8 6.8 %collective-permute-start.1 = (f32[3,2,8,256]{3,2,1,0:T(8,128)S(1)}, f32[3,2,8,256]{3,2,1,0:T(8,128)S(1)}, u32[]{:S(2)}, u32[]{:S(2)}) collective-permute-start(f32[3,2,8,256]{3,2,1,0:T(8,128)S(1)} %get-tuple-element.15.low_ref), channel_id=1, source_target_pairs={{1,0},{2,1},{3,2},{4,3},{5,4},{6,5},{7,6},{8,7},{9,8},{10,9},{11,1... | collective-permute-start | bytes 147464 | tf_op jit(solution)/shard_map/ppermute | solution.py:316

commit v2 on v1

--- a/solution.py
+++ b/solution.py
@@ -11,6 +11,7 @@
 CY = 16
 NX = 256
 FR = 32
+PACK_KIB = 60000
 STEN = 4
 NYAW = 4
 GROUPS = 16
@@ -28,11 +29,11 @@
 BF16 = jnp.bfloat16
 VMEM = pl.BlockSpec(memory_space=pltpu.VMEM)
 SMEM = pl.BlockSpec(memory_space=pltpu.SMEM)
-ANY = pl.BlockSpec(memory_space=pl.ANY)
-
-
-def params():
-    return pltpu.CompilerParams(vmem_limit_bytes=48 * 1024 * 1024)
+HBM = pl.BlockSpec(memory_space=pltpu.HBM)
+
+
+def params(kib=48 * 1024):
+    return pltpu.CompilerParams(vmem_limit_bytes=kib * 1024)
 
 
 def cost(flops, moved):
@@ -51,21 +52,42 @@
     return lax.broadcasted_iota(jnp.int32, (rows, lanes), 0)
 
 
-def pack_kernel(sample_ref, fields_ref, msg_ref, low_ref, high_ref):
+def pack_kernel(sample_hbm, fields_hbm, msg_ref, low_ref, high_ref, sample_ref, fields_ref, sems):
+    sample_copy = pltpu.make_async_copy(sample_hbm, sample_ref, sems.at[0])
+    sample_copy.start()
+    halves = [pl.ds(NX - LANES, LANES), pl.ds(0, LANES)]
+    copies = [
+        [
+            pltpu.make_async_copy(
+                fields_hbm.at[0, comp, :, :, lanes], fields_ref.at[comp, :, :, lanes], sems.at[1 + 3 * at + comp]
+            )
+            for comp in range(COMP)
+        ]
+        for at, lanes in enumerate(halves)
+    ]
+    for part in copies:
+        for copy in part:
+            copy.start()
+    for copy in copies[0]:
+        copy.wait()
+    sample_copy.wait()
     combo = (sample_ref[0, 2] * NYAW + sample_ref[0, 0]).astype(F32)
     lane = lane_iota(CY, LANES)
     for lev in range(LEV):
         packed = jnp.full((CY, LANES), combo, F32)
         for comp in range(COMP):
-            band = pltpu.roll(fields_ref[0, comp, lev, :, NX - LANES :], (comp + 1) * FR, 1)
+            band = pltpu.roll(fields_ref[comp, lev, :, NX - LANES :], (comp + 1) * FR, 1)
             packed = jnp.where((lane >= comp * FR) & (lane < (comp + 1) * FR), band, packed)
         msg_ref[2 * lev] = packed
         msg_ref[2 * lev + 1] = packed
+    for copy in copies[1]:
+        copy.wait()
+    for lev in range(LEV):
         for comp in range(COMP):
             for row in range(2):
-                low_ref[comp, row, lev : lev + 1, :] = fields_ref[0, comp, lev, row : row + 1, :]
+                low_ref[comp, row, lev : lev + 1, :] = fields_ref[comp, lev, row : row + 1, :]
                 high_ref[comp, row, lev : lev + 1, :] = fields_ref[
-                    0, comp, lev, CY - 2 + row : CY - 1 + row, :
+                    comp, lev, CY - 2 + row : CY - 1 + row, :
                 ]
 
 
@@ -129,7 +151,7 @@
 
 
 def interpolate_kernel(
-    band_ref, asked_ref, base_ref, key_ref, weight_ref, out_ref, table, hot, product, picked, outer
+    band_ref, asked_ref, base_ref, key_ref, weight_ref, out_ref, table, picked, outer
 ):
     level = lax.axis_index("group") // 2
     band = band_ref[...].reshape(NY, LANES).T[: COMP * FR]
@@ -147,12 +169,10 @@
     key_ids = row_iota(2 * FR, LANES)
     for pair in range(5):
         cells = [cell for cell in (2 * pair, 2 * pair + 1) if cell <= 2 * NYAW]
-        width = LANES * len(cells)
-        for at, cell in enumerate(cells):
-            ones = jnp.where(row_ids == base_ref[cell : cell + 1, :], 1.0, 0.0).astype(BF16)
-            hot[0:NY, at * LANES : (at + 1) * LANES] = ones
-            hot[NY : 2 * NY, at * LANES : (at + 1) * LANES] = ones
-        product[:, 0:width] = jnp.dot(table[...], hot[:, 0:width], preferred_element_type=F32)
+        ones = jnp.concatenate(
+            [jnp.where(row_ids == base_ref[cell : cell + 1, :], 1.0, 0.0).astype(BF16) for cell in cells], axis=1
+        )
+        product = jnp.dot(table[...], jnp.concatenate([ones, ones], axis=0), preferred_element_type=F32)
         for at, cell in enumerate(cells):
             weights = jnp.zeros((2 * FR, LANES), F32)
             for k in range(STEN):
@@ -192,8 +212,86 @@
         out_ref[group] = chosen
 
 
-def step_kernel(
-    sample_ref, fields_ref, planar_ref, low_ref, high_ref, before_ref, after_ref, out_ref, target, pred, edge
+def rates(flag, spacing):
+    column = lane_iota(1, LANES).astype(F32)
+    rate = SIGMA_PEAK * 4.0 * (column + 1.0) * (FR - column) / float((FR + 1) ** 2)
+    rate = jnp.where(column < FR, rate, 0.0) * flag
+    column = lane_iota(CY, NX).astype(F32)
+    row = row_iota(CY, NX)
+    first_col = float(FR + NX // 16)
+    away = column - first_col
+    count = jnp.floor(away / spacing + 0.5)
+    mask = (column >= first_col) & (column < NX - NX // 16) & (count * spacing == away)
+    mask = mask & (row >= CY * 3 // 8) & (row < CY * 5 // 8)
+    return rate, jnp.where(mask, flag, 0.0)
+
+
+def change(u, stream, cross, west, east, north, south, above, below):
+    total = (east + west) + (north + south) + (above + below) - 6.0 * u
+    return 0.1 * (total - stream * (east - west) - cross * (north - south))
+
+
+def begin_kernel(
+    sample_ref, fields_ref, low_ref, high_ref, before_ref, after_ref, pred_ref, edge_ref, right_ref
+):
+    flag = jnp.where(lax.axis_index("group") > 0, TIME_STEP, 0.0).astype(F32)
+    spacing = ((sample_ref[0, 1] + 2) * (NX // 32)).astype(F32)
+    rate, drag = rates(flag, spacing)
+    rate = jnp.concatenate([rate, jnp.zeros((1, LANES), F32)], axis=1)
+    row = row_iota(CY, NX)
+
+    level_ids = row_iota(LEV, NX)
+    for side in range(2):
+        if side == 0:
+            here = [before_ref[comp, 1] for comp in range(COMP)]
+            south = [before_ref[comp, 0] for comp in range(COMP)]
+            north = [low_ref[comp, 0] for comp in range(COMP)]
+        else:
+            here = [after_ref[comp, 0] for comp in range(COMP)]
+            south = [high_ref[comp, 1] for comp in range(COMP)]
+            north = [after_ref[comp, 1] for comp in range(COMP)]
+        for comp in range(COMP):
+            u = here[comp]
+            below = jnp.where(level_ids == 0, -u, pltpu.roll(u, 1, 0))
+            above = jnp.where(level_ids == LEV - 1, u, pltpu.roll(u, LEV - 1, 0))
+            west, east = pltpu.roll(u, 1, 1), pltpu.roll(u, NX - 1, 1)
+            moved = change(u, here[0], here[1], west, east, north[comp], south[comp], above, below)
+            edge_ref[side, comp] = u + moved - rate * u
+
+    for lev in range(LEV):
+        stream, cross = fields_ref[0, 0, lev], fields_ref[0, 1, lev]
+        loss = rate + drag * jnp.abs(stream) if 1 <= lev <= LEV // 2 else rate
+        for comp in range(COMP):
+            u = fields_ref[0, comp, lev]
+            below = -u if lev == 0 else fields_ref[0, comp, lev - 1]
+            above = u if lev == LEV - 1 else fields_ref[0, comp, lev + 1]
+            north = jnp.where(row == CY - 1, after_ref[comp, 0, lev : lev + 1, :], pltpu.roll(u, CY - 1, 0))
+            south = jnp.where(row == 0, before_ref[comp, 1, lev : lev + 1, :], pltpu.roll(u, 1, 0))
+            west, east = pltpu.roll(u, 1, 1), pltpu.roll(u, NX - 1, 1)
+            moved = change(u, stream, cross, west, east, north, south, above, below)
+            pred_ref[comp, lev] = u + moved - loss * u
+
+    row = row_iota(CY, LANES)
+    lane = lane_iota(CY, LANES)
+    for lev in range(LEV):
+        stream, cross = pred_ref[0, lev, :, LANES:], pred_ref[1, lev, :, LANES:]
+        for comp in range(COMP):
+            u = pred_ref[comp, lev, :, LANES:]
+            left = pred_ref[comp, lev, :, :LANES]
+            below = -u if lev == 0 else pred_ref[comp, lev - 1, :, LANES:]
+            above = u if lev == LEV - 1 else pred_ref[comp, lev + 1, :, LANES:]
+            north = jnp.where(row == CY - 1, edge_ref[1, comp, lev : lev + 1, LANES:], pltpu.roll(u, CY - 1, 0))
+            south = jnp.where(row == 0, edge_ref[0, comp, lev : lev + 1, LANES:], pltpu.roll(u, 1, 0))
+            east = pltpu.roll(jnp.where(lane == 0, left, u), LANES - 1, 1)
+            west = pltpu.roll(jnp.where(lane == LANES - 1, left, u), 1, 1)
+            moved = change(u, stream, cross, west, east, north, south, above, below)
+            if 1 <= lev <= LEV // 2:
+                moved = moved - drag[:, LANES:] * jnp.abs(stream) * u
+            right_ref[comp, lev] = 0.5 * (fields_ref[0, comp, lev, :, LANES:] + u + moved)
+
+
+def finish_kernel(
+    sample_ref, fields_ref, planar_ref, pred_ref, edge_ref, right_ref, out_ref, target, full, edge, result, sems
 ):
     flag = jnp.where(lax.axis_index("group") > 0, TIME_STEP, 0.0).astype(F32)
     yaw = sample_ref[0, 0]
@@ -204,20 +302,8 @@
         cosine = jnp.where(yaw == at, jnp.float32(np.cos(angles[at])), cosine)
         sine = jnp.where(yaw == at, jnp.float32(np.sin(angles[at])), sine)
     spacing = ((sample_ref[0, 1] + 2) * (NX // 32)).astype(F32)
-
-    column = lane_iota(1, LANES).astype(F32)
-    rate = SIGMA_PEAK * 4.0 * (column + 1.0) * (FR - column) / float((FR + 1) ** 2)
-    rate = jnp.where(column < FR, rate, 0.0) * flag
-    rate = jnp.concatenate([rate, jnp.zeros((1, LANES), F32)], axis=1)
-
-    column = lane_iota(CY, NX).astype(F32)
-    row = row_iota(CY, NX)
-    first_col = float(FR + NX // 16)
-    away = column - first_col
-    count = jnp.floor(away / spacing + 0.5)
-    mask = (column >= first_col) & (column < NX - NX // 16) & (count * spacing == away)
-    mask = mask & (row >= CY * 3 // 8) & (row < CY * 5 // 8)
-    drag = jnp.where(mask, flag, 0.0)
+    rate, drag = rates(flag, spacing)
+    drag = drag[:, :LANES]
 
     for lev in range(LEV):
         for half in range(2):
@@ -229,85 +315,58 @@
                         at = half * HALF + 4 * j + part
                         target[comp, lev, at : at + 1, :] = turned[2 * comp + j : 2 * comp + j + 1]
         first, second = target[0, lev], target[1, lev]
-        target[0, lev] = cosine * first - sine * second
-        target[1, lev] = sine * first + cosine * second
-
-    def west_east(u):
-        return pltpu.roll(u, 1, 1), pltpu.roll(u, NX - 1, 1)
-
-    def padded(aim):
-        return jnp.concatenate([aim, jnp.zeros(aim.shape, F32)], axis=1)
-
-    def change(u, stream, cross, north, south, above, below, aim, drag_rate):
-        west, east = west_east(u)
-        total = (east + west) + (north + south) + (above + below) - 6.0 * u
-        total = total - stream * (east - west) - cross * (north - south)
-        total = 0.1 * total + rate * (padded(aim) - u)
-        if drag_rate is not None:
-            total = total - drag_rate * u
-        return total
-
-    level_ids = row_iota(LEV, NX)
+        aims = [cosine * first - sine * second, sine * first + cosine * second, target[2, lev]]
+        for comp in range(COMP):
+            pull = rate * aims[comp]
+            target[comp, lev] = pull
+            full[comp, lev] = pred_ref[comp, lev, :, :LANES] + pull
     for side in range(2):
-        if side == 0:
-            here = [before_ref[comp, 1] for comp in range(COMP)]
-            south = [before_ref[comp, 0] for comp in range(COMP)]
-            north = [low_ref[comp, 0] for comp in range(COMP)]
-        else:
-            here = [after_ref[comp, 0] for comp in range(COMP)]
-            south = [high_ref[comp, 1] for comp in range(COMP)]
-            north = [after_ref[comp, 1] for comp in range(COMP)]
         packed = jnp.concatenate([planar_ref[2 * lev + side, 6:7, :] for lev in range(LEV)], axis=0)
         aims = [packed] + [pltpu.roll(packed, LANES - comp * FR, 1) for comp in range(1, COMP)]
         aims = [cosine * aims[0] - sine * aims[1], sine * aims[0] + cosine * aims[1], aims[2]]
         for comp in range(COMP):
-            u = here[comp]
-            below = jnp.where(level_ids == 0, -u, pltpu.roll(u, 1, 0))
-            above = jnp.where(level_ids == LEV - 1, u, pltpu.roll(u, LEV - 1, 0))
-            edge[side, comp] = u + change(
-                u, here[0], here[1], north[comp], south[comp], above, below, aims[comp], None
-            )
-
-    def stage(read, low_row, high_row, write):
-        for lev in range(LEV):
-            stream, cross = read(0, lev), read(1, lev)
-            drag_rate = drag * jnp.abs(stream) if 1 <= lev <= LEV // 2 else None
-            for comp in range(COMP):
-                u = (stream, cross)[comp] if comp < 2 else read(comp, lev)
-                below = -u if lev == 0 else read(comp, lev - 1)
-                above = u if lev == LEV - 1 else read(comp, lev + 1)
-                north = jnp.where(row == CY - 1, high_row(comp, lev), pltpu.roll(u, CY - 1, 0))
-                south = jnp.where(row == 0, low_row(comp, lev), pltpu.roll(u, 1, 0))
-                moved = change(u, stream, cross, north, south, above, below, target[comp, lev], drag_rate)
-                write(comp, lev, u, moved)
-
-    def write_pred(comp, lev, u, moved):
-        pred[comp, lev] = u + moved
-
-    def write_out(comp, lev, u, moved):
-        out_ref[0, comp, lev] = 0.5 * (fields_ref[0, comp, lev] + u + moved)
-
-    stage(
-        lambda comp, lev: fields_ref[0, comp, lev],
-        lambda comp, lev: before_ref[comp, 1, lev : lev + 1, :],
-        lambda comp, lev: after_ref[comp, 0, lev : lev + 1, :],
-        write_pred,
-    )
-    stage(
-        lambda comp, lev: pred[comp, lev],
-        lambda comp, lev: edge[0, comp, lev : lev + 1, :],
-        lambda comp, lev: edge[1, comp, lev : lev + 1, :],
-        write_out,
-    )
+            edge[side, comp] = edge_ref[side, comp, :, :LANES] + rate * aims[comp]
+
+    row = row_iota(CY, LANES)
+    lane = lane_iota(CY, LANES)
+    copies = []
+    for lev in range(LEV):
+        stream, cross = full[0, lev], full[1, lev]
+        loss = rate + drag * jnp.abs(stream) if 1 <= lev <= LEV // 2 else rate
+        last = 0.05 * (1.0 - pred_ref[0, lev, :, LANES:])
+        for comp in range(COMP):
+            u = full[comp, lev]
+            right = pred_ref[comp, lev, :, LANES:]
+            pull = target[comp, lev]
+            below = -u if lev == 0 else full[comp, lev - 1]
+            above = u if lev == LEV - 1 else full[comp, lev + 1]
+            north = jnp.where(row == CY - 1, edge[1, comp, lev : lev + 1, :], pltpu.roll(u, CY - 1, 0))
+            south = jnp.where(row == 0, edge[0, comp, lev : lev + 1, :], pltpu.roll(u, 1, 0))
+            east = pltpu.roll(jnp.where(lane == 0, right, u), LANES - 1, 1)
+            west = pltpu.roll(jnp.where(lane == LANES - 1, right, u), 1, 1)
+            moved = change(u, stream, cross, west, east, north, south, above, below) + (pull - loss * u)
+            result[comp, lev, :, :LANES] = 0.5 * (fields_ref[0, comp, lev, :, :LANES] + u + moved)
+            passed = jnp.where(lane == LANES - 1, pltpu.roll(pull, LANES - 1, 1), 0.0)
+            result[comp, lev, :, LANES:] = right_ref[comp, lev] + last * passed
+        copy = pltpu.make_async_copy(result.at[:, lev], out_ref.at[0, :, lev], sems.at[lev])
+        copy.start()
+        copies.append(copy)
+    for copy in copies:
+        copy.wait()
 
 
 def local(fields, sample_index, stencil, stencil_weight):
     message, low, high = pl.pallas_call(
         pack_kernel,
         out_shape=(shape(GROUPS, CY, LANES), shape(COMP, 2, LEV, NX), shape(COMP, 2, LEV, NX)),
-        in_specs=[SMEM, VMEM],
+        in_specs=[HBM, HBM],
         out_specs=(VMEM, VMEM, VMEM),
-        compiler_params=params(),
+        scratch_shapes=[
+            pltpu.SMEM((1, COMP), jnp.int32),
+            pltpu.VMEM((COMP, LEV, CY, NX), F32),
+            pltpu.SemaphoreType.DMA((7,)),
+        ],
+        compiler_params=params(PACK_KIB),
         name="pack",
     )(sample_index, fields)
     up = [(i, (i + 1) % TILES) for i in range(TILES)]
@@ -322,7 +381,7 @@
             shape(STEN, 16, LANES, dtype=jnp.int32),
             shape(STEN, 16, LANES),
         ),
-        in_specs=[ANY, ANY],
+        in_specs=[HBM, HBM],
         out_specs=(VMEM, VMEM, VMEM),
         scratch_shapes=[
             pltpu.VMEM((NYAW, HALF, LANES), jnp.int32),
@@ -339,6 +398,20 @@
     band = lax.all_to_all(
         jnp.broadcast_to(asked[0:1], (TILES, CY, LANES)), "tile", 0, 0, tiled=True
     )
+    pred, edge, right = pl.pallas_call(
+        begin_kernel,
+        out_shape=(
+            shape(COMP, LEV, CY, NX),
+            shape(2, COMP, LEV, NX),
+            shape(COMP, LEV, CY, LANES),
+        ),
+        in_specs=[SMEM] + [VMEM] * 5,
+        out_specs=(VMEM, VMEM, VMEM),
+        compiler_params=params(),
+        cost_estimate=cost(8_000_000, 1_000_000),
+        name="begin",
+    )(sample_index, fields, low, high, before, after)
+    band, pred, edge, right = lax.optimization_barrier((band, pred, edge, right))
     answers = pl.pallas_call(
         interpolate_kernel,
         out_shape=shape(GROUPS, 8, LANES),
@@ -346,8 +419,6 @@
         out_specs=VMEM,
         scratch_shapes=[
             pltpu.VMEM((VC * 2 * FR, 2 * NY), BF16),
-            pltpu.VMEM((2 * NY, 2 * LANES), BF16),
-            pltpu.VMEM((VC * 2 * FR, 2 * LANES), F32),
             pltpu.VMEM((NYAW * NYAW, 8, LANES), F32),
             pltpu.VMEM((16, LANES), F32),
         ],
@@ -356,18 +427,20 @@
     )(band, asked, base, key, weight)
     planar = lax.all_to_all(answers, "group", 0, 0, tiled=True)
     return pl.pallas_call(
-        step_kernel,
+        finish_kernel,
         out_shape=shape(1, COMP, LEV, CY, NX),
-        in_specs=[SMEM] + [VMEM] * 6,
-        out_specs=VMEM,
+        in_specs=[SMEM] + [VMEM] * 5,
+        out_specs=HBM,
         scratch_shapes=[
             pltpu.VMEM((COMP, LEV, CY, LANES), F32),
+            pltpu.VMEM((COMP, LEV, CY, LANES), F32),
+            pltpu.VMEM((2, COMP, LEV, LANES), F32),
             pltpu.VMEM((COMP, LEV, CY, NX), F32),
-            pltpu.VMEM((2, COMP, LEV, NX), F32),
+            pltpu.SemaphoreType.DMA((LEV,)),
         ],
         compiler_params=params(),
-        name="step",
-    )(sample_index, fields, planar, low, high, before, after)
+        name="finish",
+    )(sample_index, fields, planar, pred, edge, right)
 
 
 def solution(mesh):

time: 53.6 us -> 50.6 us (0.944)
  blocking collectives: 13.3 us -> 24.1 us
  waiting for transfers between devices: 10.8 us -> 3.03 us
  starting transfers between devices: 20.6 us -> 15.7 us
  local copies, waits for them, and re-layouts: 2.34 us -> 0.69 us
  Pallas kernels: 5.73 us -> 6.66 us
    all_to_all x0 -> x1, blocking collectives: none -> 10.7 us  [local(): planar = lax.all_to_all(answers, 'group', 0, 0, tiled=True)]
    all_to_all x1, waiting for transfers between devices: 9.3 us -> 0.01 us  [local(): lax.all_to_all(jnp.broadcast_to(asked[0:1], (TILES, CY, LANES)), 'tile',...]
    all_to_all x1 -> x0, starting transfers between devices: 5.03 us -> none  [local(): planar = lax.all_to_all(answers, 'group', 0, 0, tiled=True)]
    ppermute x1, starting transfers between devices: 0.45 us -> 2.26 us  [local(): before = lax.ppermute(high, 'tile', up)]
    ppermute x1, starting transfers between devices: 5.31 us -> 3.57 us  [local(): after = lax.ppermute(low, 'tile', down)]
    unnamed x12, local copies, waits for them, and re-layouts: 1.67 us -> 0.02 us
    ppermute x1, waiting for transfers between devices: 1.5 us -> 3.03 us  [local(): before = lax.ppermute(high, 'tile', up)]
    pallas_call x1, Pallas kernels: 0.69 us -> 1.87 us  [local(): pl.pallas_call(pack_kernel, out_shape=(shape(GROUPS, CY, LANES), shape(CO...]
  transfers between devices with their start and end apart: 4 -> 3, of which waited for: 2 -> 1; matrix products, arithmetic and copies ran while one was open for 0% -> 0% of each run, Pallas kernels for 1% -> 3%
where the time goes in v2:
time: 50.6 us; the launch traced here: 50.3 us
  blocking collectives  24.1 us (48%)
  starting transfers between devices  15.7 us (31%)
  Pallas kernels  6.66 us (13%)
  waiting for transfers between devices  3.03 us (6%)
  local copies, waits for them, and re-layouts  0.69 us (1%)
    all_to_all x1, blocking collectives, local(): asked = lax.all_to_all(message, 'group', 0, 0, tiled=True)  13.5 us
    all_to_all x1, blocking collectives, local(): planar = lax.all_to_all(answers, 'group', 0, 0, tiled=True)  10.7 us
    all_to_all x1, starting transfers between devices, local(): lax.all_to_all(jnp.broadcast_to(asked[0:1], (TILES, CY, LANES)), 'tile',...  9.85 us
    ppermute x1, starting transfers between devices, local(): after = lax.ppermute(low, 'tile', down)  3.57 us
    ppermute x1, waiting for transfers between devices, local(): before = lax.ppermute(high, 'tile', up)  3.03 us
    ppermute x1, starting transfers between devices, local(): before = lax.ppermute(high, 'tile', up)  2.26 us
    pallas_call x1, Pallas kernels, local(): pl.pallas_call(pack_kernel, out_shape=(shape(GROUPS, CY, LANES), shape(CO...  1.87 us
    pallas_call x1, Pallas kernels, local(): pl.pallas_call(finish_kernel, out_shape=shape(1, COMP, LEV, CY, NX), in_s...  1.66 us
  transfers between devices with their start and end apart: 3, of which 1 were waited for; matrix products, arithmetic and copies ran while one was open for 0% of the time, Pallas kernels for 3%

profile of v2, /device:TPU:1, one launch (start us, length us, event | category | flops | bytes accessed | tf_op | source)
XLA Modules:
  0.0 50.3 jit_solution(16102060513733589470)
XLA Ops:
  0.0 0.0 copy-start.1
  0.0 0.0 copy-start.2
  0.0 1.9 %pack.1 = (f32[16,16,128]{2,1,0:T(8,128)}, f32[3,2,8,256]{3,2,1,0:T(8,128)}, f32[3,2,8,256]{3,2,1,0:T(8,128)}) custom-call(s32[1,3]{1,0:T(1,128)} %sample_ref.3, f32[1,3,8,16,256]{4,3,2,1,0:T(8,128)} %fields_ref.3), custom_call_target="tpu_custom_call" | custom-call | tf_op jit(solution)/shard_map/pack/pallas_call | solution.py:359
  1.9 13.5 %all_to_all.15.asked_ref = f32[16,16,128]{2,1,0:T(8,128)S(1)} all-to-all(f32[16,16,128]{2,1,0:T(8,128)} %get-tuple-element.18), channel_id=1, replica_groups=mesh['group'=16,'tile'=16] {'group'}, dimensions={0} | all-to-all | bytes 262144 | tf_op jit(solution)/shard_map/all_to_all | solution.py:376
  15.4 0.7 %broadcast_in_dim.8 = f32[16,16,128]{2,1,0:T(8,128)} broadcast(f32[16,128]{1,0:T(8,128)S(1)} %slice_bitcast_fusion), dimensions={1,2} | broadcast | bytes 139264 | tf_op jit(solution)/shard_map/broadcast_in_dim | solution.py:399
  16.0 9.9 %all-to-all-start.1 = ((f32[16,16,128]{2,1,0:T(8,128)}), f32[16,16,128]{2,1,0:T(8,128)S(1)}, u32[]{:S(2)}, u32[]{:S(2)}) async-start(f32[16,16,128]{2,1,0:T(8,128)} %broadcast_in_dim.8), calls=%async_computation.1 | async-start | bytes 262144 | tf_op jit(solution)/shard_map/all_to_all | solution.py:398
  25.9 2.3 %collective-permute-start = (f32[3,2,8,256]{3,2,1,0:T(8,128)}, f32[3,2,8,256]{3,2,1,0:T(8,128)S(1)}, u32[]{:S(2)}, u32[]{:S(2)}) collective-permute-start(f32[3,2,8,256]{3,2,1,0:T(8,128)} %get-tuple-element.20.high_ref), channel_id=1, source_target_pairs={{0,1},{1,2},{2,3},{3,4},{4,5},{5,6},{6,7},{7,8},{8,9},{9,10},{10,1... | collective-permute-start | bytes 147464 | tf_op jit(solution)/shard_map/ppermute | solution.py:374
  28.2 0.0 copy-start
  28.2 0.0 copy-start.3
  28.2 0.0 copy-start.4
  28.2 0.0 copy-start.5
  28.2 3.6 %collective-permute-start.1 = (f32[3,2,8,256]{3,2,1,0:T(8,128)}, f32[3,2,8,256]{3,2,1,0:T(8,128)S(1)}, u32[]{:S(2)}, u32[]{:S(2)}) collective-permute-start(f32[3,2,8,256]{3,2,1,0:T(8,128)} %get-tuple-element.19.low_ref), channel_id=1, source_target_pairs={{1,0},{2,1},{3,2},{4,3},{5,4},{6,5},{7,6},{8,7},{9,8},{10,9},{11,1... | collective-permute-start | bytes 147464 | tf_op jit(solution)/shard_map/ppermute | solution.py:375
  31.7 0.0 copy-done.1
  31.8 0.0 copy-done.2
  31.8 0.5 prepare.1
  32.3 3.0 %collective-permute-done.before_ref = f32[3,2,8,256]{3,2,1,0:T(8,128)S(1)} collective-permute-done((f32[3,2,8,256]{3,2,1,0:T(8,128)}, f32[3,2,8,256]{3,2,1,0:T(8,128)S(1)}, u32[]{:S(2)}, u32[]{:S(2)}) %collective-permute-start) | collective-permute-done | bytes 49184 | tf_op jit(solution)/shard_map/ppermute | solution.py:374
  35.3 0.0 collective-permute-done.1.after_ref
  35.3 0.0 copy-done
  35.3 0.0 copy-done.3
  35.3 0.0 copy-done.4
  35.3 0.0 copy-done.5
  35.3 1.1 %begin.1 = (f32[3,8,16,256]{3,2,1,0:T(8,128)S(1)}, f32[2,3,8,256]{3,2,1,0:T(8,128)S(1)}, f32[3,8,16,128]{3,2,1,0:T(8,128)S(1)}) custom-call(s32[1,3]{1,0:T(1,128)S(1)} %copy-done.5, f32[1,3,8,16,256]{4,3,2,1,0:T(8,128)S(1)} %copy-done, f32[3,2,8,256]{3,2,1,0:T(8,128)S(1)} %copy-done.3, f32[3,2,8,256]{3,2,1,0:T(8,128)S(1)} %copy-done.4, ...), custom_call_target="tpu_custom_call" | custom-call | flops 8000000 | bytes 1000000 | tf_op jit(solution)/shard_map/begin/pallas_call | solution.py:401
  36.4 0.0 all-to-all-done.1.band_ref
  36.4 1.5 %interpolate.1 = f32[16,8,128]{2,1,0:T(8,128)S(1)} custom-call(f32[16,16,128]{2,1,0:T(8,128)S(1)} %all-to-all-done.1.band_ref, f32[16,16,128]{2,1,0:T(8,128)S(1)} %all_to_all.15.asked_ref, s32[16,128]{1,0:T(8,128)S(1)} %get-tuple-element.25.base_ref, s32[4,16,128]{2,1,0:T(8,128)S(1)} %get-tuple-element.26.key_ref, f32[4,16,128]{2,1,0:T(8,128)S(1)} %get-tuple-element.27.weight_ref), custom_call_target="tpu_custom_call" | custom-call | tf_op jit(solution)/shard_map/interpolate/pallas_call | solution.py:415
  38.0 10.7 %all_to_all.16.planar_ref = f32[16,8,128]{2,1,0:T(8,128)S(1)} all-to-all(f32[16,8,128]{2,1,0:T(8,128)S(1)} %interpolate.1), channel_id=1, replica_groups=mesh['group'=16,'tile'=16] {'group'}, dimensions={0} | all-to-all | bytes 131072 | tf_op jit(solution)/shard_map/all_to_all | solution.py:428
  48.6 1.7 %finish.1 = f32[1,3,8,16,256]{4,3,2,1,0:T(8,128)} custom-call(s32[1,3]{1,0:T(1,128)S(1)} %copy-done.5, f32[1,3,8,16,256]{4,3,2,1,0:T(8,128)S(1)} %copy-done, f32[16,8,128]{2,1,0:T(8,128)S(1)} %all_to_all.16.planar_ref, f32[3,8,16,256]{3,2,1,0:T(8,128)S(1)} %get-tuple-element.28.pred_ref, f32[2,3,8,256]{3,2,1,0:T(8,128)S(1)} %get-tuple-element.29.edge_ref, ...), custom_call_target="tpu_custom_call" | custom-call | tf_op jit(solution)/shard_map/finish/pallas_call | solution.py:429
  (1 shorter events, 0.0 us)
Async XLA Ops:
  0.0 31.8 %copy-start.1 = (s32[4,256,128]{2,1,0:T(8,128)S(1)}, s32[4,256,128]{2,1,0:T(8,128)}, u32[]{:S(2)}) copy-start(s32[4,256,128]{2,1,0:T(8,128)} %stencil_ref.1) | copy-start | bytes 1572868
  0.0 31.8 %copy-start.2 = (f32[4,256,128]{2,1,0:T(8,128)S(1)}, f32[4,256,128]{2,1,0:T(8,128)}, u32[]{:S(2)}) copy-start(f32[4,256,128]{2,1,0:T(8,128)} %weight_ref.1) | copy-start | bytes 1572868
  16.0 20.4 %all-to-all-start.1 = ((f32[16,16,128]{2,1,0:T(8,128)}), f32[16,16,128]{2,1,0:T(8,128)S(1)}, u32[]{:S(2)}, u32[]{:S(2)}) async-start(f32[16,16,128]{2,1,0:T(8,128)} %broadcast_in_dim.8), calls=%async_computation.1 | async-start | bytes 262144 | tf_op jit(solution)/shard_map/all_to_all | solution.py:398
  25.9 9.4 %collective-permute-start = (f32[3,2,8,256]{3,2,1,0:T(8,128)}, f32[3,2,8,256]{3,2,1,0:T(8,128)S(1)}, u32[]{:S(2)}, u32[]{:S(2)}) collective-permute-start(f32[3,2,8,256]{3,2,1,0:T(8,128)} %get-tuple-element.20.high_ref), channel_id=1, source_target_pairs={{0,1},{1,2},{2,3},{3,4},{4,5},{5,6},{6,7},{7,8},{8,9},{9,10},{10,1... | collective-permute-start | bytes 147464 | tf_op jit(solution)/shard_map/ppermute | solution.py:374
  28.2 7.1 %copy-start = (f32[1,3,8,16,256]{4,3,2,1,0:T(8,128)S(1)}, f32[1,3,8,16,256]{4,3,2,1,0:T(8,128)}, u32[]{:S(2)}) copy-start(f32[1,3,8,16,256]{4,3,2,1,0:T(8,128)} %fields_ref.3) | copy-start | bytes 1179652
  28.2 7.1 %copy-start.3 = (f32[3,2,8,256]{3,2,1,0:T(8,128)S(1)}, f32[3,2,8,256]{3,2,1,0:T(8,128)}, u32[]{:S(2)}) copy-start(f32[3,2,8,256]{3,2,1,0:T(8,128)} %get-tuple-element.19.low_ref) | copy-start | bytes 147460
  28.2 7.1 %copy-start.4 = (f32[3,2,8,256]{3,2,1,0:T(8,128)S(1)}, f32[3,2,8,256]{3,2,1,0:T(8,128)}, u32[]{:S(2)}) copy-start(f32[3,2,8,256]{3,2,1,0:T(8,128)} %get-tuple-element.20.high_ref) | copy-start | bytes 147460
  28.2 7.1 %copy-start.5 = (s32[1,3]{1,0:T(1,128)S(1)}, s32[1,3]{1,0:T(1,128)}, u32[]{:S(2)}) copy-start(s32[1,3]{1,0:T(1,128)} %sample_ref.3) | copy-start | bytes 40
  28.2 7.1 %collective-permute-start.1 = (f32[3,2,8,256]{3,2,1,0:T(8,128)}, f32[3,2,8,256]{3,2,1,0:T(8,128)S(1)}, u32[]{:S(2)}, u32[]{:S(2)}) collective-permute-start(f32[3,2,8,256]{3,2,1,0:T(8,128)} %get-tuple-element.19.low_ref), channel_id=1, source_target_pairs={{1,0},{2,1},{3,2},{4,3},{5,4},{6,5},{7,6},{8,7},{9,8},{10,9},{11,1... | collective-permute-start | bytes 147464 | tf_op jit(solution)/shard_map/ppermute | solution.py:375

commit v3 on v2

--- a/solution.py
+++ b/solution.py
@@ -20,6 +20,7 @@
 HALF = CY // 2
 LANES = 128
 VC = NYAW * COMP
+CELLS = 2 * NYAW + 1
 
 TIME_STEP = 0.2
 YAW_STEP = 0.2
@@ -59,7 +60,7 @@
     copies = [
         [
             pltpu.make_async_copy(
-                fields_hbm.at[0, comp, :, :, lanes], fields_ref.at[comp, :, :, lanes], sems.at[1 + 3 * at + comp]
+                fields_hbm.at[comp, :, lanes], fields_ref.at[at, comp], sems.at[1 + 3 * at + comp]
             )
             for comp in range(COMP)
         ]
@@ -76,23 +77,22 @@
     for lev in range(LEV):
         packed = jnp.full((CY, LANES), combo, F32)
         for comp in range(COMP):
-            band = pltpu.roll(fields_ref[comp, lev, :, NX - LANES :], (comp + 1) * FR, 1)
+            band = pltpu.roll(fields_ref[0, comp, lev * CY : (lev + 1) * CY, :], (comp + 1) * FR, 1)
             packed = jnp.where((lane >= comp * FR) & (lane < (comp + 1) * FR), band, packed)
         msg_ref[2 * lev] = packed
         msg_ref[2 * lev + 1] = packed
     for copy in copies[1]:
         copy.wait()
-    for lev in range(LEV):
-        for comp in range(COMP):
-            for row in range(2):
-                low_ref[comp, row, lev : lev + 1, :] = fields_ref[comp, lev, row : row + 1, :]
-                high_ref[comp, row, lev : lev + 1, :] = fields_ref[
-                    comp, lev, CY - 2 + row : CY - 1 + row, :
-                ]
+    for comp in range(COMP):
+        for row in range(2):
+            for at, lanes in enumerate(halves):
+                part = fields_ref.at[at, comp]
+                low_ref[comp, row, :, lanes] = part[pl.ds(row, LEV, stride=CY), :]
+                high_ref[comp, row, :, lanes] = part[pl.ds(CY - 2 + row, LEV, stride=CY), :]
 
 
 def prepare_kernel(
-    stencil_ref, weight_ref, base_ref, key_ref, out_weight_ref, sten, wts, sten_x, wts_x, perm, sems
+    stencil_ref, weight_ref, hot_ref, spread_ref, sten, wts, sten_x, wts_x, perm, sems
 ):
     half = lax.axis_index("group") % 2
     start = lax.axis_index("tile") * CY + half * HALF
@@ -116,7 +116,7 @@
     def gathered(main, extra):
         parts = []
         for part in range(4):
-            rows = [main[yaw, part + 4 * j : part + 4 * j + 1, :] for yaw in range(NYAW) for j in range(2)]
+            rows = [main[yaw, 2 * part : 2 * part + 2, :] for yaw in range(NYAW)]
             outer = jnp.where(half == 0, extra[part, HALF - 1 : HALF, :], extra[part, 0:1, :])
             rows.append(outer)
             rows.append(jnp.zeros((7, LANES), outer.dtype))
@@ -142,16 +142,25 @@
         below = jnp.where((delta == -1.0) | (delta == NY - 1.0), 1.0, below)
     base = rows[0] - below
     base = jnp.where(base < 0.0, base + NY, base)
-    base_ref[...] = base.astype(jnp.int32)
+    keys = []
     for k in range(STEN):
         offset = rows[k] - base
         offset = jnp.where(offset < 0.0, offset + NY, offset)
-        key_ref[k] = (offset * FR + cols[k]).astype(jnp.int32)
-        out_weight_ref[k] = weight[:, k * LANES : (k + 1) * LANES]
+        keys.append(offset * FR + cols[k])
+    row_ids = row_iota(NY, LANES).astype(F32)
+    key_ids = row_iota(2 * FR, LANES).astype(F32)
+    for cell in range(CELLS):
+        lanes = slice(cell * LANES, (cell + 1) * LANES)
+        hot_ref[:, lanes] = jnp.where(row_ids == base[cell : cell + 1], 1.0, 0.0).astype(BF16)
+        spread = jnp.zeros((2 * FR, LANES), F32)
+        for k in range(STEN):
+            share = weight[cell : cell + 1, k * LANES : (k + 1) * LANES]
+            spread = spread + jnp.where(key_ids == keys[k][cell : cell + 1], share, 0.0)
+        spread_ref[:, lanes] = spread
 
 
 def interpolate_kernel(
-    band_ref, asked_ref, base_ref, key_ref, weight_ref, out_ref, table, picked, outer
+    band_ref, asked_ref, hot_ref, spread_ref, out_ref, table, picked, outer
 ):
     level = lax.axis_index("group") // 2
     band = band_ref[...].reshape(NY, LANES).T[: COMP * FR]
@@ -165,20 +174,12 @@
                 at = ((veer * COMP + comp) * 2 + step) * FR
                 table[at : at + FR, 0:NY] = upper[comp * FR : (comp + 1) * FR]
                 table[at : at + FR, NY : 2 * NY] = lower[comp * FR : (comp + 1) * FR]
-    row_ids = row_iota(NY, LANES)
-    key_ids = row_iota(2 * FR, LANES)
     for pair in range(5):
-        cells = [cell for cell in (2 * pair, 2 * pair + 1) if cell <= 2 * NYAW]
-        ones = jnp.concatenate(
-            [jnp.where(row_ids == base_ref[cell : cell + 1, :], 1.0, 0.0).astype(BF16) for cell in cells], axis=1
-        )
+        cells = [cell for cell in (2 * pair, 2 * pair + 1) if cell < CELLS]
+        ones = hot_ref[:, 2 * pair * LANES : (2 * pair + len(cells)) * LANES]
         product = jnp.dot(table[...], jnp.concatenate([ones, ones], axis=0), preferred_element_type=F32)
         for at, cell in enumerate(cells):
-            weights = jnp.zeros((2 * FR, LANES), F32)
-            for k in range(STEN):
-                weights = weights + jnp.where(
-                    key_ids == key_ref[k, cell : cell + 1, :], weight_ref[k, cell : cell + 1, :], 0.0
-                )
+            weights = spread_ref[:, cell * LANES : (cell + 1) * LANES]
             for one in range(VC):
                 value = jnp.sum(
                     product[one * 2 * FR : (one + 1) * 2 * FR, at * LANES : (at + 1) * LANES] * weights,
@@ -188,7 +189,7 @@
                 veer, comp = divmod(one, COMP)
                 if cell < 2 * NYAW:
                     yaw, j = divmod(cell, 2)
-                    picked[veer * NYAW + yaw, 2 * comp + j : 2 * comp + j + 1, :] = value
+                    picked[veer * NYAW + yaw, 4 * j + comp : 4 * j + comp + 1, :] = value
                 else:
                     outer[one : one + 1, :] = value
     lane = lane_iota(1, LANES)
@@ -199,16 +200,22 @@
                 rolled[(comp - yaw) % 4][veer * COMP + comp : veer * COMP + comp + 1] for comp in range(COMP)
             ]
             row = jnp.where(lane < FR, rows[0], jnp.where(lane < 2 * FR, rows[1], rows[2]))
-            picked[veer * NYAW + yaw, 6:7, :] = row
+            picked[veer * NYAW + yaw, 3:4, :] = row
             picked[veer * NYAW + yaw, 7:8, :] = row
     tile_lane = lane_iota(8, LANES)
     for group in range(GROUPS):
         asked = jnp.where(tile_lane >= COMP * FR, asked_ref[group, 0:8, :], 0.0)
         asked = asked + pltpu.roll(asked, FR, 1)
         asked = asked + pltpu.roll(asked, 2 * FR, 1)
-        chosen = picked[0]
-        for combo in range(1, NYAW * NYAW):
-            chosen = jnp.where(asked == float(combo), picked[combo], chosen)
+        veer_asked = jnp.floor(asked * (1.0 / NYAW))
+        yaw_asked = asked - NYAW * veer_asked
+        of_yaw = [yaw_asked == float(yaw) for yaw in range(NYAW)]
+        chosen = None
+        for veer in range(NYAW):
+            one = picked[veer * NYAW]
+            for yaw in range(1, NYAW):
+                one = jnp.where(of_yaw[yaw], picked[veer * NYAW + yaw], one)
+            chosen = one if veer == 0 else jnp.where(veer_asked == float(veer), one, chosen)
         out_ref[group] = chosen
 
 
@@ -232,7 +239,7 @@
 
 
 def begin_kernel(
-    sample_ref, fields_ref, low_ref, high_ref, before_ref, after_ref, pred_ref, edge_ref, right_ref
+    sample_ref, fields_ref, high_ref, low_ref, after_ref, before_ref, pred_ref, edge_ref, right_ref
 ):
     flag = jnp.where(lax.axis_index("group") > 0, TIME_STEP, 0.0).astype(F32)
     spacing = ((sample_ref[0, 1] + 2) * (NX // 32)).astype(F32)
@@ -291,7 +298,7 @@
 
 
 def finish_kernel(
-    sample_ref, fields_ref, planar_ref, pred_ref, edge_ref, right_ref, out_ref, target, full, edge, result, sems
+    sample_ref, fields_ref, planar_ref, pred_ref, edge_ref, right_ref, out_ref, unpacked, target, full, edge, result, sems
 ):
     flag = jnp.where(lax.axis_index("group") > 0, TIME_STEP, 0.0).astype(F32)
     yaw = sample_ref[0, 0]
@@ -310,18 +317,20 @@
             packed = planar_ref[2 * lev + half]
             for part in range(4):
                 turned = packed if part == 0 else pltpu.roll(packed, LANES - part * FR, 1)
-                for comp in range(COMP):
-                    for j in range(2):
-                        at = half * HALF + 4 * j + part
-                        target[comp, lev, at : at + 1, :] = turned[2 * comp + j : 2 * comp + j + 1]
-        first, second = target[0, lev], target[1, lev]
-        aims = [cosine * first - sine * second, sine * first + cosine * second, target[2, lev]]
+                unpacked[2 * lev + half, 8 * part : 8 * part + 8, :] = turned
+        aims = [
+            jnp.concatenate(
+                [unpacked[2 * lev + half, pl.ds(comp, HALF, stride=4), :] for half in range(2)], axis=0
+            )
+            for comp in range(COMP)
+        ]
+        aims = [cosine * aims[0] - sine * aims[1], sine * aims[0] + cosine * aims[1], aims[2]]
         for comp in range(COMP):
             pull = rate * aims[comp]
             target[comp, lev] = pull
             full[comp, lev] = pred_ref[comp, lev, :, :LANES] + pull
     for side in range(2):
-        packed = jnp.concatenate([planar_ref[2 * lev + side, 6:7, :] for lev in range(LEV)], axis=0)
+        packed = jnp.concatenate([planar_ref[2 * lev + side, 3:4, :] for lev in range(LEV)], axis=0)
         aims = [packed] + [pltpu.roll(packed, LANES - comp * FR, 1) for comp in range(1, COMP)]
         aims = [cosine * aims[0] - sine * aims[1], sine * aims[0] + cosine * aims[1], aims[2]]
         for comp in range(COMP):
@@ -363,26 +372,25 @@
         out_specs=(VMEM, VMEM, VMEM),
         scratch_shapes=[
             pltpu.SMEM((1, COMP), jnp.int32),
-            pltpu.VMEM((COMP, LEV, CY, NX), F32),
+            pltpu.VMEM((2, COMP, LEV * CY, LANES), F32),
             pltpu.SemaphoreType.DMA((7,)),
         ],
         compiler_params=params(PACK_KIB),
         name="pack",
-    )(sample_index, fields)
+    )(sample_index, fields.reshape(COMP, LEV * CY, NX))
     up = [(i, (i + 1) % TILES) for i in range(TILES)]
     down = [(j, i) for i, j in up]
+    after = lax.ppermute(low, "tile", down)
     before = lax.ppermute(high, "tile", up)
-    after = lax.ppermute(low, "tile", down)
     asked = lax.all_to_all(message, "group", 0, 0, tiled=True)
-    base, key, weight = pl.pallas_call(
+    hot, spread = pl.pallas_call(
         prepare_kernel,
         out_shape=(
-            shape(16, LANES, dtype=jnp.int32),
-            shape(STEN, 16, LANES, dtype=jnp.int32),
-            shape(STEN, 16, LANES),
+            shape(NY, CELLS * LANES, dtype=BF16),
+            shape(2 * FR, CELLS * LANES),
         ),
         in_specs=[HBM, HBM],
-        out_specs=(VMEM, VMEM, VMEM),
+        out_specs=(VMEM, VMEM),
         scratch_shapes=[
             pltpu.VMEM((NYAW, HALF, LANES), jnp.int32),
             pltpu.VMEM((NYAW, HALF, LANES), F32),
@@ -392,7 +400,7 @@
             pltpu.SemaphoreType.DMA((4,)),
         ],
         compiler_params=params(),
-        cost_estimate=cost(2 * 80 * 512 * 512, 200_000),
+        cost_estimate=cost(100_000_000_000, 200_000),
         name="prepare",
     )(stencil, stencil_weight)
     band = lax.all_to_all(
@@ -410,12 +418,12 @@
         compiler_params=params(),
         cost_estimate=cost(8_000_000, 1_000_000),
         name="begin",
-    )(sample_index, fields, low, high, before, after)
+    )(sample_index, fields, high, low, after, before)
     band, pred, edge, right = lax.optimization_barrier((band, pred, edge, right))
     answers = pl.pallas_call(
         interpolate_kernel,
         out_shape=shape(GROUPS, 8, LANES),
-        in_specs=[VMEM] * 5,
+        in_specs=[VMEM] * 4,
         out_specs=VMEM,
         scratch_shapes=[
             pltpu.VMEM((VC * 2 * FR, 2 * NY), BF16),
@@ -424,7 +432,7 @@
         ],
         compiler_params=params(),
         name="interpolate",
-    )(band, asked, base, key, weight)
+    )(band, asked, hot, spread)
     planar = lax.all_to_all(answers, "group", 0, 0, tiled=True)
     return pl.pallas_call(
         finish_kernel,
@@ -432,6 +440,7 @@
         in_specs=[SMEM] + [VMEM] * 5,
         out_specs=HBM,
         scratch_shapes=[
+            pltpu.VMEM((2 * LEV, 4 * HALF, LANES), F32),
             pltpu.VMEM((COMP, LEV, CY, LANES), F32),
             pltpu.VMEM((COMP, LEV, CY, LANES), F32),
             pltpu.VMEM((2, COMP, LEV, LANES), F32),

time: 50.6 us -> 49.8 us (0.984)
  blocking collectives: 24.1 us -> 10.5 us
  starting transfers between devices: 15.7 us -> 23.5 us
  waiting for transfers between devices: 3.03 us -> 6.71 us
  local copies, waits for them, and re-layouts: 0.69 us -> 1.96 us
    all_to_all x1 -> x0, blocking collectives: 13.5 us -> none  [local(): asked = lax.all_to_all(message, 'group', 0, 0, tiled=True)]
    all_to_all x0 -> x1, starting transfers between devices: none -> 7.48 us  [local(): asked = lax.all_to_all(message, 'group', 0, 0, tiled=True)]
    all_to_all x1, waiting for transfers between devices: 0.01 us -> 6.7 us  [local(): lax.all_to_all(jnp.broadcast_to(asked[0:1], (TILES, CY, LANES)), 'tile',...]
    ppermute x1, waiting for transfers between devices: 3.03 us -> 0.01 us  [local(): before = lax.ppermute(high, 'tile', up)]
    all_to_all x1, starting transfers between devices: 9.85 us -> 8.47 us  [local(): lax.all_to_all(jnp.broadcast_to(asked[0:1], (TILES, CY, LANES)), 'tile',...]
    unnamed x12, local copies, waits for them, and re-layouts: 0.02 us -> 1.29 us
    ppermute x1, starting transfers between devices: 3.57 us -> 4.42 us  [local(): after = lax.ppermute(low, 'tile', down)]
    ppermute x1, starting transfers between devices: 2.26 us -> 3.09 us  [local(): before = lax.ppermute(high, 'tile', up)]
  transfers between devices with their start and end apart: 3 -> 4, of which waited for: 1 -> 1; matrix products, arithmetic and copies ran while one was open for 0% -> 1% of each run, Pallas kernels for 3% -> 4%
where the time goes in v3:
time: 49.8 us; the launch traced here: 49.4 us
  starting transfers between devices  23.5 us (47%)
  blocking collectives  10.5 us (21%)
  waiting for transfers between devices  6.71 us (13%)
  Pallas kernels  6.69 us (13%)
  local copies, waits for them, and re-layouts  1.96 us (4%)
    all_to_all x1, blocking collectives, local(): planar = lax.all_to_all(answers, 'group', 0, 0, tiled=True)  10.5 us
    all_to_all x1, starting transfers between devices, local(): lax.all_to_all(jnp.broadcast_to(asked[0:1], (TILES, CY, LANES)), 'tile',...  8.47 us
    all_to_all x1, starting transfers between devices, local(): asked = lax.all_to_all(message, 'group', 0, 0, tiled=True)  7.48 us
    all_to_all x1, waiting for transfers between devices, local(): lax.all_to_all(jnp.broadcast_to(asked[0:1], (TILES, CY, LANES)), 'tile',...  6.7 us
    ppermute x1, starting transfers between devices, local(): after = lax.ppermute(low, 'tile', down)  4.42 us
    ppermute x1, starting transfers between devices, local(): before = lax.ppermute(high, 'tile', up)  3.09 us
    pallas_call x1, Pallas kernels, local(): pl.pallas_call(pack_kernel, out_shape=(shape(GROUPS, CY, LANES), shape(CO...  1.83 us
    pallas_call x1, Pallas kernels, local(): pl.pallas_call(finish_kernel, out_shape=shape(1, COMP, LEV, CY, NX), in_s...  1.61 us
  transfers between devices with their start and end apart: 4, of which 1 were waited for; matrix products, arithmetic and copies ran while one was open for 1% of the time, Pallas kernels for 4%

profile of v3, /device:TPU:1, one launch (start us, length us, event | category | flops | bytes accessed | tf_op | source)
XLA Modules:
  0.0 49.4 jit_solution(8455061837234833384)
XLA Ops:
  0.0 0.0 copy-start.4
  0.0 1.8 %pack.1 = (f32[16,16,128]{2,1,0:T(8,128)}, f32[3,2,8,256]{3,2,1,0:T(8,128)}, f32[3,2,8,256]{3,2,1,0:T(8,128)}) custom-call(s32[1,3]{1,0:T(1,128)} %sample_ref.3, f32[3,128,256]{2,1,0:T(8,128)} %bitcast.3), custom_call_target="tpu_custom_call" | custom-call | tf_op jit(solution)/shard_map/pack/pallas_call | solution.py:368
  1.8 0.0 copy-start.2
  1.8 0.0 copy-start.1
  1.9 7.5 %all-to-all-start = ((f32[16,16,128]{2,1,0:T(8,128)}), f32[16,16,128]{2,1,0:T(8,128)S(1)}, u32[]{:S(2)}, u32[]{:S(2)}) async-start(f32[16,16,128]{2,1,0:T(8,128)} %get-tuple-element.17), calls=%async_computation | async-start | bytes 262144 | tf_op jit(solution)/shard_map/all_to_all | solution.py:385
  9.3 0.0 copy-done.2
  9.3 3.1 %collective-permute-start.1 = (f32[3,2,8,256]{3,2,1,0:T(8,128)S(1)}, f32[3,2,8,256]{3,2,1,0:T(8,128)S(1)}, u32[]{:S(2)}, u32[]{:S(2)}) collective-permute-start(f32[3,2,8,256]{3,2,1,0:T(8,128)S(1)} %copy-done.2), channel_id=1, source_target_pairs={{0,1},{1,2},{2,3},{3,4},{4,5},{5,6},{6,7},{7,8},{8,9},{9,10},{10,1... | collective-permute-start | bytes 147464 | tf_op jit(solution)/shard_map/ppermute | solution.py:384
  12.4 0.0 copy-done.1
  12.4 4.4 %collective-permute-start = (f32[3,2,8,256]{3,2,1,0:T(8,128)S(1)}, f32[3,2,8,256]{3,2,1,0:T(8,128)S(1)}, u32[]{:S(2)}, u32[]{:S(2)}) collective-permute-start(f32[3,2,8,256]{3,2,1,0:T(8,128)S(1)} %copy-done.1), channel_id=1, source_target_pairs={{1,0},{2,1},{3,2},{4,3},{5,4},{6,5},{7,6},{8,7},{9,8},{10,9},{11,1... | collective-permute-start | bytes 147464 | tf_op jit(solution)/shard_map/ppermute | solution.py:383
  16.9 0.0 all-to-all-done.asked_ref
  16.9 0.7 %broadcast_in_dim.8 = f32[16,16,128]{2,1,0:T(8,128)} broadcast(f32[16,128]{1,0:T(8,128)S(1)} %slice_bitcast_fusion), dimensions={1,2} | broadcast | bytes 139264 | tf_op jit(solution)/shard_map/broadcast_in_dim | solution.py:407
  17.5 8.5 %all-to-all-start.1 = ((f32[16,16,128]{2,1,0:T(8,128)}), f32[16,16,128]{2,1,0:T(8,128)S(1)}, u32[]{:S(2)}, u32[]{:S(2)}) async-start(f32[16,16,128]{2,1,0:T(8,128)} %broadcast_in_dim.8), calls=%async_computation.1 | async-start | bytes 262144 | tf_op jit(solution)/shard_map/all_to_all | solution.py:406
  26.0 0.0 copy-done.4
  26.0 0.0 copy-start.5
  26.0 1.0 %copy-done.5 = f32[4,256,128]{2,1,0:T(8,128)S(1)} copy-done((f32[4,256,128]{2,1,0:T(8,128)S(1)}, f32[4,256,128]{2,1,0:T(8,128)}, u32[]{:S(2)}) %copy-start.5) | copy-done | bytes 524312
  27.1 0.0 copy-start
  27.1 0.0 copy-start.3
  27.1 0.7 %prepare.1 = (bf16[256,1152]{1,0:T(8,128)(2,1)S(1)}, f32[64,1152]{1,0:T(8,128)S(1)}) custom-call(s32[4,256,128]{2,1,0:T(8,128)S(1)} %copy-done.4, f32[4,256,128]{2,1,0:T(8,128)S(1)} %copy-done.5), custom_call_target="tpu_custom_call" | custom-call | flops 99999997952 | bytes 200000 | tf_op jit(solution)/shard_map/prepare/pallas_call | solution.py:386
  27.8 0.0 collective-permute-done.1.before_ref
  27.8 0.0 collective-permute-done.after_ref
  27.8 0.2 copy-done
  28.1 0.0 copy-done.3
  28.1 1.1 %begin.1 = (f32[3,8,16,256]{3,2,1,0:T(8,128)S(1)}, f32[2,3,8,256]{3,2,1,0:T(8,128)S(1)}, f32[3,8,16,128]{3,2,1,0:T(8,128)S(1)}) custom-call(s32[1,3]{1,0:T(1,128)S(1)} %copy-done.3, f32[1,3,8,16,256]{4,3,2,1,0:T(8,128)S(1)} %copy-done, f32[3,2,8,256]{3,2,1,0:T(8,128)S(1)} %copy-done.2, f32[3,2,8,256]{3,2,1,0:T(8,128)S(1)} %copy-done.1, ...), custom_call_target="tpu_custom_call" | custom-call | flops 8000000 | bytes 1000000 | tf_op jit(solution)/shard_map/begin/pallas_call | solution.py:409
  29.2 6.7 %all-to-all-done.1.band_ref = f32[16,16,128]{2,1,0:T(8,128)S(1)} async-done(((f32[16,16,128]{2,1,0:T(8,128)}), f32[16,16,128]{2,1,0:T(8,128)S(1)}, u32[]{:S(2)}, u32[]{:S(2)}) %all-to-all-start.1) | async-done | bytes 131104 | tf_op jit(solution)/shard_map/all_to_all | solution.py:406
  35.9 1.4 %interpolate.1 = f32[16,8,128]{2,1,0:T(8,128)S(1)} custom-call(f32[16,16,128]{2,1,0:T(8,128)S(1)} %all-to-all-done.1.band_ref, f32[16,16,128]{2,1,0:T(8,128)S(1)} %all-to-all-done.asked_ref, bf16[256,1152]{1,0:T(8,128)(2,1)S(1)} %get-tuple-element.24.hot_ref, f32[64,1152]{1,0:T(8,128)S(1)} %get-tuple-element.25.spread_ref), custom_call_target="tpu_custom_call" | custom-call | tf_op jit(solution)/shard_map/interpolate/pallas_call | solution.py:423
  37.3 10.5 %all_to_all.15.planar_ref = f32[16,8,128]{2,1,0:T(8,128)S(1)} all-to-all(f32[16,8,128]{2,1,0:T(8,128)S(1)} %interpolate.1), channel_id=1, replica_groups=mesh['group'=16,'tile'=16] {'group'}, dimensions={0} | all-to-all | bytes 131072 | tf_op jit(solution)/shard_map/all_to_all | solution.py:436
  47.8 1.6 %finish.1 = f32[1,3,8,16,256]{4,3,2,1,0:T(8,128)} custom-call(s32[1,3]{1,0:T(1,128)S(1)} %copy-done.3, f32[1,3,8,16,256]{4,3,2,1,0:T(8,128)S(1)} %copy-done, f32[16,8,128]{2,1,0:T(8,128)S(1)} %all_to_all.15.planar_ref, f32[3,8,16,256]{3,2,1,0:T(8,128)S(1)} %get-tuple-element.26.pred_ref, f32[2,3,8,256]{3,2,1,0:T(8,128)S(1)} %get-tuple-element.27.edge_ref, ...), custom_call_target="tpu_custom_call" | custom-call | tf_op jit(solution)/shard_map/finish/pallas_call | solution.py:437
  (1 shorter events, 0.0 us)
Async XLA Ops:
  0.0 26.0 %copy-start.4 = (s32[4,256,128]{2,1,0:T(8,128)S(1)}, s32[4,256,128]{2,1,0:T(8,128)}, u32[]{:S(2)}) copy-start(s32[4,256,128]{2,1,0:T(8,128)} %stencil_ref.1) | copy-start | bytes 1572868
  1.8 7.5 %copy-start.2 = (f32[3,2,8,256]{3,2,1,0:T(8,128)S(1)}, f32[3,2,8,256]{3,2,1,0:T(8,128)}, u32[]{:S(2)}) copy-start(f32[3,2,8,256]{3,2,1,0:T(8,128)} %get-tuple-element.18.high_ref) | copy-start | bytes 147460
  1.8 10.6 %copy-start.1 = (f32[3,2,8,256]{3,2,1,0:T(8,128)S(1)}, f32[3,2,8,256]{3,2,1,0:T(8,128)}, u32[]{:S(2)}) copy-start(f32[3,2,8,256]{3,2,1,0:T(8,128)} %get-tuple-element.19.low_ref) | copy-start | bytes 147460
  1.9 15.0 %all-to-all-start = ((f32[16,16,128]{2,1,0:T(8,128)}), f32[16,16,128]{2,1,0:T(8,128)S(1)}, u32[]{:S(2)}, u32[]{:S(2)}) async-start(f32[16,16,128]{2,1,0:T(8,128)} %get-tuple-element.17), calls=%async_computation | async-start | bytes 262144 | tf_op jit(solution)/shard_map/all_to_all | solution.py:385
  9.3 18.5 %collective-permute-start.1 = (f32[3,2,8,256]{3,2,1,0:T(8,128)S(1)}, f32[3,2,8,256]{3,2,1,0:T(8,128)S(1)}, u32[]{:S(2)}, u32[]{:S(2)}) collective-permute-start(f32[3,2,8,256]{3,2,1,0:T(8,128)S(1)} %copy-done.2), channel_id=1, source_target_pairs={{0,1},{1,2},{2,3},{3,4},{4,5},{5,6},{6,7},{7,8},{8,9},{9,10},{10,1... | collective-permute-start | bytes 147464 | tf_op jit(solution)/shard_map/ppermute | solution.py:384
  12.4 15.4 %collective-permute-start = (f32[3,2,8,256]{3,2,1,0:T(8,128)S(1)}, f32[3,2,8,256]{3,2,1,0:T(8,128)S(1)}, u32[]{:S(2)}, u32[]{:S(2)}) collective-permute-start(f32[3,2,8,256]{3,2,1,0:T(8,128)S(1)} %copy-done.1), channel_id=1, source_target_pairs={{1,0},{2,1},{3,2},{4,3},{5,4},{6,5},{7,6},{8,7},{9,8},{10,9},{11,1... | collective-permute-start | bytes 147464 | tf_op jit(solution)/shard_map/ppermute | solution.py:383
  17.5 18.3 %all-to-all-start.1 = ((f32[16,16,128]{2,1,0:T(8,128)}), f32[16,16,128]{2,1,0:T(8,128)S(1)}, u32[]{:S(2)}, u32[]{:S(2)}) async-start(f32[16,16,128]{2,1,0:T(8,128)} %broadcast_in_dim.8), calls=%async_computation.1 | async-start | bytes 262144 | tf_op jit(solution)/shard_map/all_to_all | solution.py:406
  26.0 1.0 %copy-start.5 = (f32[4,256,128]{2,1,0:T(8,128)S(1)}, f32[4,256,128]{2,1,0:T(8,128)}, u32[]{:S(2)}) copy-start(f32[4,256,128]{2,1,0:T(8,128)} %weight_ref.1) | copy-start | bytes 1572868
  27.1 1.0 %copy-start = (f32[1,3,8,16,256]{4,3,2,1,0:T(8,128)S(1)}, f32[1,3,8,16,256]{4,3,2,1,0:T(8,128)}, u32[]{:S(2)}) copy-start(f32[1,3,8,16,256]{4,3,2,1,0:T(8,128)} %fields_ref.3) | copy-start | bytes 1179652
  27.1 1.0 %copy-start.3 = (s32[1,3]{1,0:T(1,128)S(1)}, s32[1,3]{1,0:T(1,128)}, u32[]{:S(2)}) copy-start(s32[1,3]{1,0:T(1,128)} %sample_ref.3) | copy-start | bytes 40

commit v4 on v3

--- a/solution.py
+++ b/solution.py
@@ -19,7 +19,6 @@
 TILES = NY // CY
 HALF = CY // 2
 LANES = 128
-VC = NYAW * COMP
 CELLS = 2 * NYAW + 1
 
 TIME_STEP = 0.2
@@ -73,14 +72,16 @@
         copy.wait()
     sample_copy.wait()
     combo = (sample_ref[0, 2] * NYAW + sample_ref[0, 0]).astype(F32)
-    lane = lane_iota(CY, LANES)
+    lane = lane_iota(HALF, LANES)
     for lev in range(LEV):
-        packed = jnp.full((CY, LANES), combo, F32)
-        for comp in range(COMP):
-            band = pltpu.roll(fields_ref[0, comp, lev * CY : (lev + 1) * CY, :], (comp + 1) * FR, 1)
-            packed = jnp.where((lane >= comp * FR) & (lane < (comp + 1) * FR), band, packed)
-        msg_ref[2 * lev] = packed
-        msg_ref[2 * lev + 1] = packed
+        bands = [fields_ref[0, comp, lev * CY : (lev + 1) * CY, :] for comp in range(COMP)]
+        for at in range(2):
+            packed = pltpu.roll(bands[at][:HALF], FR, 1)
+            packed = jnp.where(lane < FR, packed, pltpu.roll(bands[2][:HALF], 2 * FR, 1))
+            packed = jnp.where(lane < 2 * FR, packed, pltpu.roll(bands[at][HALF:], 3 * FR, 1))
+            packed = jnp.where(lane < 3 * FR, packed, bands[2][HALF:])
+            msg_ref[2 * lev + at, 0:HALF, :] = packed
+            msg_ref[2 * lev + at, HALF:CY, :] = jnp.full((HALF, LANES), combo, F32)
     for copy in copies[1]:
         copy.wait()
     for comp in range(COMP):
@@ -94,17 +95,19 @@
 def prepare_kernel(
     stencil_ref, weight_ref, hot_ref, spread_ref, sten, wts, sten_x, wts_x, perm, sems
 ):
-    half = lax.axis_index("group") % 2
-    start = lax.axis_index("tile") * CY + half * HALF
-    beyond = (start + jnp.where(half == 0, NY - HALF, HALF)) % NY
-    start = pl.multiple_of(start, HALF)
-    beyond = pl.multiple_of(beyond, HALF)
-    copies = [
-        pltpu.make_async_copy(stencil_ref.at[:, pl.ds(start, HALF), :], sten, sems.at[0]),
-        pltpu.make_async_copy(weight_ref.at[:, pl.ds(start, HALF), :], wts, sems.at[1]),
-        pltpu.make_async_copy(stencil_ref.at[:, pl.ds(beyond, HALF), :], sten_x, sems.at[2]),
-        pltpu.make_async_copy(weight_ref.at[:, pl.ds(beyond, HALF), :], wts_x, sems.at[3]),
-    ]
+    halves = [lax.axis_index("group") % 2, 1 - lax.axis_index("group") % 2]
+    copies = []
+    for slot, half in enumerate(halves):
+        start = lax.axis_index("tile") * CY + half * HALF
+        beyond = (start + jnp.where(half == 0, NY - HALF, HALF)) % NY
+        start = pl.multiple_of(start, HALF)
+        beyond = pl.multiple_of(beyond, HALF)
+        copies += [
+            pltpu.make_async_copy(stencil_ref.at[:, pl.ds(start, HALF), :], sten.at[slot], sems.at[slot, 0]),
+            pltpu.make_async_copy(weight_ref.at[:, pl.ds(start, HALF), :], wts.at[slot], sems.at[slot, 1]),
+            pltpu.make_async_copy(stencil_ref.at[:, pl.ds(beyond, HALF), :], sten_x.at[slot], sems.at[slot, 2]),
+            pltpu.make_async_copy(weight_ref.at[:, pl.ds(beyond, HALF), :], wts_x.at[slot], sems.at[slot, 3]),
+        ]
     for copy in copies:
         copy.start()
     source = row_iota(512, 512)
@@ -116,10 +119,14 @@
     def gathered(main, extra):
         parts = []
         for part in range(4):
-            rows = [main[yaw, 2 * part : 2 * part + 2, :] for yaw in range(NYAW)]
-            outer = jnp.where(half == 0, extra[part, HALF - 1 : HALF, :], extra[part, 0:1, :])
-            rows.append(outer)
-            rows.append(jnp.zeros((7, LANES), outer.dtype))
+            rows = []
+            for slot, half in enumerate(halves):
+                rows += [main[slot, yaw, 2 * part : 2 * part + 2, :] for yaw in range(NYAW)]
+                outer = jnp.where(
+                    half == 0, extra[slot, part, HALF - 1 : HALF, :], extra[slot, part, 0:1, :]
+                )
+                rows.append(outer)
+                rows.append(jnp.zeros((7, LANES), outer.dtype))
             parts.append(jnp.concatenate(rows, axis=0))
         return jnp.concatenate(parts, axis=1)
 
@@ -133,10 +140,10 @@
     source_col = (index & 31).astype(F32).astype(BF16)
     stacked = jnp.concatenate([source_row, source_col, first, second, third], axis=0)
     sorted_ = jnp.dot(stacked, perm[...], preferred_element_type=F32)
-    weight = (sorted_[32:48] + sorted_[48:64]) + sorted_[64:80]
-    rows = [sorted_[0:16, k * LANES : (k + 1) * LANES] for k in range(STEN)]
-    cols = [sorted_[16:32, k * LANES : (k + 1) * LANES] for k in range(STEN)]
-    below = jnp.zeros((16, LANES), F32)
+    weight = (sorted_[64:96] + sorted_[96:128]) + sorted_[128:160]
+    rows = [sorted_[0:32, k * LANES : (k + 1) * LANES] for k in range(STEN)]
+    cols = [sorted_[32:64, k * LANES : (k + 1) * LANES] for k in range(STEN)]
+    below = jnp.zeros((32, LANES), F32)
     for k in range(1, STEN):
         delta = rows[k] - rows[0]
         below = jnp.where((delta == -1.0) | (delta == NY - 1.0), 1.0, below)
@@ -149,13 +156,14 @@
         keys.append(offset * FR + cols[k])
     row_ids = row_iota(NY, LANES).astype(F32)
     key_ids = row_iota(2 * FR, LANES).astype(F32)
-    for cell in range(CELLS):
+    for cell in range(2 * CELLS):
+        at = 16 * (cell // CELLS) + cell % CELLS
         lanes = slice(cell * LANES, (cell + 1) * LANES)
-        hot_ref[:, lanes] = jnp.where(row_ids == base[cell : cell + 1], 1.0, 0.0).astype(BF16)
+        hot_ref[:, lanes] = jnp.where(row_ids == base[at : at + 1], 1.0, 0.0).astype(BF16)
         spread = jnp.zeros((2 * FR, LANES), F32)
         for k in range(STEN):
-            share = weight[cell : cell + 1, k * LANES : (k + 1) * LANES]
-            spread = spread + jnp.where(key_ids == keys[k][cell : cell + 1], share, 0.0)
+            share = weight[at : at + 1, k * LANES : (k + 1) * LANES]
+            spread = spread + jnp.where(key_ids == keys[k][at : at + 1], share, 0.0)
         spread_ref[:, lanes] = spread
 
 
@@ -163,35 +171,47 @@
     band_ref, asked_ref, hot_ref, spread_ref, out_ref, table, picked, outer
 ):
     level = lax.axis_index("group") // 2
-    band = band_ref[...].reshape(NY, LANES).T[: COMP * FR]
+    blocks = []
+    for tile in range(TILES):
+        block = band_ref[tile]
+        blocks += [block, pltpu.roll(block, 2 * FR, 1)]
+    band = jnp.concatenate(blocks, axis=0).T[: 2 * FR]
+    rows = NYAW * 2 * FR
     for veer in range(NYAW):
         for step in range(2):
             shift = (NY - (veer * (level + 1) * (CY // 4) + step)) % NY
             moved = band if veer + step == 0 else pltpu.roll(band, shift, 1)
             upper = moved.astype(BF16)
             lower = (moved - upper.astype(F32)).astype(BF16)
-            for comp in range(COMP):
-                at = ((veer * COMP + comp) * 2 + step) * FR
-                table[at : at + FR, 0:NY] = upper[comp * FR : (comp + 1) * FR]
-                table[at : at + FR, NY : 2 * NY] = lower[comp * FR : (comp + 1) * FR]
-    for pair in range(5):
-        cells = [cell for cell in (2 * pair, 2 * pair + 1) if cell < CELLS]
-        ones = hot_ref[:, 2 * pair * LANES : (2 * pair + len(cells)) * LANES]
-        product = jnp.dot(table[...], jnp.concatenate([ones, ones], axis=0), preferred_element_type=F32)
-        for at, cell in enumerate(cells):
-            weights = spread_ref[:, cell * LANES : (cell + 1) * LANES]
-            for one in range(VC):
-                value = jnp.sum(
-                    product[one * 2 * FR : (one + 1) * 2 * FR, at * LANES : (at + 1) * LANES] * weights,
-                    axis=0,
-                    keepdims=True,
-                )
-                veer, comp = divmod(one, COMP)
-                if cell < 2 * NYAW:
-                    yaw, j = divmod(cell, 2)
-                    picked[veer * NYAW + yaw, 4 * j + comp : 4 * j + comp + 1, :] = value
-                else:
-                    outer[one : one + 1, :] = value
+            for plane in range(2):
+                at = plane * rows + (veer * 2 + step) * FR
+                table[at : at + FR, 0:NY] = upper[plane * FR : (plane + 1) * FR]
+                table[at : at + FR, NY : 2 * NY] = lower[plane * FR : (plane + 1) * FR]
+    for slot in range(2):
+        planes = 2 - slot
+        for pair in range(5):
+            cells = [cell for cell in (2 * pair, 2 * pair + 1) if cell < CELLS]
+            first = slot * CELLS + 2 * pair
+            ones = hot_ref[:, first * LANES : (first + len(cells)) * LANES]
+            product = jnp.dot(
+                table[0 : planes * rows], jnp.concatenate([ones, ones], axis=0), preferred_element_type=F32
+            )
+            for at, cell in enumerate(cells):
+                weights = spread_ref[:, (first + at) * LANES : (first + at + 1) * LANES]
+                for plane in range(planes):
+                    kind = 2 if plane == 1 else slot
+                    for veer in range(NYAW):
+                        top = plane * rows + veer * 2 * FR
+                        value = jnp.sum(
+                            product[top : top + 2 * FR, at * LANES : (at + 1) * LANES] * weights,
+                            axis=0,
+                            keepdims=True,
+                        )
+                        if cell < 2 * NYAW:
+                            yaw, j = divmod(cell, 2)
+                            picked[veer * NYAW + yaw, 4 * j + kind : 4 * j + kind + 1, :] = value
+                        else:
+                            outer[veer * COMP + kind : veer * COMP + kind + 1, :] = value
     lane = lane_iota(1, LANES)
     rolled = [outer[...] if turn == 0 else pltpu.roll(outer[...], turn * FR, 1) for turn in range(4)]
     for veer in range(NYAW):
@@ -202,11 +222,8 @@
             row = jnp.where(lane < FR, rows[0], jnp.where(lane < 2 * FR, rows[1], rows[2]))
             picked[veer * NYAW + yaw, 3:4, :] = row
             picked[veer * NYAW + yaw, 7:8, :] = row
-    tile_lane = lane_iota(8, LANES)
     for group in range(GROUPS):
-        asked = jnp.where(tile_lane >= COMP * FR, asked_ref[group, 0:8, :], 0.0)
-        asked = asked + pltpu.roll(asked, FR, 1)
-        asked = asked + pltpu.roll(asked, 2 * FR, 1)
+        asked = asked_ref[group, HALF:CY, :]
         veer_asked = jnp.floor(asked * (1.0 / NYAW))
         yaw_asked = asked - NYAW * veer_asked
         of_yaw = [yaw_asked == float(yaw) for yaw in range(NYAW)]
@@ -239,11 +256,23 @@
 
 
 def begin_kernel(
-    sample_ref, fields_ref, high_ref, low_ref, after_ref, before_ref, pred_ref, edge_ref, right_ref
+    sample_ref, fields_ref, high_ref, low_ref, after_ref, before_ref, pred_ref, edge_ref, right_ref, const_ref
 ):
     flag = jnp.where(lax.axis_index("group") > 0, TIME_STEP, 0.0).astype(F32)
     spacing = ((sample_ref[0, 1] + 2) * (NX // 32)).astype(F32)
     rate, drag = rates(flag, spacing)
+    yaw = sample_ref[0, 0]
+    angles = np.float32(YAW_STEP) * (np.arange(NYAW, dtype=np.float32) - np.float32(1.5))
+    cosine = jnp.float32(np.cos(angles[0]))
+    sine = jnp.float32(np.sin(angles[0]))
+    for at in range(1, NYAW):
+        cosine = jnp.where(yaw == at, jnp.float32(np.cos(angles[at])), cosine)
+        sine = jnp.where(yaw == at, jnp.float32(np.sin(angles[at])), sine)
+    const_ref[0:CY, :] = drag[:, :LANES]
+    const_ref[CY : CY + 1, :] = rate
+    const_ref[CY + 1 : CY + 2, :] = jnp.full((1, LANES), cosine, F32)
+    const_ref[CY + 2 : CY + 3, :] = jnp.full((1, LANES), sine, F32)
+    const_ref[CY + 3 : CY + 8, :] = jnp.zeros((5, LANES), F32)
     rate = jnp.concatenate([rate, jnp.zeros((1, LANES), F32)], axis=1)
     row = row_iota(CY, NX)
 
@@ -298,19 +327,12 @@
 
 
 def finish_kernel(
-    sample_ref, fields_ref, planar_ref, pred_ref, edge_ref, right_ref, out_ref, unpacked, target, full, edge, result, sems
+    const_ref, fields_ref, planar_ref, pred_ref, edge_ref, right_ref, out_ref, unpacked, target, full, edge, result, sems
 ):
-    flag = jnp.where(lax.axis_index("group") > 0, TIME_STEP, 0.0).astype(F32)
-    yaw = sample_ref[0, 0]
-    angles = np.float32(YAW_STEP) * (np.arange(NYAW, dtype=np.float32) - np.float32(1.5))
-    cosine = jnp.float32(np.cos(angles[0]))
-    sine = jnp.float32(np.sin(angles[0]))
-    for at in range(1, NYAW):
-        cosine = jnp.where(yaw == at, jnp.float32(np.cos(angles[at])), cosine)
-        sine = jnp.where(yaw == at, jnp.float32(np.sin(angles[at])), sine)
-    spacing = ((sample_ref[0, 1] + 2) * (NX // 32)).astype(F32)
-    rate, drag = rates(flag, spacing)
-    drag = drag[:, :LANES]
+    drag = const_ref[0:CY, :]
+    rate = const_ref[CY : CY + 1, :]
+    cosine = const_ref[CY + 1 : CY + 2, :]
+    sine = const_ref[CY + 2 : CY + 3, :]
 
     for lev in range(LEV):
         for half in range(2):
@@ -318,20 +340,29 @@
             for part in range(4):
                 turned = packed if part == 0 else pltpu.roll(packed, LANES - part * FR, 1)
                 unpacked[2 * lev + half, 8 * part : 8 * part + 8, :] = turned
-        aims = [
-            jnp.concatenate(
-                [unpacked[2 * lev + half, pl.ds(comp, HALF, stride=4), :] for half in range(2)], axis=0
-            )
-            for comp in range(COMP)
-        ]
+        aims = []
+        for comp in range(COMP):
+            parts = []
+            for half in range(2):
+                origin = comp if comp < 2 else half
+                kind = 2 if comp == 2 else (half + comp) % 2
+                parts.append(unpacked[2 * lev + origin, pl.ds(kind, HALF, stride=4), :])
+            aims.append(jnp.concatenate(parts, axis=0))
         aims = [cosine * aims[0] - sine * aims[1], sine * aims[0] + cosine * aims[1], aims[2]]
         for comp in range(COMP):
             pull = rate * aims[comp]
             target[comp, lev] = pull
             full[comp, lev] = pred_ref[comp, lev, :, :LANES] + pull
+    outer = [
+        jnp.concatenate([planar_ref[2 * lev + at, 3:4, :] for lev in range(LEV)], axis=0) for at in range(2)
+    ]
     for side in range(2):
-        packed = jnp.concatenate([planar_ref[2 * lev + side, 3:4, :] for lev in range(LEV)], axis=0)
-        aims = [packed] + [pltpu.roll(packed, LANES - comp * FR, 1) for comp in range(1, COMP)]
+        aims = []
+        for comp in range(COMP):
+            origin = comp if comp < 2 else side
+            kind = 2 if comp == 2 else (side + comp) % 2
+            packed = outer[origin]
+            aims.append(packed if kind == 0 else pltpu.roll(packed, LANES - kind * FR, 1))
         aims = [cosine * aims[0] - sine * aims[1], sine * aims[0] + cosine * aims[1], aims[2]]
         for comp in range(COMP):
             edge[side, comp] = edge_ref[side, comp, :, :LANES] + rate * aims[comp]
@@ -386,47 +417,48 @@
     hot, spread = pl.pallas_call(
         prepare_kernel,
         out_shape=(
-            shape(NY, CELLS * LANES, dtype=BF16),
-            shape(2 * FR, CELLS * LANES),
+            shape(NY, 2 * CELLS * LANES, dtype=BF16),
+            shape(2 * FR, 2 * CELLS * LANES),
         ),
         in_specs=[HBM, HBM],
         out_specs=(VMEM, VMEM),
         scratch_shapes=[
-            pltpu.VMEM((NYAW, HALF, LANES), jnp.int32),
-            pltpu.VMEM((NYAW, HALF, LANES), F32),
-            pltpu.VMEM((NYAW, HALF, LANES), jnp.int32),
-            pltpu.VMEM((NYAW, HALF, LANES), F32),
+            pltpu.VMEM((2, NYAW, HALF, LANES), jnp.int32),
+            pltpu.VMEM((2, NYAW, HALF, LANES), F32),
+            pltpu.VMEM((2, NYAW, HALF, LANES), jnp.int32),
+            pltpu.VMEM((2, NYAW, HALF, LANES), F32),
             pltpu.VMEM((512, 512), BF16),
-            pltpu.SemaphoreType.DMA((4,)),
+            pltpu.SemaphoreType.DMA((2, 4)),
         ],
         compiler_params=params(),
         cost_estimate=cost(100_000_000_000, 200_000),
         name="prepare",
     )(stencil, stencil_weight)
     band = lax.all_to_all(
-        jnp.broadcast_to(asked[0:1], (TILES, CY, LANES)), "tile", 0, 0, tiled=True
+        jnp.broadcast_to(asked[0:1, :HALF], (TILES, HALF, LANES)), "tile", 0, 0, tiled=True
     )
-    pred, edge, right = pl.pallas_call(
+    pred, edge, right, const = pl.pallas_call(
         begin_kernel,
         out_shape=(
             shape(COMP, LEV, CY, NX),
             shape(2, COMP, LEV, NX),
             shape(COMP, LEV, CY, LANES),
+            shape(CY + 8, LANES),
         ),
         in_specs=[SMEM] + [VMEM] * 5,
-        out_specs=(VMEM, VMEM, VMEM),
+        out_specs=(VMEM, VMEM, VMEM, VMEM),
         compiler_params=params(),
         cost_estimate=cost(8_000_000, 1_000_000),
         name="begin",
     )(sample_index, fields, high, low, after, before)
-    band, pred, edge, right = lax.optimization_barrier((band, pred, edge, right))
+    band, pred, edge, right, const = lax.optimization_barrier((band, pred, edge, right, const))
     answers = pl.pallas_call(
         interpolate_kernel,
         out_shape=shape(GROUPS, 8, LANES),
         in_specs=[VMEM] * 4,
         out_specs=VMEM,
         scratch_shapes=[
-            pltpu.VMEM((VC * 2 * FR, 2 * NY), BF16),
+            pltpu.VMEM((NYAW * 4 * FR, 2 * NY), BF16),
             pltpu.VMEM((NYAW * NYAW, 8, LANES), F32),
             pltpu.VMEM((16, LANES), F32),
         ],
@@ -437,7 +469,7 @@
     return pl.pallas_call(
         finish_kernel,
         out_shape=shape(1, COMP, LEV, CY, NX),
-        in_specs=[SMEM] + [VMEM] * 5,
+        in_specs=[VMEM] * 6,
         out_specs=HBM,
         scratch_shapes=[
             pltpu.VMEM((2 * LEV, 4 * HALF, LANES), F32),
@@ -449,7 +481,7 @@
         ],
         compiler_params=params(),
         name="finish",
-    )(sample_index, fields, planar, pred, edge, right)
+    )(const, fields, planar, pred, edge, right)
 
 
 def solution(mesh):

time: 49.8 us -> 48.6 us (0.976)
  waiting for transfers between devices: 6.71 us -> 4.66 us
  local copies, waits for them, and re-layouts: 1.96 us -> 2.73 us
    all_to_all x1, waiting for transfers between devices: 6.7 us -> 4.65 us  [local(): lax.all_to_all(jnp.broadcast_to(asked[0:1, :HALF], (TILES, HALF, LANES)),...]
    unnamed x12, local copies, waits for them, and re-layouts: 1.29 us -> 2.09 us
    pallas_call x1, Pallas kernels: 1.61 us -> 1.06 us  [local(): pl.pallas_call(finish_kernel, out_shape=shape(1, COMP, LEV, CY, NX), in_s...]
  transfers between devices with their start and end apart: 4 -> 4, of which waited for: 1 -> 1; matrix products, arithmetic and copies ran while one was open for 1% -> 1% of each run, Pallas kernels for 4% -> 5%
where the time goes in v4:
time: 48.6 us; the launch traced here: 48.2 us
  starting transfers between devices  23.3 us (48%)
  blocking collectives  10.8 us (22%)
  Pallas kernels  6.55 us (13%)
  waiting for transfers between devices  4.66 us (10%)
  local copies, waits for them, and re-layouts  2.73 us (6%)
    all_to_all x1, blocking collectives, local(): planar = lax.all_to_all(answers, 'group', 0, 0, tiled=True)  10.8 us
    all_to_all x1, starting transfers between devices, local(): lax.all_to_all(jnp.broadcast_to(asked[0:1, :HALF], (TILES, HALF, LANES)),...  8.59 us
    all_to_all x1, starting transfers between devices, local(): asked = lax.all_to_all(message, 'group', 0, 0, tiled=True)  7.35 us
    all_to_all x1, waiting for transfers between devices, local(): lax.all_to_all(jnp.broadcast_to(asked[0:1, :HALF], (TILES, HALF, LANES)),...  4.65 us
    ppermute x1, starting transfers between devices, local(): after = lax.ppermute(low, 'tile', down)  4.41 us
    ppermute x1, starting transfers between devices, local(): before = lax.ppermute(high, 'tile', up)  2.99 us
    unnamed x12, local copies, waits for them, and re-layouts  2.09 us
    pallas_call x1, Pallas kernels, local(): pl.pallas_call(pack_kernel, out_shape=(shape(GROUPS, CY, LANES), shape(CO...  1.76 us
  transfers between devices with their start and end apart: 4, of which 1 were waited for; matrix products, arithmetic and copies ran while one was open for 1% of the time, Pallas kernels for 5%

profile of v4, /device:TPU:1, one launch (start us, length us, event | category | flops | bytes accessed | tf_op | source)
XLA Modules:
  0.0 48.2 jit_solution(4229803552871248698)
XLA Ops:
  0.0 1.8 %pack.1 = (f32[16,16,128]{2,1,0:T(8,128)}, f32[3,2,8,256]{3,2,1,0:T(8,128)}, f32[3,2,8,256]{3,2,1,0:T(8,128)}) custom-call(s32[1,3]{1,0:T(1,128)} %sample_ref.1, f32[3,128,256]{2,1,0:T(8,128)} %bitcast.3), custom_call_target="tpu_custom_call" | custom-call | tf_op jit(solution)/shard_map/pack/pallas_call | solution.py:399
  1.8 7.4 %all-to-all-start = ((f32[16,16,128]{2,1,0:T(8,128)}), f32[16,16,128]{2,1,0:T(8,128)S(1)}, u32[]{:S(2)}, u32[]{:S(2)}) async-start(f32[16,16,128]{2,1,0:T(8,128)} %get-tuple-element.19), calls=%async_computation | async-start | bytes 262144 | tf_op jit(solution)/shard_map/all_to_all | solution.py:416
  9.1 3.0 %collective-permute-start.1 = (f32[3,2,8,256]{3,2,1,0:T(8,128)}, f32[3,2,8,256]{3,2,1,0:T(8,128)S(1)}, u32[]{:S(2)}, u32[]{:S(2)}) collective-permute-start(f32[3,2,8,256]{3,2,1,0:T(8,128)} %get-tuple-element.20.high_ref), channel_id=1, source_target_pairs={{0,1},{1,2},{2,3},{3,4},{4,5},{5,6},{6,7},{7,8},{8,9},{9,10},{10,1... | collective-permute-start | bytes 147464 | tf_op jit(solution)/shard_map/ppermute | solution.py:415
  12.1 4.4 %collective-permute-start = (f32[3,2,8,256]{3,2,1,0:T(8,128)}, f32[3,2,8,256]{3,2,1,0:T(8,128)S(1)}, u32[]{:S(2)}, u32[]{:S(2)}) collective-permute-start(f32[3,2,8,256]{3,2,1,0:T(8,128)} %get-tuple-element.21.low_ref), channel_id=1, source_target_pairs={{1,0},{2,1},{3,2},{4,3},{5,4},{6,5},{7,6},{8,7},{9,8},{10,9},{11,1... | collective-permute-start | bytes 147464 | tf_op jit(solution)/shard_map/ppermute | solution.py:414
  16.5 0.0 all-to-all-done.asked_ref
  16.5 0.6 %broadcast_in_dim.8 = f32[16,8,128]{2,1,0:T(8,128)} broadcast(f32[8,128]{1,0:T(8,128)S(1)} %slice_bitcast_fusion), dimensions={1,2} | broadcast | bytes 69632 | tf_op jit(solution)/shard_map/broadcast_in_dim | solution.py:438
  17.2 8.6 %all-to-all-start.1 = ((f32[16,8,128]{2,1,0:T(8,128)}), f32[16,8,128]{2,1,0:T(8,128)S(1)}, u32[]{:S(2)}, u32[]{:S(2)}) async-start(f32[16,8,128]{2,1,0:T(8,128)} %broadcast_in_dim.8), calls=%async_computation.1 | async-start | bytes 131072 | tf_op jit(solution)/shard_map/all_to_all | solution.py:437
  25.8 0.0 copy-start.4
  25.8 1.0 %copy-done.4 = s32[4,256,128]{2,1,0:T(8,128)S(1)} copy-done((s32[4,256,128]{2,1,0:T(8,128)S(1)}, s32[4,256,128]{2,1,0:T(8,128)}, u32[]{:S(2)}) %copy-start.4) | copy-done | bytes 524312
  26.8 0.0 copy-start.5
  26.8 1.0 %copy-done.5 = f32[4,256,128]{2,1,0:T(8,128)S(1)} copy-done((f32[4,256,128]{2,1,0:T(8,128)S(1)}, f32[4,256,128]{2,1,0:T(8,128)}, u32[]{:S(2)}) %copy-start.5) | copy-done | bytes 524312
  27.9 0.0 copy-start
  27.9 0.0 copy-start.1
  27.9 0.0 copy-start.2
  27.9 0.0 copy-start.3
  27.9 1.1 %prepare.1 = (bf16[256,2304]{1,0:T(8,128)(2,1)S(1)}, f32[64,2304]{1,0:T(8,128)S(1)}) custom-call(s32[4,256,128]{2,1,0:T(8,128)S(1)} %copy-done.4, f32[4,256,128]{2,1,0:T(8,128)S(1)} %copy-done.5), custom_call_target="tpu_custom_call" | custom-call | flops 99999997952 | bytes 200000 | tf_op jit(solution)/shard_map/prepare/pallas_call | solution.py:417
  29.0 0.0 collective-permute-done.1.before_ref
  29.0 0.0 collective-permute-done.after_ref
  29.0 0.0 copy-done
  29.0 0.0 copy-done.1
  29.0 0.0 copy-done.2
  29.0 0.0 copy-done.3
  29.0 1.1 %begin.1 = (f32[3,8,16,256]{3,2,1,0:T(8,128)S(1)}, f32[2,3,8,256]{3,2,1,0:T(8,128)S(1)}, f32[3,8,16,128]{3,2,1,0:T(8,128)S(1)}, f32[24,128]{1,0:T(8,128)S(1)}) custom-call(s32[1,3]{1,0:T(1,128)S(1)} %copy-done.3, f32[1,3,8,16,256]{4,3,2,1,0:T(8,128)S(1)} %copy-done, f32[3,2,8,256]{3,2,1,0:T(8,128)S(1)} %copy-done.2, f32[3,2,8,256]{3,2,1,0:T(8,128)S(1)} %copy-done.1, ...), custom_call_target="tpu_custom_call" | custom-call | flops 8000000 | bytes 1000000 | tf_op jit(solution)/shard_map/begin/pallas_call | solution.py:440
  30.1 4.7 %all-to-all-done.1.band_ref = f32[16,8,128]{2,1,0:T(8,128)S(1)} async-done(((f32[16,8,128]{2,1,0:T(8,128)}), f32[16,8,128]{2,1,0:T(8,128)S(1)}, u32[]{:S(2)}, u32[]{:S(2)}) %all-to-all-start.1) | async-done | bytes 65568 | tf_op jit(solution)/shard_map/all_to_all | solution.py:437
  34.8 1.5 %interpolate.1 = f32[16,8,128]{2,1,0:T(8,128)S(1)} custom-call(f32[16,8,128]{2,1,0:T(8,128)S(1)} %all-to-all-done.1.band_ref, f32[16,16,128]{2,1,0:T(8,128)S(1)} %all-to-all-done.asked_ref, bf16[256,2304]{1,0:T(8,128)(2,1)S(1)} %get-tuple-element.28.hot_ref, f32[64,2304]{1,0:T(8,128)S(1)} %get-tuple-element.29.spread_ref), custom_call_target="tpu_custom_call" | custom-call | tf_op jit(solution)/shard_map/interpolate/pallas_call | solution.py:455
  36.3 10.8 %all_to_all.15.planar_ref = f32[16,8,128]{2,1,0:T(8,128)S(1)} all-to-all(f32[16,8,128]{2,1,0:T(8,128)S(1)} %interpolate.1), channel_id=1, replica_groups=mesh['group'=16,'tile'=16] {'group'}, dimensions={0} | all-to-all | bytes 131072 | tf_op jit(solution)/shard_map/all_to_all | solution.py:468
  47.1 1.1 %finish.1 = f32[1,3,8,16,256]{4,3,2,1,0:T(8,128)} custom-call(f32[24,128]{1,0:T(8,128)S(1)} %get-tuple-element.26.const_ref, f32[1,3,8,16,256]{4,3,2,1,0:T(8,128)S(1)} %copy-done, f32[16,8,128]{2,1,0:T(8,128)S(1)} %all_to_all.15.planar_ref, f32[3,8,16,256]{3,2,1,0:T(8,128)S(1)} %get-tuple-element.30.pred_ref, ...), custom_call_target="tpu_custom_call" | custom-call | tf_op jit(solution)/shard_map/finish/pallas_call | solution.py:469
  (1 shorter events, 0.0 us)
Async XLA Ops:
  1.8 14.8 %all-to-all-start = ((f32[16,16,128]{2,1,0:T(8,128)}), f32[16,16,128]{2,1,0:T(8,128)S(1)}, u32[]{:S(2)}, u32[]{:S(2)}) async-start(f32[16,16,128]{2,1,0:T(8,128)} %get-tuple-element.19), calls=%async_computation | async-start | bytes 262144 | tf_op jit(solution)/shard_map/all_to_all | solution.py:416
  9.1 19.9 %collective-permute-start.1 = (f32[3,2,8,256]{3,2,1,0:T(8,128)}, f32[3,2,8,256]{3,2,1,0:T(8,128)S(1)}, u32[]{:S(2)}, u32[]{:S(2)}) collective-permute-start(f32[3,2,8,256]{3,2,1,0:T(8,128)} %get-tuple-element.20.high_ref), channel_id=1, source_target_pairs={{0,1},{1,2},{2,3},{3,4},{4,5},{5,6},{6,7},{7,8},{8,9},{9,10},{10,1... | collective-permute-start | bytes 147464 | tf_op jit(solution)/shard_map/ppermute | solution.py:415
  12.1 16.9 %collective-permute-start = (f32[3,2,8,256]{3,2,1,0:T(8,128)}, f32[3,2,8,256]{3,2,1,0:T(8,128)S(1)}, u32[]{:S(2)}, u32[]{:S(2)}) collective-permute-start(f32[3,2,8,256]{3,2,1,0:T(8,128)} %get-tuple-element.21.low_ref), channel_id=1, source_target_pairs={{1,0},{2,1},{3,2},{4,3},{5,4},{6,5},{7,6},{8,7},{9,8},{10,9},{11,1... | collective-permute-start | bytes 147464 | tf_op jit(solution)/shard_map/ppermute | solution.py:414
  17.2 17.6 %all-to-all-start.1 = ((f32[16,8,128]{2,1,0:T(8,128)}), f32[16,8,128]{2,1,0:T(8,128)S(1)}, u32[]{:S(2)}, u32[]{:S(2)}) async-start(f32[16,8,128]{2,1,0:T(8,128)} %broadcast_in_dim.8), calls=%async_computation.1 | async-start | bytes 131072 | tf_op jit(solution)/shard_map/all_to_all | solution.py:437
  25.8 1.0 %copy-start.4 = (s32[4,256,128]{2,1,0:T(8,128)S(1)}, s32[4,256,128]{2,1,0:T(8,128)}, u32[]{:S(2)}) copy-start(s32[4,256,128]{2,1,0:T(8,128)} %stencil_ref.1) | copy-start | bytes 1572868
  26.8 1.0 %copy-start.5 = (f32[4,256,128]{2,1,0:T(8,128)S(1)}, f32[4,256,128]{2,1,0:T(8,128)}, u32[]{:S(2)}) copy-start(f32[4,256,128]{2,1,0:T(8,128)} %weight_ref.1) | copy-start | bytes 1572868
  27.9 1.1 %copy-start = (f32[1,3,8,16,256]{4,3,2,1,0:T(8,128)S(1)}, f32[1,3,8,16,256]{4,3,2,1,0:T(8,128)}, u32[]{:S(2)}) copy-start(f32[1,3,8,16,256]{4,3,2,1,0:T(8,128)} %fields_ref.3) | copy-start | bytes 1179652
  27.9 1.2 %copy-start.1 = (f32[3,2,8,256]{3,2,1,0:T(8,128)S(1)}, f32[3,2,8,256]{3,2,1,0:T(8,128)}, u32[]{:S(2)}) copy-start(f32[3,2,8,256]{3,2,1,0:T(8,128)} %get-tuple-element.21.low_ref) | copy-start | bytes 147460
  27.9 1.2 %copy-start.2 = (f32[3,2,8,256]{3,2,1,0:T(8,128)S(1)}, f32[3,2,8,256]{3,2,1,0:T(8,128)}, u32[]{:S(2)}) copy-start(f32[3,2,8,256]{3,2,1,0:T(8,128)} %get-tuple-element.20.high_ref) | copy-start | bytes 147460
  27.9 1.2 %copy-start.3 = (s32[1,3]{1,0:T(1,128)S(1)}, s32[1,3]{1,0:T(1,128)}, u32[]{:S(2)}) copy-start(s32[1,3]{1,0:T(1,128)} %sample_ref.1) | copy-start | bytes 40

commit v5 on v4

--- a/solution.py
+++ b/solution.py
@@ -17,6 +17,7 @@
 GROUPS = 16
 NY = 256
 TILES = NY // CY
+TILE_ORDER = [(tile + 11) % TILES for tile in range(TILES)]
 HALF = CY // 2
 LANES = 128
 CELLS = 2 * NYAW + 1
@@ -173,7 +174,7 @@
     level = lax.axis_index("group") // 2
     blocks = []
     for tile in range(TILES):
-        block = band_ref[tile]
+        block = band_ref[TILE_ORDER.index(tile)]
         blocks += [block, pltpu.roll(block, 2 * FR, 1)]
     band = jnp.concatenate(blocks, axis=0).T[: 2 * FR]
     rows = NYAW * 2 * FR
@@ -184,29 +185,26 @@
             upper = moved.astype(BF16)
             lower = (moved - upper.astype(F32)).astype(BF16)
             for plane in range(2):
-                at = plane * rows + (veer * 2 + step) * FR
-                table[at : at + FR, 0:NY] = upper[plane * FR : (plane + 1) * FR]
-                table[at : at + FR, NY : 2 * NY] = lower[plane * FR : (plane + 1) * FR]
+                at = 2 * plane * rows + (veer * 2 + step) * FR
+                table[at : at + FR, :] = upper[plane * FR : (plane + 1) * FR]
+                table[at + rows : at + rows + FR, :] = lower[plane * FR : (plane + 1) * FR]
     for slot in range(2):
         planes = 2 - slot
         for pair in range(5):
             cells = [cell for cell in (2 * pair, 2 * pair + 1) if cell < CELLS]
             first = slot * CELLS + 2 * pair
             ones = hot_ref[:, first * LANES : (first + len(cells)) * LANES]
-            product = jnp.dot(
-                table[0 : planes * rows], jnp.concatenate([ones, ones], axis=0), preferred_element_type=F32
-            )
+            product = jnp.dot(table[0 : 2 * planes * rows], ones, preferred_element_type=F32)
             for at, cell in enumerate(cells):
                 weights = spread_ref[:, (first + at) * LANES : (first + at + 1) * LANES]
                 for plane in range(planes):
                     kind = 2 if plane == 1 else slot
                     for veer in range(NYAW):
-                        top = plane * rows + veer * 2 * FR
-                        value = jnp.sum(
-                            product[top : top + 2 * FR, at * LANES : (at + 1) * LANES] * weights,
-                            axis=0,
-                            keepdims=True,
-                        )
+                        top = 2 * plane * rows + veer * 2 * FR
+                        span = slice(at * LANES, (at + 1) * LANES)
+                        upper = product[top : top + 2 * FR, span]
+                        lower = product[top + rows : top + rows + 2 * FR, span]
+                        value = jnp.sum((upper + lower) * weights, axis=0, keepdims=True)
                         if cell < 2 * NYAW:
                             yaw, j = divmod(cell, 2)
                             picked[veer * NYAW + yaw, 4 * j + kind : 4 * j + kind + 1, :] = value
@@ -435,7 +433,12 @@
         name="prepare",
     )(stencil, stencil_weight)
     band = lax.all_to_all(
-        jnp.broadcast_to(asked[0:1, :HALF], (TILES, HALF, LANES)), "tile", 0, 0, tiled=True
+        jnp.broadcast_to(asked[0:1, :HALF], (TILES, HALF, LANES)),
+        "tile",
+        0,
+        0,
+        axis_index_groups=[TILE_ORDER],
+        tiled=True,
     )
     pred, edge, right, const = pl.pallas_call(
         begin_kernel,
@@ -458,7 +461,7 @@
         in_specs=[VMEM] * 4,
         out_specs=VMEM,
         scratch_shapes=[
-            pltpu.VMEM((NYAW * 4 * FR, 2 * NY), BF16),
+            pltpu.VMEM((NYAW * 8 * FR, NY), BF16),
             pltpu.VMEM((NYAW * NYAW, 8, LANES), F32),
             pltpu.VMEM((16, LANES), F32),
         ],

time: 48.6 us -> 44.2 us (0.909)
  waiting for transfers between devices: 4.66 us -> 0.01 us
  starting transfers between devices: 23.3 us -> 24.4 us
  blocking collectives: 10.8 us -> 10.1 us
    all_to_all x1, waiting for transfers between devices: 4.65 us -> 0.01 us  [local(): lax.all_to_all(jnp.broadcast_to(asked[0:1, :HALF], (TILES, HALF, LANES)),...]
    all_to_all x1, starting transfers between devices: 8.59 us -> 9.64 us  [local(): lax.all_to_all(jnp.broadcast_to(asked[0:1, :HALF], (TILES, HALF, LANES)),...]
    all_to_all x1, blocking collectives: 10.8 us -> 10.1 us  [local(): planar = lax.all_to_all(answers, 'group', 0, 0, tiled=True)]
  transfers between devices with their start and end apart: 4 -> 4, of which waited for: 1 -> 0; matrix products, arithmetic and copies ran while one was open for 1% -> 1% of each run, Pallas kernels for 5% -> 5%
where the time goes in v5:
time: 44.2 us; the launch traced here: 43.8 us
  starting transfers between devices  24.4 us (55%)
  blocking collectives  10.1 us (23%)
  Pallas kernels  6.53 us (15%)
  local copies, waits for them, and re-layouts  2.73 us (6%)
    all_to_all x1, blocking collectives, local(): planar = lax.all_to_all(answers, 'group', 0, 0, tiled=True)  10.1 us
    all_to_all x1, starting transfers between devices, local(): lax.all_to_all(jnp.broadcast_to(asked[0:1, :HALF], (TILES, HALF, LANES)),...  9.64 us
    all_to_all x1, starting transfers between devices, local(): asked = lax.all_to_all(message, 'group', 0, 0, tiled=True)  7.35 us
    ppermute x1, starting transfers between devices, local(): after = lax.ppermute(low, 'tile', down)  4.41 us
    ppermute x1, starting transfers between devices, local(): before = lax.ppermute(high, 'tile', up)  2.99 us
    unnamed x12, local copies, waits for them, and re-layouts  2.09 us
    pallas_call x1, Pallas kernels, local(): pl.pallas_call(pack_kernel, out_shape=(shape(GROUPS, CY, LANES), shape(CO...  1.76 us
    pallas_call x1, Pallas kernels, local(): pl.pallas_call(interpolate_kernel, out_shape=shape(GROUPS, 8, LANES), in_...  1.5 us
  transfers between devices with their start and end apart: 4, of which 0 were waited for; matrix products, arithmetic and copies ran while one was open for 1% of the time, Pallas kernels for 5%

profile of v5, /device:TPU:1, one launch (start us, length us, event | category | flops | bytes accessed | tf_op | source)
XLA Modules:
  0.0 43.8 jit_solution(16517212973104308913)
XLA Ops:
  0.0 1.8 %pack.1 = (f32[16,16,128]{2,1,0:T(8,128)}, f32[3,2,8,256]{3,2,1,0:T(8,128)}, f32[3,2,8,256]{3,2,1,0:T(8,128)}) custom-call(s32[1,3]{1,0:T(1,128)} %sample_ref.1, f32[3,128,256]{2,1,0:T(8,128)} %bitcast.3), custom_call_target="tpu_custom_call" | custom-call | tf_op jit(solution)/shard_map/pack/pallas_call | solution.py:397
  1.8 7.4 %all-to-all-start = ((f32[16,16,128]{2,1,0:T(8,128)}), f32[16,16,128]{2,1,0:T(8,128)S(1)}, u32[]{:S(2)}, u32[]{:S(2)}) async-start(f32[16,16,128]{2,1,0:T(8,128)} %get-tuple-element.19), calls=%async_computation | async-start | bytes 262144 | tf_op jit(solution)/shard_map/all_to_all | solution.py:414
  9.1 3.0 %collective-permute-start.1 = (f32[3,2,8,256]{3,2,1,0:T(8,128)}, f32[3,2,8,256]{3,2,1,0:T(8,128)S(1)}, u32[]{:S(2)}, u32[]{:S(2)}) collective-permute-start(f32[3,2,8,256]{3,2,1,0:T(8,128)} %get-tuple-element.20.high_ref), channel_id=1, source_target_pairs={{0,1},{1,2},{2,3},{3,4},{4,5},{5,6},{6,7},{7,8},{8,9},{9,10},{10,1... | collective-permute-start | bytes 147464 | tf_op jit(solution)/shard_map/ppermute | solution.py:413
  12.1 4.4 %collective-permute-start = (f32[3,2,8,256]{3,2,1,0:T(8,128)}, f32[3,2,8,256]{3,2,1,0:T(8,128)S(1)}, u32[]{:S(2)}, u32[]{:S(2)}) collective-permute-start(f32[3,2,8,256]{3,2,1,0:T(8,128)} %get-tuple-element.21.low_ref), channel_id=1, source_target_pairs={{1,0},{2,1},{3,2},{4,3},{5,4},{6,5},{7,6},{8,7},{9,8},{10,9},{11,1... | collective-permute-start | bytes 147464 | tf_op jit(solution)/shard_map/ppermute | solution.py:412
  16.5 0.0 all-to-all-done.asked_ref
  16.5 0.6 %broadcast_in_dim.8 = f32[16,8,128]{2,1,0:T(8,128)} broadcast(f32[8,128]{1,0:T(8,128)S(1)} %slice_bitcast_fusion), dimensions={1,2} | broadcast | bytes 69632 | tf_op jit(solution)/shard_map/broadcast_in_dim | solution.py:436
  17.2 9.6 %all-to-all-start.1 = ((f32[16,8,128]{2,1,0:T(8,128)}), f32[16,8,128]{2,1,0:T(8,128)S(1)}, u32[]{:S(2)}, u32[]{:S(2)}) async-start(f32[16,8,128]{2,1,0:T(8,128)} %broadcast_in_dim.8), calls=%async_computation.1 | async-start | bytes 131072 | tf_op jit(solution)/shard_map/all_to_all | solution.py:435
  26.8 0.0 copy-start.4
  26.8 1.0 %copy-done.4 = s32[4,256,128]{2,1,0:T(8,128)S(1)} copy-done((s32[4,256,128]{2,1,0:T(8,128)S(1)}, s32[4,256,128]{2,1,0:T(8,128)}, u32[]{:S(2)}) %copy-start.4) | copy-done | bytes 524312
  27.9 0.0 copy-start.5
  27.9 1.0 %copy-done.5 = f32[4,256,128]{2,1,0:T(8,128)S(1)} copy-done((f32[4,256,128]{2,1,0:T(8,128)S(1)}, f32[4,256,128]{2,1,0:T(8,128)}, u32[]{:S(2)}) %copy-start.5) | copy-done | bytes 524312
  28.9 0.0 copy-start
  28.9 0.0 copy-start.1
  28.9 0.0 copy-start.2
  28.9 0.0 copy-start.3
  28.9 1.1 %prepare.1 = (bf16[256,2304]{1,0:T(8,128)(2,1)S(1)}, f32[64,2304]{1,0:T(8,128)S(1)}) custom-call(s32[4,256,128]{2,1,0:T(8,128)S(1)} %copy-done.4, f32[4,256,128]{2,1,0:T(8,128)S(1)} %copy-done.5), custom_call_target="tpu_custom_call" | custom-call | flops 99999997952 | bytes 200000 | tf_op jit(solution)/shard_map/prepare/pallas_call | solution.py:415
  30.0 0.0 collective-permute-done.1.before_ref
  30.0 0.0 collective-permute-done.after_ref
  30.0 0.0 copy-done
  30.0 0.0 copy-done.1
  30.1 0.0 copy-done.2
  30.1 0.0 copy-done.3
  30.1 1.1 %begin.1 = (f32[3,8,16,256]{3,2,1,0:T(8,128)S(1)}, f32[2,3,8,256]{3,2,1,0:T(8,128)S(1)}, f32[3,8,16,128]{3,2,1,0:T(8,128)S(1)}, f32[24,128]{1,0:T(8,128)S(1)}) custom-call(s32[1,3]{1,0:T(1,128)S(1)} %copy-done.3, f32[1,3,8,16,256]{4,3,2,1,0:T(8,128)S(1)} %copy-done, f32[3,2,8,256]{3,2,1,0:T(8,128)S(1)} %copy-done.2, f32[3,2,8,256]{3,2,1,0:T(8,128)S(1)} %copy-done.1, ...), custom_call_target="tpu_custom_call" | custom-call | flops 8000000 | bytes 1000000 | tf_op jit(solution)/shard_map/begin/pallas_call | solution.py:443
  31.2 0.0 all-to-all-done.1.band_ref
  31.2 1.5 %interpolate.1 = f32[16,8,128]{2,1,0:T(8,128)S(1)} custom-call(f32[16,8,128]{2,1,0:T(8,128)S(1)} %all-to-all-done.1.band_ref, f32[16,16,128]{2,1,0:T(8,128)S(1)} %all-to-all-done.asked_ref, bf16[256,2304]{1,0:T(8,128)(2,1)S(1)} %get-tuple-element.28.hot_ref, f32[64,2304]{1,0:T(8,128)S(1)} %get-tuple-element.29.spread_ref), custom_call_target="tpu_custom_call" | custom-call | tf_op jit(solution)/shard_map/interpolate/pallas_call | solution.py:458
  32.7 10.1 %all_to_all.15.planar_ref = f32[16,8,128]{2,1,0:T(8,128)S(1)} all-to-all(f32[16,8,128]{2,1,0:T(8,128)S(1)} %interpolate.1), channel_id=1, replica_groups=mesh['group'=16,'tile'=16] {'group'}, dimensions={0} | all-to-all | bytes 131072 | tf_op jit(solution)/shard_map/all_to_all | solution.py:471
  42.8 1.1 %finish.1 = f32[1,3,8,16,256]{4,3,2,1,0:T(8,128)} custom-call(f32[24,128]{1,0:T(8,128)S(1)} %get-tuple-element.26.const_ref, f32[1,3,8,16,256]{4,3,2,1,0:T(8,128)S(1)} %copy-done, f32[16,8,128]{2,1,0:T(8,128)S(1)} %all_to_all.15.planar_ref, f32[3,8,16,256]{3,2,1,0:T(8,128)S(1)} %get-tuple-element.30.pred_ref, ...), custom_call_target="tpu_custom_call" | custom-call | tf_op jit(solution)/shard_map/finish/pallas_call | solution.py:472
  (1 shorter events, 0.0 us)
Async XLA Ops:
  1.8 14.8 %all-to-all-start = ((f32[16,16,128]{2,1,0:T(8,128)}), f32[16,16,128]{2,1,0:T(8,128)S(1)}, u32[]{:S(2)}, u32[]{:S(2)}) async-start(f32[16,16,128]{2,1,0:T(8,128)} %get-tuple-element.19), calls=%async_computation | async-start | bytes 262144 | tf_op jit(solution)/shard_map/all_to_all | solution.py:414
  9.1 20.9 %collective-permute-start.1 = (f32[3,2,8,256]{3,2,1,0:T(8,128)}, f32[3,2,8,256]{3,2,1,0:T(8,128)S(1)}, u32[]{:S(2)}, u32[]{:S(2)}) collective-permute-start(f32[3,2,8,256]{3,2,1,0:T(8,128)} %get-tuple-element.20.high_ref), channel_id=1, source_target_pairs={{0,1},{1,2},{2,3},{3,4},{4,5},{5,6},{6,7},{7,8},{8,9},{9,10},{10,1... | collective-permute-start | bytes 147464 | tf_op jit(solution)/shard_map/ppermute | solution.py:413
  12.1 17.9 %collective-permute-start = (f32[3,2,8,256]{3,2,1,0:T(8,128)}, f32[3,2,8,256]{3,2,1,0:T(8,128)S(1)}, u32[]{:S(2)}, u32[]{:S(2)}) collective-permute-start(f32[3,2,8,256]{3,2,1,0:T(8,128)} %get-tuple-element.21.low_ref), channel_id=1, source_target_pairs={{1,0},{2,1},{3,2},{4,3},{5,4},{6,5},{7,6},{8,7},{9,8},{10,9},{11,1... | collective-permute-start | bytes 147464 | tf_op jit(solution)/shard_map/ppermute | solution.py:412
  17.2 14.0 %all-to-all-start.1 = ((f32[16,8,128]{2,1,0:T(8,128)}), f32[16,8,128]{2,1,0:T(8,128)S(1)}, u32[]{:S(2)}, u32[]{:S(2)}) async-start(f32[16,8,128]{2,1,0:T(8,128)} %broadcast_in_dim.8), calls=%async_computation.1 | async-start | bytes 131072 | tf_op jit(solution)/shard_map/all_to_all | solution.py:435
  26.8 1.0 %copy-start.4 = (s32[4,256,128]{2,1,0:T(8,128)S(1)}, s32[4,256,128]{2,1,0:T(8,128)}, u32[]{:S(2)}) copy-start(s32[4,256,128]{2,1,0:T(8,128)} %stencil_ref.1) | copy-start | bytes 1572868
  27.9 1.0 %copy-start.5 = (f32[4,256,128]{2,1,0:T(8,128)S(1)}, f32[4,256,128]{2,1,0:T(8,128)}, u32[]{:S(2)}) copy-start(f32[4,256,128]{2,1,0:T(8,128)} %weight_ref.1) | copy-start | bytes 1572868
  28.9 1.1 %copy-start = (f32[1,3,8,16,256]{4,3,2,1,0:T(8,128)S(1)}, f32[1,3,8,16,256]{4,3,2,1,0:T(8,128)}, u32[]{:S(2)}) copy-start(f32[1,3,8,16,256]{4,3,2,1,0:T(8,128)} %fields_ref.3) | copy-start | bytes 1179652
  28.9 1.2 %copy-start.1 = (f32[3,2,8,256]{3,2,1,0:T(8,128)S(1)}, f32[3,2,8,256]{3,2,1,0:T(8,128)}, u32[]{:S(2)}) copy-start(f32[3,2,8,256]{3,2,1,0:T(8,128)} %get-tuple-element.21.low_ref) | copy-start | bytes 147460
  28.9 1.2 %copy-start.2 = (f32[3,2,8,256]{3,2,1,0:T(8,128)S(1)}, f32[3,2,8,256]{3,2,1,0:T(8,128)}, u32[]{:S(2)}) copy-start(f32[3,2,8,256]{3,2,1,0:T(8,128)} %get-tuple-element.20.high_ref) | copy-start | bytes 147460
  28.9 1.2 %copy-start.3 = (s32[1,3]{1,0:T(1,128)S(1)}, s32[1,3]{1,0:T(1,128)}, u32[]{:S(2)}) copy-start(s32[1,3]{1,0:T(1,128)} %sample_ref.1) | copy-start | bytes 40

commit v6 on v5

--- a/solution.py
+++ b/solution.py
@@ -18,6 +18,7 @@
 NY = 256
 TILES = NY // CY
 TILE_ORDER = [(tile + 11) % TILES for tile in range(TILES)]
+GROUP_ORDER = [(group + 9) % GROUPS for group in range(GROUPS)]
 HALF = CY // 2
 LANES = 128
 CELLS = 2 * NYAW + 1
@@ -231,7 +232,7 @@
             for yaw in range(1, NYAW):
                 one = jnp.where(of_yaw[yaw], picked[veer * NYAW + yaw], one)
             chosen = one if veer == 0 else jnp.where(veer_asked == float(veer), one, chosen)
-        out_ref[group] = chosen
+        out_ref[GROUP_ORDER.index(group)] = chosen
 
 
 def rates(flag, spacing):
@@ -334,7 +335,7 @@
 
     for lev in range(LEV):
         for half in range(2):
-            packed = planar_ref[2 * lev + half]
+            packed = planar_ref[GROUP_ORDER.index(2 * lev + half)]
             for part in range(4):
                 turned = packed if part == 0 else pltpu.roll(packed, LANES - part * FR, 1)
                 unpacked[2 * lev + half, 8 * part : 8 * part + 8, :] = turned
@@ -352,7 +353,7 @@
             target[comp, lev] = pull
             full[comp, lev] = pred_ref[comp, lev, :, :LANES] + pull
     outer = [
-        jnp.concatenate([planar_ref[2 * lev + at, 3:4, :] for lev in range(LEV)], axis=0) for at in range(2)
+        jnp.concatenate([planar_ref[GROUP_ORDER.index(2 * lev + at), 3:4, :] for lev in range(LEV)], axis=0) for at in range(2)
     ]
     for side in range(2):
         aims = []
@@ -468,7 +469,7 @@
         compiler_params=params(),
         name="interpolate",
     )(band, asked, hot, spread)
-    planar = lax.all_to_all(answers, "group", 0, 0, tiled=True)
+    planar = lax.all_to_all(answers, "group", 0, 0, axis_index_groups=[GROUP_ORDER], tiled=True)
     return pl.pallas_call(
         finish_kernel,
         out_shape=shape(1, COMP, LEV, CY, NX),

time: 44.2 us -> 43.1 us (0.975)
  blocking collectives: 10.1 us -> 8.92 us
    all_to_all x1, blocking collectives: 10.1 us -> 8.92 us  [local(): lax.all_to_all(answers, 'group', 0, 0, axis_index_groups=[GROUP_ORDER], t...]
where the time goes in v6:
time: 43.1 us; the launch traced here: 42.7 us
  starting transfers between devices  24.4 us (57%)
  blocking collectives  8.92 us (21%)
  Pallas kernels  6.53 us (15%)
  local copies, waits for them, and re-layouts  2.73 us (6%)
    all_to_all x1, starting transfers between devices, local(): lax.all_to_all(jnp.broadcast_to(asked[0:1, :HALF], (TILES, HALF, LANES)),...  9.64 us
    all_to_all x1, blocking collectives, local(): lax.all_to_all(answers, 'group', 0, 0, axis_index_groups=[GROUP_ORDER], t...  8.92 us
    all_to_all x1, starting transfers between devices, local(): asked = lax.all_to_all(message, 'group', 0, 0, tiled=True)  7.35 us
    ppermute x1, starting transfers between devices, local(): after = lax.ppermute(low, 'tile', down)  4.41 us
    ppermute x1, starting transfers between devices, local(): before = lax.ppermute(high, 'tile', up)  2.99 us
    unnamed x12, local copies, waits for them, and re-layouts  2.09 us
    pallas_call x1, Pallas kernels, local(): pl.pallas_call(pack_kernel, out_shape=(shape(GROUPS, CY, LANES), shape(CO...  1.76 us
    pallas_call x1, Pallas kernels, local(): pl.pallas_call(interpolate_kernel, out_shape=shape(GROUPS, 8, LANES), in_...  1.5 us
  transfers between devices with their start and end apart: 4, of which 0 were waited for; matrix products, arithmetic and copies ran while one was open for 1% of the time, Pallas kernels for 5%

profile of v6, /device:TPU:1, one launch (start us, length us, event | category | flops | bytes accessed | tf_op | source)
XLA Modules:
  0.0 42.7 jit_solution(17775528380226823760)
XLA Ops:
  0.0 1.8 %pack.1 = (f32[16,16,128]{2,1,0:T(8,128)}, f32[3,2,8,256]{3,2,1,0:T(8,128)}, f32[3,2,8,256]{3,2,1,0:T(8,128)}) custom-call(s32[1,3]{1,0:T(1,128)} %sample_ref.1, f32[3,128,256]{2,1,0:T(8,128)} %bitcast.3), custom_call_target="tpu_custom_call" | custom-call | tf_op jit(solution)/shard_map/pack/pallas_call | solution.py:398
  1.8 7.4 %all-to-all-start = ((f32[16,16,128]{2,1,0:T(8,128)}), f32[16,16,128]{2,1,0:T(8,128)S(1)}, u32[]{:S(2)}, u32[]{:S(2)}) async-start(f32[16,16,128]{2,1,0:T(8,128)} %get-tuple-element.19), calls=%async_computation | async-start | bytes 262144 | tf_op jit(solution)/shard_map/all_to_all | solution.py:415
  9.1 3.0 %collective-permute-start.1 = (f32[3,2,8,256]{3,2,1,0:T(8,128)}, f32[3,2,8,256]{3,2,1,0:T(8,128)S(1)}, u32[]{:S(2)}, u32[]{:S(2)}) collective-permute-start(f32[3,2,8,256]{3,2,1,0:T(8,128)} %get-tuple-element.20.high_ref), channel_id=1, source_target_pairs={{0,1},{1,2},{2,3},{3,4},{4,5},{5,6},{6,7},{7,8},{8,9},{9,10},{10,1... | collective-permute-start | bytes 147464 | tf_op jit(solution)/shard_map/ppermute | solution.py:414
  12.1 4.4 %collective-permute-start = (f32[3,2,8,256]{3,2,1,0:T(8,128)}, f32[3,2,8,256]{3,2,1,0:T(8,128)S(1)}, u32[]{:S(2)}, u32[]{:S(2)}) collective-permute-start(f32[3,2,8,256]{3,2,1,0:T(8,128)} %get-tuple-element.21.low_ref), channel_id=1, source_target_pairs={{1,0},{2,1},{3,2},{4,3},{5,4},{6,5},{7,6},{8,7},{9,8},{10,9},{11,1... | collective-permute-start | bytes 147464 | tf_op jit(solution)/shard_map/ppermute | solution.py:413
  16.5 0.0 all-to-all-done.asked_ref
  16.5 0.6 %broadcast_in_dim.8 = f32[16,8,128]{2,1,0:T(8,128)} broadcast(f32[8,128]{1,0:T(8,128)S(1)} %slice_bitcast_fusion), dimensions={1,2} | broadcast | bytes 69632 | tf_op jit(solution)/shard_map/broadcast_in_dim | solution.py:437
  17.2 9.6 %all-to-all-start.1 = ((f32[16,8,128]{2,1,0:T(8,128)}), f32[16,8,128]{2,1,0:T(8,128)S(1)}, u32[]{:S(2)}, u32[]{:S(2)}) async-start(f32[16,8,128]{2,1,0:T(8,128)} %broadcast_in_dim.8), calls=%async_computation.1 | async-start | bytes 131072 | tf_op jit(solution)/shard_map/all_to_all | solution.py:436
  26.8 0.0 copy-start.4
  26.8 1.0 %copy-done.4 = s32[4,256,128]{2,1,0:T(8,128)S(1)} copy-done((s32[4,256,128]{2,1,0:T(8,128)S(1)}, s32[4,256,128]{2,1,0:T(8,128)}, u32[]{:S(2)}) %copy-start.4) | copy-done | bytes 524312
  27.9 0.0 copy-start.5
  27.9 1.0 %copy-done.5 = f32[4,256,128]{2,1,0:T(8,128)S(1)} copy-done((f32[4,256,128]{2,1,0:T(8,128)S(1)}, f32[4,256,128]{2,1,0:T(8,128)}, u32[]{:S(2)}) %copy-start.5) | copy-done | bytes 524312
  28.9 0.0 copy-start
  28.9 0.0 copy-start.1
  28.9 0.0 copy-start.2
  28.9 0.0 copy-start.3
  28.9 1.1 %prepare.1 = (bf16[256,2304]{1,0:T(8,128)(2,1)S(1)}, f32[64,2304]{1,0:T(8,128)S(1)}) custom-call(s32[4,256,128]{2,1,0:T(8,128)S(1)} %copy-done.4, f32[4,256,128]{2,1,0:T(8,128)S(1)} %copy-done.5), custom_call_target="tpu_custom_call" | custom-call | flops 99999997952 | bytes 200000 | tf_op jit(solution)/shard_map/prepare/pallas_call | solution.py:416
  30.0 0.0 collective-permute-done.1.before_ref
  30.0 0.0 collective-permute-done.after_ref
  30.0 0.0 copy-done
  30.0 0.0 copy-done.1
  30.1 0.0 copy-done.2
  30.1 0.0 copy-done.3
  30.1 1.1 %begin.1 = (f32[3,8,16,256]{3,2,1,0:T(8,128)S(1)}, f32[2,3,8,256]{3,2,1,0:T(8,128)S(1)}, f32[3,8,16,128]{3,2,1,0:T(8,128)S(1)}, f32[24,128]{1,0:T(8,128)S(1)}) custom-call(s32[1,3]{1,0:T(1,128)S(1)} %copy-done.3, f32[1,3,8,16,256]{4,3,2,1,0:T(8,128)S(1)} %copy-done, f32[3,2,8,256]{3,2,1,0:T(8,128)S(1)} %copy-done.2, f32[3,2,8,256]{3,2,1,0:T(8,128)S(1)} %copy-done.1, ...), custom_call_target="tpu_custom_call" | custom-call | flops 8000000 | bytes 1000000 | tf_op jit(solution)/shard_map/begin/pallas_call | solution.py:444
  31.2 0.0 all-to-all-done.1.band_ref
  31.2 1.5 %interpolate.1 = f32[16,8,128]{2,1,0:T(8,128)S(1)} custom-call(f32[16,8,128]{2,1,0:T(8,128)S(1)} %all-to-all-done.1.band_ref, f32[16,16,128]{2,1,0:T(8,128)S(1)} %all-to-all-done.asked_ref, bf16[256,2304]{1,0:T(8,128)(2,1)S(1)} %get-tuple-element.28.hot_ref, f32[64,2304]{1,0:T(8,128)S(1)} %get-tuple-element.29.spread_ref), custom_call_target="tpu_custom_call" | custom-call | tf_op jit(solution)/shard_map/interpolate/pallas_call | solution.py:459
  32.7 8.9 %all_to_all.15.planar_ref = f32[16,8,128]{2,1,0:T(8,128)S(1)} all-to-all(f32[16,8,128]{2,1,0:T(8,128)S(1)} %interpolate.1), channel_id=1, replica_groups={{144,160,176,192,208,224,240,0,16,32,48,64,80,96,112,128},{145,161,177,..., dimensions={0} | all-to-all | bytes 131072 | tf_op jit(solution)/shard_map/all_to_all | solution.py:472
  41.6 1.1 %finish.1 = f32[1,3,8,16,256]{4,3,2,1,0:T(8,128)} custom-call(f32[24,128]{1,0:T(8,128)S(1)} %get-tuple-element.26.const_ref, f32[1,3,8,16,256]{4,3,2,1,0:T(8,128)S(1)} %copy-done, f32[16,8,128]{2,1,0:T(8,128)S(1)} %all_to_all.15.planar_ref, f32[3,8,16,256]{3,2,1,0:T(8,128)S(1)} %get-tuple-element.30.pred_ref, ...), custom_call_target="tpu_custom_call" | custom-call | tf_op jit(solution)/shard_map/finish/pallas_call | solution.py:473
  (1 shorter events, 0.0 us)
Async XLA Ops:
  1.8 14.8 %all-to-all-start = ((f32[16,16,128]{2,1,0:T(8,128)}), f32[16,16,128]{2,1,0:T(8,128)S(1)}, u32[]{:S(2)}, u32[]{:S(2)}) async-start(f32[16,16,128]{2,1,0:T(8,128)} %get-tuple-element.19), calls=%async_computation | async-start | bytes 262144 | tf_op jit(solution)/shard_map/all_to_all | solution.py:415
  9.1 20.9 %collective-permute-start.1 = (f32[3,2,8,256]{3,2,1,0:T(8,128)}, f32[3,2,8,256]{3,2,1,0:T(8,128)S(1)}, u32[]{:S(2)}, u32[]{:S(2)}) collective-permute-start(f32[3,2,8,256]{3,2,1,0:T(8,128)} %get-tuple-element.20.high_ref), channel_id=1, source_target_pairs={{0,1},{1,2},{2,3},{3,4},{4,5},{5,6},{6,7},{7,8},{8,9},{9,10},{10,1... | collective-permute-start | bytes 147464 | tf_op jit(solution)/shard_map/ppermute | solution.py:414
  12.1 17.9 %collective-permute-start = (f32[3,2,8,256]{3,2,1,0:T(8,128)}, f32[3,2,8,256]{3,2,1,0:T(8,128)S(1)}, u32[]{:S(2)}, u32[]{:S(2)}) collective-permute-start(f32[3,2,8,256]{3,2,1,0:T(8,128)} %get-tuple-element.21.low_ref), channel_id=1, source_target_pairs={{1,0},{2,1},{3,2},{4,3},{5,4},{6,5},{7,6},{8,7},{9,8},{10,9},{11,1... | collective-permute-start | bytes 147464 | tf_op jit(solution)/shard_map/ppermute | solution.py:413
  17.2 14.0 %all-to-all-start.1 = ((f32[16,8,128]{2,1,0:T(8,128)}), f32[16,8,128]{2,1,0:T(8,128)S(1)}, u32[]{:S(2)}, u32[]{:S(2)}) async-start(f32[16,8,128]{2,1,0:T(8,128)} %broadcast_in_dim.8), calls=%async_computation.1 | async-start | bytes 131072 | tf_op jit(solution)/shard_map/all_to_all | solution.py:436
  26.8 1.0 %copy-start.4 = (s32[4,256,128]{2,1,0:T(8,128)S(1)}, s32[4,256,128]{2,1,0:T(8,128)}, u32[]{:S(2)}) copy-start(s32[4,256,128]{2,1,0:T(8,128)} %stencil_ref.1) | copy-start | bytes 1572868
  27.9 1.0 %copy-start.5 = (f32[4,256,128]{2,1,0:T(8,128)S(1)}, f32[4,256,128]{2,1,0:T(8,128)}, u32[]{:S(2)}) copy-start(f32[4,256,128]{2,1,0:T(8,128)} %weight_ref.1) | copy-start | bytes 1572868
  28.9 1.1 %copy-start = (f32[1,3,8,16,256]{4,3,2,1,0:T(8,128)S(1)}, f32[1,3,8,16,256]{4,3,2,1,0:T(8,128)}, u32[]{:S(2)}) copy-start(f32[1,3,8,16,256]{4,3,2,1,0:T(8,128)} %fields_ref.3) | copy-start | bytes 1179652
  28.9 1.2 %copy-start.1 = (f32[3,2,8,256]{3,2,1,0:T(8,128)S(1)}, f32[3,2,8,256]{3,2,1,0:T(8,128)}, u32[]{:S(2)}) copy-start(f32[3,2,8,256]{3,2,1,0:T(8,128)} %get-tuple-element.21.low_ref) | copy-start | bytes 147460
  28.9 1.2 %copy-start.2 = (f32[3,2,8,256]{3,2,1,0:T(8,128)S(1)}, f32[3,2,8,256]{3,2,1,0:T(8,128)}, u32[]{:S(2)}) copy-start(f32[3,2,8,256]{3,2,1,0:T(8,128)} %get-tuple-element.20.high_ref) | copy-start | bytes 147460
  28.9 1.2 %copy-start.3 = (s32[1,3]{1,0:T(1,128)S(1)}, s32[1,3]{1,0:T(1,128)}, u32[]{:S(2)}) copy-start(s32[1,3]{1,0:T(1,128)} %sample_ref.1) | copy-start | bytes 40

commit v7 on v6

--- a/solution.py
+++ b/solution.py
@@ -18,7 +18,7 @@
 NY = 256
 TILES = NY // CY
 TILE_ORDER = [(tile + 11) % TILES for tile in range(TILES)]
-GROUP_ORDER = [(group + 9) % GROUPS for group in range(GROUPS)]
+GROUP_ORDER = [(group + 13) % GROUPS for group in range(GROUPS)]
 HALF = CY // 2
 LANES = 128
 CELLS = 2 * NYAW + 1

time: 43.1 us -> 42.6 us (0.988)
  blocking collectives: 8.92 us -> 8.48 us
    all_to_all x1, blocking collectives: 8.92 us -> 8.48 us  [local(): lax.all_to_all(answers, 'group', 0, 0, axis_index_groups=[GROUP_ORDER], t...]
  transfers between devices with their start and end apart: 4 -> 4, of which waited for: 0 -> 0; matrix products, arithmetic and copies ran while one was open for 1% -> 2% of each run, Pallas kernels for 5% -> 5%
where the time goes in v7:
time: 42.6 us; the launch traced here: 42.2 us
  starting transfers between devices  24.4 us (57%)
  blocking collectives  8.48 us (20%)
  Pallas kernels  6.53 us (15%)
  local copies, waits for them, and re-layouts  2.73 us (6%)
    all_to_all x1, starting transfers between devices, local(): lax.all_to_all(jnp.broadcast_to(asked[0:1, :HALF], (TILES, HALF, LANES)),...  9.64 us
    all_to_all x1, blocking collectives, local(): lax.all_to_all(answers, 'group', 0, 0, axis_index_groups=[GROUP_ORDER], t...  8.48 us
    all_to_all x1, starting transfers between devices, local(): asked = lax.all_to_all(message, 'group', 0, 0, tiled=True)  7.35 us
    ppermute x1, starting transfers between devices, local(): after = lax.ppermute(low, 'tile', down)  4.41 us
    ppermute x1, starting transfers between devices, local(): before = lax.ppermute(high, 'tile', up)  2.99 us
    unnamed x12, local copies, waits for them, and re-layouts  2.09 us
    pallas_call x1, Pallas kernels, local(): pl.pallas_call(pack_kernel, out_shape=(shape(GROUPS, CY, LANES), shape(CO...  1.76 us
    pallas_call x1, Pallas kernels, local(): pl.pallas_call(interpolate_kernel, out_shape=shape(GROUPS, 8, LANES), in_...  1.5 us
  transfers between devices with their start and end apart: 4, of which 0 were waited for; matrix products, arithmetic and copies ran while one was open for 2% of the time, Pallas kernels for 5%

profile of v7, /device:TPU:1, one launch (start us, length us, event | category | flops | bytes accessed | tf_op | source)
XLA Modules:
  0.0 42.2 jit_solution(14647341524872670522)
XLA Ops:
  0.0 1.8 %pack.1 = (f32[16,16,128]{2,1,0:T(8,128)}, f32[3,2,8,256]{3,2,1,0:T(8,128)}, f32[3,2,8,256]{3,2,1,0:T(8,128)}) custom-call(s32[1,3]{1,0:T(1,128)} %sample_ref.1, f32[3,128,256]{2,1,0:T(8,128)} %bitcast.3), custom_call_target="tpu_custom_call" | custom-call | tf_op jit(solution)/shard_map/pack/pallas_call | solution.py:398
  1.8 7.4 %all-to-all-start = ((f32[16,16,128]{2,1,0:T(8,128)}), f32[16,16,128]{2,1,0:T(8,128)S(1)}, u32[]{:S(2)}, u32[]{:S(2)}) async-start(f32[16,16,128]{2,1,0:T(8,128)} %get-tuple-element.19), calls=%async_computation | async-start | bytes 262144 | tf_op jit(solution)/shard_map/all_to_all | solution.py:415
  9.1 3.0 %collective-permute-start.1 = (f32[3,2,8,256]{3,2,1,0:T(8,128)}, f32[3,2,8,256]{3,2,1,0:T(8,128)S(1)}, u32[]{:S(2)}, u32[]{:S(2)}) collective-permute-start(f32[3,2,8,256]{3,2,1,0:T(8,128)} %get-tuple-element.20.high_ref), channel_id=1, source_target_pairs={{0,1},{1,2},{2,3},{3,4},{4,5},{5,6},{6,7},{7,8},{8,9},{9,10},{10,1... | collective-permute-start | bytes 147464 | tf_op jit(solution)/shard_map/ppermute | solution.py:414
  12.1 4.4 %collective-permute-start = (f32[3,2,8,256]{3,2,1,0:T(8,128)}, f32[3,2,8,256]{3,2,1,0:T(8,128)S(1)}, u32[]{:S(2)}, u32[]{:S(2)}) collective-permute-start(f32[3,2,8,256]{3,2,1,0:T(8,128)} %get-tuple-element.21.low_ref), channel_id=1, source_target_pairs={{1,0},{2,1},{3,2},{4,3},{5,4},{6,5},{7,6},{8,7},{9,8},{10,9},{11,1... | collective-permute-start | bytes 147464 | tf_op jit(solution)/shard_map/ppermute | solution.py:413
  16.5 0.0 all-to-all-done.asked_ref
  16.5 0.6 %broadcast_in_dim.8 = f32[16,8,128]{2,1,0:T(8,128)} broadcast(f32[8,128]{1,0:T(8,128)S(1)} %slice_bitcast_fusion), dimensions={1,2} | broadcast | bytes 69632 | tf_op jit(solution)/shard_map/broadcast_in_dim | solution.py:437
  17.2 9.6 %all-to-all-start.1 = ((f32[16,8,128]{2,1,0:T(8,128)}), f32[16,8,128]{2,1,0:T(8,128)S(1)}, u32[]{:S(2)}, u32[]{:S(2)}) async-start(f32[16,8,128]{2,1,0:T(8,128)} %broadcast_in_dim.8), calls=%async_computation.1 | async-start | bytes 131072 | tf_op jit(solution)/shard_map/all_to_all | solution.py:436
  26.8 0.0 copy-start.4
  26.8 1.0 %copy-done.4 = s32[4,256,128]{2,1,0:T(8,128)S(1)} copy-done((s32[4,256,128]{2,1,0:T(8,128)S(1)}, s32[4,256,128]{2,1,0:T(8,128)}, u32[]{:S(2)}) %copy-start.4) | copy-done | bytes 524312
  27.9 0.0 copy-start.5
  27.9 1.0 %copy-done.5 = f32[4,256,128]{2,1,0:T(8,128)S(1)} copy-done((f32[4,256,128]{2,1,0:T(8,128)S(1)}, f32[4,256,128]{2,1,0:T(8,128)}, u32[]{:S(2)}) %copy-start.5) | copy-done | bytes 524312
  28.9 0.0 copy-start
  28.9 0.0 copy-start.1
  28.9 0.0 copy-start.2
  28.9 0.0 copy-start.3
  28.9 1.1 %prepare.1 = (bf16[256,2304]{1,0:T(8,128)(2,1)S(1)}, f32[64,2304]{1,0:T(8,128)S(1)}) custom-call(s32[4,256,128]{2,1,0:T(8,128)S(1)} %copy-done.4, f32[4,256,128]{2,1,0:T(8,128)S(1)} %copy-done.5), custom_call_target="tpu_custom_call" | custom-call | flops 99999997952 | bytes 200000 | tf_op jit(solution)/shard_map/prepare/pallas_call | solution.py:416
  30.0 0.0 collective-permute-done.1.before_ref
  30.0 0.0 collective-permute-done.after_ref
  30.0 0.0 copy-done
  30.0 0.0 copy-done.1
  30.1 0.0 copy-done.2
  30.1 0.0 copy-done.3
  30.1 1.1 %begin.1 = (f32[3,8,16,256]{3,2,1,0:T(8,128)S(1)}, f32[2,3,8,256]{3,2,1,0:T(8,128)S(1)}, f32[3,8,16,128]{3,2,1,0:T(8,128)S(1)}, f32[24,128]{1,0:T(8,128)S(1)}) custom-call(s32[1,3]{1,0:T(1,128)S(1)} %copy-done.3, f32[1,3,8,16,256]{4,3,2,1,0:T(8,128)S(1)} %copy-done, f32[3,2,8,256]{3,2,1,0:T(8,128)S(1)} %copy-done.2, f32[3,2,8,256]{3,2,1,0:T(8,128)S(1)} %copy-done.1, ...), custom_call_target="tpu_custom_call" | custom-call | flops 8000000 | bytes 1000000 | tf_op jit(solution)/shard_map/begin/pallas_call | solution.py:444
  31.2 0.0 all-to-all-done.1.band_ref
  31.2 1.5 %interpolate.1 = f32[16,8,128]{2,1,0:T(8,128)S(1)} custom-call(f32[16,8,128]{2,1,0:T(8,128)S(1)} %all-to-all-done.1.band_ref, f32[16,16,128]{2,1,0:T(8,128)S(1)} %all-to-all-done.asked_ref, bf16[256,2304]{1,0:T(8,128)(2,1)S(1)} %get-tuple-element.28.hot_ref, f32[64,2304]{1,0:T(8,128)S(1)} %get-tuple-element.29.spread_ref), custom_call_target="tpu_custom_call" | custom-call | tf_op jit(solution)/shard_map/interpolate/pallas_call | solution.py:459
  32.7 8.5 %all_to_all.15.planar_ref = f32[16,8,128]{2,1,0:T(8,128)S(1)} all-to-all(f32[16,8,128]{2,1,0:T(8,128)S(1)} %interpolate.1), channel_id=1, replica_groups={{208,224,240,0,16,32,48,64,80,96,112,128,144,160,176,192},{209,225,241,..., dimensions={0} | all-to-all | bytes 131072 | tf_op jit(solution)/shard_map/all_to_all | solution.py:472
  41.2 1.1 %finish.1 = f32[1,3,8,16,256]{4,3,2,1,0:T(8,128)} custom-call(f32[24,128]{1,0:T(8,128)S(1)} %get-tuple-element.26.const_ref, f32[1,3,8,16,256]{4,3,2,1,0:T(8,128)S(1)} %copy-done, f32[16,8,128]{2,1,0:T(8,128)S(1)} %all_to_all.15.planar_ref, f32[3,8,16,256]{3,2,1,0:T(8,128)S(1)} %get-tuple-element.30.pred_ref, ...), custom_call_target="tpu_custom_call" | custom-call | tf_op jit(solution)/shard_map/finish/pallas_call | solution.py:473
  (1 shorter events, 0.0 us)
Async XLA Ops:
  1.8 14.8 %all-to-all-start = ((f32[16,16,128]{2,1,0:T(8,128)}), f32[16,16,128]{2,1,0:T(8,128)S(1)}, u32[]{:S(2)}, u32[]{:S(2)}) async-start(f32[16,16,128]{2,1,0:T(8,128)} %get-tuple-element.19), calls=%async_computation | async-start | bytes 262144 | tf_op jit(solution)/shard_map/all_to_all | solution.py:415
  9.1 20.9 %collective-permute-start.1 = (f32[3,2,8,256]{3,2,1,0:T(8,128)}, f32[3,2,8,256]{3,2,1,0:T(8,128)S(1)}, u32[]{:S(2)}, u32[]{:S(2)}) collective-permute-start(f32[3,2,8,256]{3,2,1,0:T(8,128)} %get-tuple-element.20.high_ref), channel_id=1, source_target_pairs={{0,1},{1,2},{2,3},{3,4},{4,5},{5,6},{6,7},{7,8},{8,9},{9,10},{10,1... | collective-permute-start | bytes 147464 | tf_op jit(solution)/shard_map/ppermute | solution.py:414
  12.1 17.9 %collective-permute-start = (f32[3,2,8,256]{3,2,1,0:T(8,128)}, f32[3,2,8,256]{3,2,1,0:T(8,128)S(1)}, u32[]{:S(2)}, u32[]{:S(2)}) collective-permute-start(f32[3,2,8,256]{3,2,1,0:T(8,128)} %get-tuple-element.21.low_ref), channel_id=1, source_target_pairs={{1,0},{2,1},{3,2},{4,3},{5,4},{6,5},{7,6},{8,7},{9,8},{10,9},{11,1... | collective-permute-start | bytes 147464 | tf_op jit(solution)/shard_map/ppermute | solution.py:413
  17.2 14.0 %all-to-all-start.1 = ((f32[16,8,128]{2,1,0:T(8,128)}), f32[16,8,128]{2,1,0:T(8,128)S(1)}, u32[]{:S(2)}, u32[]{:S(2)}) async-start(f32[16,8,128]{2,1,0:T(8,128)} %broadcast_in_dim.8), calls=%async_computation.1 | async-start | bytes 131072 | tf_op jit(solution)/shard_map/all_to_all | solution.py:436
  26.8 1.0 %copy-start.4 = (s32[4,256,128]{2,1,0:T(8,128)S(1)}, s32[4,256,128]{2,1,0:T(8,128)}, u32[]{:S(2)}) copy-start(s32[4,256,128]{2,1,0:T(8,128)} %stencil_ref.1) | copy-start | bytes 1572868
  27.9 1.0 %copy-start.5 = (f32[4,256,128]{2,1,0:T(8,128)S(1)}, f32[4,256,128]{2,1,0:T(8,128)}, u32[]{:S(2)}) copy-start(f32[4,256,128]{2,1,0:T(8,128)} %weight_ref.1) | copy-start | bytes 1572868
  28.9 1.1 %copy-start = (f32[1,3,8,16,256]{4,3,2,1,0:T(8,128)S(1)}, f32[1,3,8,16,256]{4,3,2,1,0:T(8,128)}, u32[]{:S(2)}) copy-start(f32[1,3,8,16,256]{4,3,2,1,0:T(8,128)} %fields_ref.3) | copy-start | bytes 1179652
  28.9 1.2 %copy-start.1 = (f32[3,2,8,256]{3,2,1,0:T(8,128)S(1)}, f32[3,2,8,256]{3,2,1,0:T(8,128)}, u32[]{:S(2)}) copy-start(f32[3,2,8,256]{3,2,1,0:T(8,128)} %get-tuple-element.21.low_ref) | copy-start | bytes 147460
  28.9 1.2 %copy-start.2 = (f32[3,2,8,256]{3,2,1,0:T(8,128)S(1)}, f32[3,2,8,256]{3,2,1,0:T(8,128)}, u32[]{:S(2)}) copy-start(f32[3,2,8,256]{3,2,1,0:T(8,128)} %get-tuple-element.20.high_ref) | copy-start | bytes 147460
  28.9 1.2 %copy-start.3 = (s32[1,3]{1,0:T(1,128)S(1)}, s32[1,3]{1,0:T(1,128)}, u32[]{:S(2)}) copy-start(s32[1,3]{1,0:T(1,128)} %sample_ref.1) | copy-start | bytes 40
